TPU v7x, 128 devices: a whole 4x4x4 slice. The times are simulated.
128 devices in a mesh: expert: 16 (over y, x), tensor: 8 (over z, core).
Axes of the slice: x: 4, y: 4, z: 4, core: 2. Of those that a mesh axis runs over, the one named last changes fastest.
Arguments:
- tokens: bfloat16 [2048, 4096], P('expert'), may hold values from -6 to 6
- expert_ids: int32 [2048, 8], P('expert'), may hold values from 0 to 15, all different within a row; in each aligned block of 128 rows (0 to 127, 128 to 255, ...) at most 72 rows name the same one
- gate_probs: float32 [2048, 8], P('expert'), may hold values from 0.03 to 0.5
- grad_out: bfloat16 [2048, 4096], P('expert'), may hold values from -6 to 6
- gate_up: bfloat16 [16, 2, 1536, 4096], P('expert', None, 'tensor'), may hold values from -0.09375 to 0.09375
- down_proj: bfloat16 [16, 1536, 4096], P('expert', 'tensor'), may hold values from -0.15625 to 0.15625
Outputs:
- mixed: bfloat16 [2048, 4096], P('expert', 'tensor')
- grad_tokens: bfloat16 [2048, 4096], P('expert', 'tensor')
- grad_gate_up: bfloat16 [16, 2, 1536, 4096], P('expert', None, 'tensor')
- grad_down: bfloat16 [16, 1536, 4096], P('expert', 'tensor')
Inputs may be any that keep to these rules, and one draw needn't show every extreme that they name: `expert_ids`: each token names 8 different experts. Among the 128 tokens of one index of the expert axis no expert is named by more than 72 tokens, a bound that some block reaches.
All inputs are finite; a program needn't handle non-finite values.
Results may differ from a plain program's by a relative error of at most 0.019.
Values may be sent and summed in bfloat16 or wider, within the bound.
No kernel may reach another device: no remote copies, remote signals or barrier semaphores. Data moves between devices by JAX's collectives and lax.ppermute only.
A program may use at most 192 MiB of HBM per device.

v0:
```python
import jax
import jax.numpy as jnp
from jax import lax
from jax.sharding import PartitionSpec as P

TOPK = 8
EXPERTS = 16
CAP = 72


def combine_rows(partials_in, row_weight, target, tok_count):
    summed = lax.psum_scatter(
        partials_in.astype(jnp.float32).astype(jnp.bfloat16),
        "tensor",
        scatter_dimension=3,
        tiled=True,
    ).astype(jnp.float32)
    returned = lax.all_to_all(
        summed.astype(jnp.bfloat16), "expert", split_axis=0, concat_axis=0, tiled=True
    ).astype(summed.dtype)
    share_width = returned.shape[3]
    picked = returned.reshape(-1, share_width)[target]
    weighted = picked.reshape(tok_count, TOPK, share_width) * row_weight[:, :, None]
    return jnp.sum(weighted, axis=1)


def on_device(tokens, expert_ids, gate_probs, grad_out, gate_up, down_proj):
    tok_count, model_width = tokens.shape
    groups = lax.axis_size("expert")
    local_experts = gate_up.shape[0]
    block_units = gate_up.shape[2]
    flat_ids = expert_ids.reshape(-1)
    onehot = (flat_ids[:, None] == jnp.arange(EXPERTS, dtype=jnp.int32)[None, :]).astype(jnp.int32)
    before = jnp.cumsum(onehot, axis=0) - onehot
    slot_index = jnp.sum(before * onehot, axis=1)
    target = flat_ids * CAP + slot_index
    pair_count = flat_ids.shape[0]
    pair_of_slot = (
        jnp.zeros((EXPERTS * CAP,), jnp.int32)
        .at[target]
        .set(jnp.arange(pair_count, dtype=jnp.int32))
    )
    filled = jnp.zeros((EXPERTS * CAP,), jnp.int32).at[target].set(1) > 0
    token_of_slot = pair_of_slot // TOPK
    weight_of_slot = jnp.where(filled, gate_probs.reshape(-1)[pair_of_slot], 0.0)
    send_tokens = jnp.where(filled[:, None], tokens[token_of_slot], jnp.zeros((), tokens.dtype))
    send_cot = (weight_of_slot[:, None] * grad_out[token_of_slot]).astype(jnp.bfloat16)
    shape_four = (groups, local_experts, CAP, model_width)
    inputs, cot = (
        lax.all_to_all(
            send_tokens.reshape(shape_four), "expert", split_axis=0, concat_axis=0, tiled=True
        ),
        lax.all_to_all(
            send_cot.reshape(shape_four), "expert", split_axis=0, concat_axis=0, tiled=True
        ),
    )
    w_gate_up = gate_up.reshape(local_experts, 2 * block_units, model_width)
    gated = jnp.einsum("secd,efd->secf", inputs, w_gate_up, preferred_element_type=jnp.float32)
    gate = gated[..., :block_units]
    upval = gated[..., block_units:]
    sig = jax.nn.sigmoid(gate)
    hidden = (gate * sig * upval).astype(jnp.bfloat16)
    partial_out = jnp.einsum(
        "secf,efd->secd", hidden, down_proj, preferred_element_type=jnp.float32
    ).astype(jnp.bfloat16)
    mixed = combine_rows(partial_out, gate_probs, target, tok_count).astype(jnp.bfloat16)
    dhid = jnp.einsum("secd,efd->secf", cot, down_proj, preferred_element_type=jnp.float32)
    grad_down = jnp.einsum(
        "secf,secd->efd", hidden, cot, preferred_element_type=jnp.float32
    ).astype(jnp.bfloat16)
    dgate = dhid * upval * sig * (1.0 + gate * (1.0 - sig))
    dup = dhid * gate * sig
    dgu = jnp.concatenate([dgate, dup], axis=3).astype(jnp.bfloat16)
    grad_gate_up = jnp.einsum("secf,secd->efd", dgu, inputs, preferred_element_type=jnp.float32)
    grad_gate_up = grad_gate_up.reshape(local_experts, 2, block_units, model_width).astype(
        jnp.bfloat16
    )
    partial_back = jnp.einsum(
        "secf,efd->secd", dgu, w_gate_up, preferred_element_type=jnp.float32
    ).astype(jnp.bfloat16)
    unit_weight = jnp.ones((tok_count, TOPK), jnp.float32)
    grad_tokens = combine_rows(partial_back, unit_weight, target, tok_count).astype(jnp.bfloat16)
    return (mixed, grad_tokens, grad_gate_up, grad_down)


def solution(mesh):
    return jax.shard_map(
        on_device,
        mesh=mesh,
        in_specs=(
            P("expert", None),
            P("expert", None),
            P("expert", None),
            P("expert", None),
            P("expert", None, "tensor", None),
            P("expert", "tensor", None),
        ),
        out_specs=(
            P("expert", "tensor"),
            P("expert", "tensor"),
            P("expert", None, "tensor", None),
            P("expert", "tensor", None),
        ),
        check_vma=False,
    )
```

profile of v0, /device:TPU:2, one launch (start us, length us, event | category | flops | bytes accessed | tf_op | source)
XLA Modules:
  0.0 529.4 jit_solution(5550989198559816800)
XLA Ops:
  7.2 0.0 copy-start
  7.2 0.8 broadcast_multiply_fusion
  8.0 0.9 copy.23
  8.9 0.1 eq.29
  9.0 0.1 eq.25
  9.1 0.1 copy.22
  9.2 0.1 mul.70
  9.3 0.8 copy.29
  10.1 0.1 reshape.184
  10.2 4.5 reduce-window.6
  14.7 0.1 slice.26
  14.8 0.1 copy.25
  15.0 0.1 copy.26
  15.0 0.1 broadcast_add_fusion
  15.2 4.3 scatter_custom_fusion.1
  19.5 4.3 scatter_custom_fusion
  23.9 4.6 gather_fusion.2
  28.5 0.1 broadcast_in_dim.37
  28.6 19.8 %gather_fusion = bf16[1152,4096]{1,0:T(8,128)(2,1)} fusion(bf16[128,4096]{1,0:T(8,128)(2,1)} %param.6, s32[2048]{0:T(1024)S(1)} %get-tuple-element.12), kind=kCustom, calls=%fused_computation | custom fusion | bytes 18878976 | tf_op jit(solution)/shard_map/gather | solution.py:46
  48.4 8.0 %broadcast_select_fusion = bf16[16,1,72,4096]{3,2,1,0:T(8,128)(2,1)} fusion(bf16[16,1,72,4096]{3,2,1,0:T(8,128)(2,1)} %bitcast.143, pred[16,72]{1,0:T(8,128)(4,1)S(1)} %broadcast_in_dim.37), kind=kLoop, calls=%fused_computation.19 | loop fusion | flops 4718592 | bytes 18875520 | tf_op jit(solution)/shard_map/jit(_where)/select_n | solution.py:46
  56.4 8.1 %all-to-all-start = ((bf16[16,1,72,4096]{3,2,1,0:T(8,128)(2,1)}), bf16[16,1,72,4096]{3,2,1,0:T(8,128)(2,1)}, u32[]{:S(2)}, u32[]{:S(2)}) async-start(bf16[16,1,72,4096]{3,2,1,0:T(8,128)(2,1)} %broadcast_select_fusion), calls=%async_computation | async-start | bytes 18874368 | tf_op jit(solution)/shard_map/all_to_all | solution.py:50
  64.6 0.1 mul.76
  64.7 19.8 %gather_fusion.3 = bf16[1152,4096]{1,0:T(8,128)(2,1)} fusion(bf16[128,4096]{1,0:T(8,128)(2,1)} %param.9, s32[2048]{0:T(1024)S(1)} %get-tuple-element.12), kind=kCustom, calls=%fused_computation.3 | custom fusion | bytes 18878976 | tf_op jit(solution)/shard_map/gather | solution.py:47
  84.4 11.3 %fusion = bf16[16,1,72,4096]{3,2,1,0:T(8,128)(2,1)} fusion(bf16[16,1,72,4096]{3,2,1,0:T(8,128)(2,1)} %bitcast.142, f32[16,72]{1,0:T(8,128)S(1)} %mul.76), kind=kLoop, calls=%fused_computation.8 | loop fusion | flops 14155776 | bytes 18878976 | tf_op jit(solution)/shard_map/convert_element_type | solution.py:47
  95.8 105.0 %all-to-all-done = bf16[16,1,72,4096]{3,2,1,0:T(8,128)(2,1)} async-done(((bf16[16,1,72,4096]{3,2,1,0:T(8,128)(2,1)}), bf16[16,1,72,4096]{3,2,1,0:T(8,128)(2,1)}, u32[]{:S(2)}, u32[]{:S(2)}) %all-to-all-start) | async-done | bytes 9437216 | tf_op jit(solution)/shard_map/all_to_all | solution.py:50
  200.8 8.9 %all-to-all-start.2 = ((bf16[16,1,72,4096]{3,2,1,0:T(8,128)(2,1)}), bf16[16,1,72,4096]{3,2,1,0:T(8,128)(2,1)}, u32[]{:S(2)}, u32[]{:S(2)}) async-start(bf16[16,1,72,4096]{3,2,1,0:T(8,128)(2,1)} %fusion), calls=%async_computation.3 | async-start | bytes 18874368 | tf_op jit(solution)/shard_map/all_to_all | solution.py:53
  209.7 0.2 reduce-scatter.5.cloned.1.call-start
  209.9 0.0 copy-done
  209.9 8.8 %fusion.26 = f32[16,1,72,384]{3,2,0,1:T(8,128)} fusion(bf16[384,4096,1]{1,0,2:T(8,128)(2,1)S(1)} %bitcast.140, bf16[16,1,72,4096]{3,2,1,0:T(8,128)(2,1)} %all-to-all-done), kind=kOutput, calls=%fused_computation.30 | convolution fusion | flops 3623878656 | bytes 14352384 | tf_op jit(solution)/shard_map/secd,efd->secf/dot_general | solution.py:58
  218.7 124.8 %all-to-all-done.2 = bf16[16,1,72,4096]{3,2,1,0:T(8,128)(2,1)} async-done(((bf16[16,1,72,4096]{3,2,1,0:T(8,128)(2,1)}), bf16[16,1,72,4096]{3,2,1,0:T(8,128)(2,1)}, u32[]{:S(2)}, u32[]{:S(2)}) %all-to-all-start.2) | async-done | bytes 9437216 | tf_op jit(solution)/shard_map/all_to_all | solution.py:53
  343.6 8.8 %fusion.38 = (bf16[16,72,192]{2,1,0:T(8,128)(2,1)S(1)}, bf16[16,72,192]{2,1,0:T(8,128)(2,1)S(1)}, bf16[16,1,72,192]{3,2,0,1:T(8,128)(2,1)}) fusion(f32[16,1,72,384]{3,2,0,1:T(8,128)} %fusion.26, bf16[1,192,4096]{2,1,0:T(8,128)(2,1)} %param.11, bf16[16,1,72,4096]{3,2,1,0:T(8,128)(2,1)} %all-to-all-done.2), kind=kOutput, calls=%fused_computation.43 | convolution fusion | flops 1815478272 | bytes 14106624 | tf_op jit(solution)/shard_map/secd,efd->secf/dot_general | solution.py:67
  352.3 0.0 copy-start.1
  352.3 0.0 copy-start.2
  352.3 0.8 copy-done.1
  353.1 0.2 copy-done.2
  353.3 7.6 %convert_bitcast_fusion = bf16[16,1,72,4096]{3,2,0,1:T(8,128)(2,1)} fusion(bf16[384,4096,1]{1,0,2:T(8,128)(2,1)S(1)} %bitcast.141, bf16[16,72,192]{2,1,0:T(8,128)(2,1)S(1)} %get-tuple-element.7, bf16[16,72,192]{2,1,0:T(8,128)(2,1)S(1)} %get-tuple-element.6), kind=kOutput, calls=%fused_computation.17 | convolution fusion | flops 3630366720 | bytes 13467648 | tf_op jit(solution)/shard_map/secf,efd->secd/dot_general | solution.py:78
  360.9 0.0 reduce-scatter.5.cloned.1.call-update
  360.9 0.3 reduce-scatter.3.cloned.1.call-start
  361.2 7.9 %convert_bitcast_fusion.1 = bf16[16,1,72,4096]{3,2,0,1:T(8,128)(2,1)} fusion(bf16[1,192,4096]{2,1,0:T(8,128)(2,1)} %param.11, bf16[16,1,72,192]{3,2,0,1:T(8,128)(2,1)} %get-tuple-element.8), kind=kOutput, calls=%fused_computation.18 | convolution fusion | flops 1816657920 | bytes 11452416 | tf_op jit(solution)/shard_map/secf,efd->secd/dot_general | solution.py:63
  369.1 0.0 reduce-scatter.3.cloned.1.call-update
  369.2 2.5 fusion.39
  371.7 4.1 dot_general.39
  375.8 46.4 %reduce-scatter.5.cloned.1.call-done = bf16[16,1,72,512]{3,2,0,1:T(8,128)(2,1)} async-done(((bf16[16,1,72,4096]{3,2,0,1:T(8,128)(2,1)}), bf16[16,1,72,512]{3,2,0,1:T(8,128)(2,1)}) %reduce-scatter.5.cloned.1.call-update) | async-done | bytes 1179664 | tf_op jit(solution)/shard_map/reduce_scatter | solution.py:12
  422.2 7.3 %all-to-all-start.3 = ((bf16[16,1,72,512]{3,2,1,0:T(8,128)(2,1)}), bf16[16,1,72,512]{3,2,1,0:T(8,128)(2,1)}, u32[]{:S(2)}, u32[]{:S(2)}) async-start(bf16[16,1,72,512]{3,2,1,0:T(8,128)(2,1)} %bitcast.145), calls=%async_computation.5 | async-start | bytes 2359296 | tf_op jit(solution)/shard_map/all_to_all | solution.py:18
  429.4 10.6 %fusion.11 = bf16[1,2,192,4096]{3,2,1,0:T(8,128)(2,1)} fusion(bf16[16,1,72,4096]{3,2,1,0:T(8,128)(2,1)} %all-to-all-done, bf16[2,192,72,16]{1,0,2,3:T(2,128)(2,1)} %dot_general.39), kind=kOutput, calls=%fused_computation.21 | convolution fusion | flops 3625451520 | bytes 13467648 | tf_op jit(solution)/shard_map/secf,secd->efd/dot_general | solution.py:74
  440.0 41.6 %reduce-scatter.3.cloned.1.call-done = bf16[16,1,72,512]{3,2,0,1:T(8,128)(2,1)} async-done(((bf16[16,1,72,4096]{3,2,0,1:T(8,128)(2,1)}), bf16[16,1,72,512]{3,2,0,1:T(8,128)(2,1)}) %reduce-scatter.3.cloned.1.call-update) | async-done | bytes 1179664 | tf_op jit(solution)/shard_map/reduce_scatter | solution.py:12
  481.7 0.0 all-to-all-done.3
  481.7 7.7 %all-to-all-start.1 = ((bf16[16,1,72,512]{3,2,1,0:T(8,128)(2,1)}), bf16[16,1,72,512]{3,2,1,0:T(8,128)(2,1)}, u32[]{:S(2)}, u32[]{:S(2)}) async-start(bf16[16,1,72,512]{3,2,1,0:T(8,128)(2,1)} %bitcast.144), calls=%async_computation.2 | async-start | bytes 2359296 | tf_op jit(solution)/shard_map/all_to_all | solution.py:18
  489.4 7.3 %fusion.20 = bf16[1,192,4096]{2,1,0:T(8,128)(2,1)} fusion(bf16[16,1,72,4096]{3,2,1,0:T(8,128)(2,1)} %all-to-all-done.2, bf16[16,1,72,192]{3,2,0,1:T(8,128)(2,1)} %get-tuple-element.8), kind=kOutput, calls=%fused_computation.24 | convolution fusion | flops 1812725760 | bytes 11452416 | tf_op jit(solution)/shard_map/secf,secd->efd/dot_general | solution.py:68
  496.6 3.0 bitcast_convert_fusion.1
  499.7 6.9 %gather_fusion.4 = f32[1024,512]{1,0:T(8,128)} fusion(f32[1152,512]{1,0:T(8,128)} %bitcast_convert_fusion.1, s32[1024]{0:T(1024)S(1)} %broadcast_clamp_fusion), kind=kCustom, calls=%fused_computation.4 | custom fusion | bytes 4198400 | tf_op jit(solution)/shard_map/gather | solution.py:22
  506.6 2.8 bitcast_reduce_fusion
  509.4 0.0 all-to-all-done.1
  509.4 3.0 bitcast_convert_fusion.2
  512.4 6.9 %gather_fusion.1 = f32[1024,512]{1,0:T(8,128)} fusion(f32[1152,512]{1,0:T(8,128)} %bitcast_convert_fusion.2, s32[1024]{0:T(1024)S(1)} %broadcast_clamp_fusion), kind=kCustom, calls=%fused_computation.1 | custom fusion | bytes 4198400 | tf_op jit(solution)/shard_map/gather | solution.py:22
  519.3 2.9 fusion.23
  (11 shorter events, 0.1 us)
Async XLA Ops:
  7.2 202.7 %copy-start = (bf16[1,2,192,4096]{3,2,1,0:T(8,128)(2,1)S(1)}, bf16[1,2,192,4096]{3,2,1,0:T(8,128)(2,1)}, u32[]{:S(2)}) copy-start(bf16[1,2,192,4096]{3,2,1,0:T(8,128)(2,1)} %param.10) | copy-start | bytes 9437188
  56.4 144.4 %all-to-all-start = ((bf16[16,1,72,4096]{3,2,1,0:T(8,128)(2,1)}), bf16[16,1,72,4096]{3,2,1,0:T(8,128)(2,1)}, u32[]{:S(2)}, u32[]{:S(2)}) async-start(bf16[16,1,72,4096]{3,2,1,0:T(8,128)(2,1)} %broadcast_select_fusion), calls=%async_computation | async-start | bytes 18874368 | tf_op jit(solution)/shard_map/all_to_all | solution.py:50
  200.8 142.8 %all-to-all-start.2 = ((bf16[16,1,72,4096]{3,2,1,0:T(8,128)(2,1)}), bf16[16,1,72,4096]{3,2,1,0:T(8,128)(2,1)}, u32[]{:S(2)}, u32[]{:S(2)}) async-start(bf16[16,1,72,4096]{3,2,1,0:T(8,128)(2,1)} %fusion), calls=%async_computation.3 | async-start | bytes 18874368 | tf_op jit(solution)/shard_map/all_to_all | solution.py:53
  209.7 212.5 %reduce-scatter.5.cloned.1.call-start = ((), (), s32[]{:S(2)}) async-start(), calls=%async_computation.7 | async-start | bytes 10616832 | tf_op jit(solution)/shard_map/reduce_scatter | solution.py:12
  352.3 0.8 copy-start.1
  352.3 1.0 copy-start.2
  360.9 120.7 %reduce-scatter.3.cloned.1.call-start = ((), (), s32[]{:S(2)}) async-start(), calls=%async_computation.6 | async-start | bytes 10616832 | tf_op jit(solution)/shard_map/reduce_scatter | solution.py:12
  422.2 59.5 %all-to-all-start.3 = ((bf16[16,1,72,512]{3,2,1,0:T(8,128)(2,1)}), bf16[16,1,72,512]{3,2,1,0:T(8,128)(2,1)}, u32[]{:S(2)}, u32[]{:S(2)}) async-start(bf16[16,1,72,512]{3,2,1,0:T(8,128)(2,1)} %bitcast.145), calls=%async_computation.5 | async-start | bytes 2359296 | tf_op jit(solution)/shard_map/all_to_all | solution.py:18
  481.7 27.7 %all-to-all-start.1 = ((bf16[16,1,72,512]{3,2,1,0:T(8,128)(2,1)}), bf16[16,1,72,512]{3,2,1,0:T(8,128)(2,1)}, u32[]{:S(2)}, u32[]{:S(2)}) async-start(bf16[16,1,72,512]{3,2,1,0:T(8,128)(2,1)} %bitcast.144), calls=%async_computation.2 | async-start | bytes 2359296 | tf_op jit(solution)/shard_map/all_to_all | solution.py:18
Sparse Core Ops, SparseCore 0:
  361.0 61.0 reduce-scatter.4
  424.6 57.0 reduce-scatter.2
where the time goes:
time: 536 us; the launch traced here: 529 us
  waiting for transfers between devices  318 us (59%)
  local copies, waits for them, and re-layouts  74.4 us (14%)
  matrix products  51 us (10%)
  other arithmetic  39.2 us (7%)
  starting transfers between devices  32.4 us (6%)
  between operations  14.5 us (3%)
    all_to_all x1, waiting for transfers between devices, on_device(): lax.all_to_all(send_cot.reshape(shape_four), 'expert', split_axis=0, conc...  125 us
    all_to_all x1, waiting for transfers between devices, on_device(): lax.all_to_all(send_tokens.reshape(shape_four), 'expert', split_axis=0, c...  105 us
    reduce_scatter x2, waiting for transfers between devices, combine_rows(): lax.psum_scatter(partials_in.astype(jnp.float32).astype(jnp.bfloat16), 't...  88 us
    gather x1, local copies, waits for them, and re-layouts, on_device(): tokens[token_of_slot]  19.8 us
    gather x1, local copies, waits for them, and re-layouts, on_device(): grad_out[token_of_slot]  19.8 us
    all_to_all x2, starting transfers between devices, combine_rows(): lax.all_to_all(summed.astype(jnp.bfloat16), 'expert', split_axis=0, conca...  14.9 us
    gather x2, local copies, waits for them, and re-layouts, combine_rows(): picked = returned.reshape(-1, share_width)[target]  13.9 us
    convert_element_type x1, other arithmetic, on_device(): (weight_of_slot[:, None] * grad_out[token_of_slot]).astype(jnp.bfloat16)  11.3 us
  transfers between devices with their start and end apart: 6, of which 4 were waited for; matrix products, arithmetic and copies ran while one was open for 16% of the time, Pallas kernels for 0%

commit v1 on v0

v1 whole, which is shorter than its diff:
```python
import jax
import jax.numpy as jnp
from jax import lax
from jax.experimental import pallas as pl
from jax.experimental.pallas import tpu as pltpu
from jax.sharding import PartitionSpec as P

EXPERTS = 16
CAP = 72
GROUPS = 16
TOK = 128
D = 4096
UNITS = 192
TENSOR = 8
SHARE = D // TENSOR
STEP_GROUPS = 4
PAIRS = STEP_GROUPS // 2
ROWS = STEP_GROUPS * CAP
STEPS = GROUPS // STEP_GROUPS
ALL_ROWS = GROUPS * CAP
F32 = jnp.float32
BF16 = jnp.bfloat16
VMEM_LIMIT = 56 * 1024 * 1024


def nt(a, b):
    return lax.dot_general(a, b, (((1,), (1,)), ((), ())), preferred_element_type=F32)


def nn(a, b):
    return lax.dot_general(a, b, (((1,), (0,)), ((), ())), preferred_element_type=F32)


def forward_kernel(x_ref, row_ref, wgu_ref, wd_ref, in_ref, gate_ref, up_ref, hid_ref, out_ref):
    for j in range(PAIRS):
        x = x_ref[2 * j : 2 * j + 2].reshape(2 * TOK, D)
        hit = lax.broadcasted_iota(jnp.int32, (2 * CAP, 2 * TOK), 0) == row_ref[j]
        onehot = jnp.where(hit, 1.0, 0.0).astype(BF16)
        in_ref[2 * CAP * j : 2 * CAP * (j + 1), :] = nn(onehot, x).astype(BF16)
    rows = in_ref[...]
    gate = nt(rows, wgu_ref[0])
    up = nt(rows, wgu_ref[1])
    gate_ref[...] = gate
    up_ref[...] = up
    hidden = (gate * jax.nn.sigmoid(gate) * up).astype(BF16)
    hid_ref[...] = hidden
    for c in range(TENSOR):
        cols = slice(SHARE * c, SHARE * (c + 1))
        out_ref[c] = nn(hidden, wd_ref[:, cols]).astype(BF16)


def backward_kernel(g_ref, row_ref, w_ref, gate_ref, up_ref, wgu_ref, wd_ref, cot_ref, dgu_ref, back_ref):
    for j in range(PAIRS):
        g = g_ref[2 * j : 2 * j + 2].reshape(2 * TOK, D)
        hit = lax.broadcasted_iota(jnp.int32, (2 * CAP, 2 * TOK), 0) == row_ref[j]
        onehot = jnp.where(hit, 1.0, 0.0).astype(BF16)
        weight = jnp.sum(jnp.where(hit, w_ref[j], 0.0), axis=1, keepdims=True)
        cot_ref[2 * CAP * j : 2 * CAP * (j + 1), :] = (nn(onehot, g) * weight).astype(BF16)
    dhid = nt(cot_ref[...], wd_ref[...])
    gate = gate_ref[...]
    up = up_ref[...]
    sig = jax.nn.sigmoid(gate)
    dgate = (dhid * up * sig * (1.0 + gate * (1.0 - sig))).astype(BF16)
    dup = (dhid * gate * sig).astype(BF16)
    dgu_ref[0] = dgate
    dgu_ref[1] = dup
    for c in range(TENSOR):
        cols = slice(SHARE * c, SHARE * (c + 1))
        back_ref[c] = (nn(dgate, wgu_ref[0, :, cols]) + nn(dup, wgu_ref[1, :, cols])).astype(BF16)


def combine_kernel(weighted, r_ref, w_ref, o_ref):
    w = w_ref[...]
    mask = w > 0.0
    ones = jnp.where(mask, 1.0, 0.0)
    lower = lax.broadcasted_iota(jnp.int32, (TOK, TOK), 1) < lax.broadcasted_iota(jnp.int32, (TOK, TOK), 0)
    slot = nn(jnp.where(lower, 1.0, 0.0).astype(BF16), ones.astype(BF16))
    slot = jnp.where(mask, slot, -1.0).astype(jnp.int32)
    scale = w if weighted else ones
    total = jnp.zeros(o_ref.shape, F32)
    for e in range(EXPERTS):
        hit = lax.broadcasted_iota(jnp.int32, (TOK, CAP), 1) == slot[:, e : e + 1]
        onehot = jnp.where(hit, 1.0, 0.0).astype(BF16)
        total += nn(onehot, r_ref[e]) * scale[:, e : e + 1]
    o_ref[...] = total.astype(BF16)


def params():
    return pltpu.CompilerParams(vmem_limit_bytes=VMEM_LIMIT, dimension_semantics=("arbitrary",))


def gathered_spec(which):
    return pl.BlockSpec((STEP_GROUPS, TENSOR, None, TOK // TENSOR, D), lambda i: (i, 0, which, 0, 0))


def whole(shape):
    return pl.BlockSpec(shape, lambda i: (0,) * len(shape), pipeline_mode=pl.Buffered(1))


ROW_SPEC = pl.BlockSpec((PAIRS, 1, 2 * TOK), lambda i: (i, 0, 0))
WIDE_SPEC = pl.BlockSpec((ROWS, D), lambda i: (i, 0))
UNIT_SPEC = pl.BlockSpec((ROWS, UNITS), lambda i: (i, 0))
SHARE_SPEC = pl.BlockSpec((TENSOR, ROWS, SHARE), lambda i: (0, i, 0))


def forward(gathered, row_of, wgu, wd):
    return pl.pallas_call(
        forward_kernel,
        grid=(STEPS,),
        in_specs=[gathered_spec(0), ROW_SPEC, whole(wgu.shape), whole(wd.shape)],
        out_specs=[WIDE_SPEC, UNIT_SPEC, UNIT_SPEC, UNIT_SPEC, SHARE_SPEC],
        out_shape=[
            jax.ShapeDtypeStruct((ALL_ROWS, D), BF16),
            jax.ShapeDtypeStruct((ALL_ROWS, UNITS), F32),
            jax.ShapeDtypeStruct((ALL_ROWS, UNITS), F32),
            jax.ShapeDtypeStruct((ALL_ROWS, UNITS), BF16),
            jax.ShapeDtypeStruct((TENSOR, ALL_ROWS, SHARE), BF16),
        ],
        compiler_params=params(),
        cost_estimate=pl.CostEstimate(flops=8_000_000_000, bytes_accessed=42_000_000, transcendentals=221184),
    )(gathered, row_of, wgu, wd)


def backward(gathered, row_of, weight, gate, up, wgu, wd):
    return pl.pallas_call(
        backward_kernel,
        grid=(STEPS,),
        in_specs=[
            gathered_spec(1), ROW_SPEC, ROW_SPEC, UNIT_SPEC, UNIT_SPEC, whole(wgu.shape), whole(wd.shape),
        ],
        out_specs=[
            WIDE_SPEC, pl.BlockSpec((2, ROWS, UNITS), lambda i: (0, i, 0)), SHARE_SPEC,
        ],
        out_shape=[
            jax.ShapeDtypeStruct((ALL_ROWS, D), BF16),
            jax.ShapeDtypeStruct((2, ALL_ROWS, UNITS), BF16),
            jax.ShapeDtypeStruct((TENSOR, ALL_ROWS, SHARE), BF16),
        ],
        compiler_params=params(),
        cost_estimate=pl.CostEstimate(flops=8_000_000_000, bytes_accessed=42_000_000, transcendentals=221184),
    )(gathered, row_of, weight, gate, up, wgu, wd)


def combine(returned, own_weight, weighted):
    return pl.pallas_call(
        lambda *refs: combine_kernel(weighted, *refs),
        out_shape=jax.ShapeDtypeStruct((TOK, returned.shape[2]), BF16),
        compiler_params=pltpu.CompilerParams(vmem_limit_bytes=VMEM_LIMIT),
        cost_estimate=pl.CostEstimate(flops=200_000_000, bytes_accessed=1_400_000, transcendentals=0),
    )(returned, own_weight)


def reduce_and_return(partial_rows):
    summed = lax.psum_scatter(partial_rows, "tensor", scatter_dimension=0, tiled=False)
    return lax.all_to_all(
        summed.reshape(GROUPS, CAP, SHARE), "expert", split_axis=0, concat_axis=0, tiled=True
    )


def on_device(tokens, expert_ids, gate_probs, grad_out, gate_up, down_proj):
    part = TOK // TENSOR
    first = lax.axis_index("tensor") * part
    mine = jnp.concatenate(
        [
            lax.dynamic_slice_in_dim(tokens, first, part, 0),
            lax.dynamic_slice_in_dim(grad_out, first, part, 0),
        ],
        axis=0,
    )
    gathered = lax.all_gather(mine, ("expert", "tensor"), axis=0, tiled=True)
    gathered = gathered.reshape(GROUPS, TENSOR, 2, part, D)

    named = expert_ids[:, :, None] == jnp.arange(EXPERTS, dtype=jnp.int32)
    own_weight = jnp.sum(jnp.where(named, gate_probs[:, :, None], 0.0), axis=1)
    weight = lax.all_to_all(own_weight.T, "expert", split_axis=0, concat_axis=0, tiled=True)
    mask = weight > 0.0
    place = jnp.arange(TOK, dtype=jnp.int32)
    earlier = (place[:, None] < place[None, :]).astype(BF16)
    slot = jnp.dot(mask.astype(BF16), earlier, preferred_element_type=F32).astype(jnp.int32)
    offset = CAP * (jnp.arange(GROUPS, dtype=jnp.int32) % 2)
    row_of = jnp.where(mask, slot + offset[:, None], -1).reshape(GROUPS // 2, 1, 2 * TOK)
    weight = weight.reshape(GROUPS // 2, 1, 2 * TOK)

    wgu, wd = gate_up[0], down_proj[0]
    inputs, gate, up, hidden, partial_out = forward(gathered, row_of, wgu, wd)
    out_back = reduce_and_return(partial_out)
    cot, dgu, partial_back = backward(gathered, row_of, weight, gate, up, wgu, wd)
    grad_back = reduce_and_return(partial_back)
    grad_down = jnp.einsum("rf,rd->fd", hidden, cot, preferred_element_type=F32).astype(BF16)
    grad_gate_up = jnp.einsum("crf,rd->cfd", dgu, inputs, preferred_element_type=F32).astype(BF16)
    mixed = combine(out_back, own_weight, True)
    grad_tokens = combine(grad_back, own_weight, False)
    return (mixed, grad_tokens, grad_gate_up[None], grad_down[None])


def solution(mesh):
    return jax.shard_map(
        on_device,
        mesh=mesh,
        in_specs=(
            P("expert", None),
            P("expert", None),
            P("expert", None),
            P("expert", None),
            P("expert", None, "tensor", None),
            P("expert", "tensor", None),
        ),
        out_specs=(
            P("expert", "tensor"),
            P("expert", "tensor"),
            P("expert", None, "tensor", None),
            P("expert", "tensor", None),
        ),
        check_vma=False,
    )
```

time: 536 us -> 293 us (0.55); the launches traced: 529 us -> 292 us
  waiting for transfers between devices: 318 us -> 189 us
  local copies, waits for them, and re-layouts: 74.4 us -> 3.48 us
  Pallas kernels: 0 us -> 45.2 us
  other arithmetic: 39.2 us -> 2.04 us
  matrix products: 51 us -> 17.3 us
  starting transfers between devices: 32.4 us -> 22.1 us
    all_to_all x4 -> x3, waiting for transfers between devices: 230 us -> 6.07 us  [the longest x1 6.06 us: on_device(): lax.all_to_all(own_weight.T, 'expert', split_axis=0, concat_axis=0, tiled...]
    all_gather x0 -> x1, waiting for transfers between devices: none -> 96.1 us  [on_device(): gathered = lax.all_gather(mine, ('expert', 'tensor'), axis=0, tiled=True)]
    gather x5 -> x0, local copies, waits for them, and re-layouts: 58 us -> none  [the longest x1 19.8 us: on_device(): tokens[token_of_slot]]
    pallas_call x0 -> x4, Pallas kernels: none -> 45.2 us  [the longest x1 21.5 us: backward(): pl.pallas_call(backward_kernel, grid=(STEPS,), in_specs=[gathered_spec(1)...]
    dot_general x6 -> x3, matrix products: 51 us -> 17.3 us  [the longest x1 9.36 us: on_device(): jnp.einsum('crf,rd->cfd', dgu, inputs, preferred_element_type=F32)]
    convert_element_type x2 -> x0, other arithmetic: 11.4 us -> none  [the longest x1 11.3 us: on_device(): (weight_of_slot[:, None] * grad_out[token_of_slot]).astype(jnp.bfloat16)]
    all_to_all x4 -> x3, starting transfers between devices: 31.9 us -> 22 us  [the longest x2 14.5 us: reduce_and_return(): lax.all_to_all(summed.reshape(GROUPS, CAP, SHARE), 'expert', split_axis=0...]
    scatter x2 -> x0, local copies, waits for them, and re-layouts: 8.63 us -> none  [the longest x1 4.32 us: on_device(): pair_of_slot = jnp.zeros((EXPERTS * CAP,), jnp.int32).at[target].set(jnp....]
  transfers between devices with their start and end apart: 6 -> 6, of which waited for: 4 -> 4; matrix products, arithmetic and copies ran while one was open for 16% -> 7% of each run, Pallas kernels for 0% -> 8%
where the time goes in v1:
time: 293 us; the launch traced here: 292 us
  waiting for transfers between devices  189 us (65%)
  Pallas kernels  45.2 us (15%)
  starting transfers between devices  22.1 us (8%)
  matrix products  17.3 us (6%)
  between operations  13.8 us (5%)
  local copies, waits for them, and re-layouts  3.48 us (1%)
    all_gather x1, waiting for transfers between devices, on_device(): gathered = lax.all_gather(mine, ('expert', 'tensor'), axis=0, tiled=True)  96.1 us
    reduce_scatter x2, waiting for transfers between devices, reduce_and_return(): lax.psum_scatter(partial_rows, 'tensor', scatter_dimension=0, tiled=False)  86.4 us
    pallas_call x1, Pallas kernels, backward(): pl.pallas_call(backward_kernel, grid=(STEPS,), in_specs=[gathered_spec(1)...  21.5 us
    pallas_call x1, Pallas kernels, forward(): pl.pallas_call(forward_kernel, grid=(STEPS,), in_specs=[gathered_spec(0),...  18 us
    all_to_all x2, starting transfers between devices, reduce_and_return(): lax.all_to_all(summed.reshape(GROUPS, CAP, SHARE), 'expert', split_axis=0...  14.5 us
    dot_general x1, matrix products, on_device(): jnp.einsum('crf,rd->cfd', dgu, inputs, preferred_element_type=F32)  9.36 us
    all_to_all x1, starting transfers between devices, on_device(): lax.all_to_all(own_weight.T, 'expert', split_axis=0, concat_axis=0, tiled...  7.48 us
    dot_general x1, matrix products, on_device(): jnp.einsum('rf,rd->fd', hidden, cot, preferred_element_type=F32)  7.17 us
  transfers between devices with their start and end apart: 6, of which 4 were waited for; matrix products, arithmetic and copies ran while one was open for 7% of the time, Pallas kernels for 8%

profile of v1, /device:TPU:2, one launch (start us, length us, event | category | flops | bytes accessed | tf_op | source)
XLA Modules:
  0.0 292.5 jit_solution(9399755541160150807)
XLA Ops:
  7.2 0.0 all-gather.2.cloned.1.call-start
  7.2 1.0 constant_dynamic-slice_fusion
  8.2 0.7 pad_maximum_fusion
  8.9 0.0 all-gather.2.cloned.1.call-update
  9.0 1.3 select_reduce_fusion
  10.3 7.5 %all-to-all-start = ((f32[16,1,128]{2,1,0:T(1,128)}), f32[16,1,128]{2,1,0:T(1,128)S(1)}, u32[]{:S(2)}, u32[]{:S(2)}) async-start(f32[16,1,128]{2,1,0:T(1,128)} %bitcast.3), calls=%async_computation | async-start | bytes 16384 | tf_op jit(solution)/shard_map/all_to_all | solution.py:175
  17.7 0.0 reduce-scatter.3.cloned.1.call-start
  17.8 6.1 %all-to-all-done = f32[16,1,128]{2,1,0:T(1,128)S(1)} async-done(((f32[16,1,128]{2,1,0:T(1,128)}), f32[16,1,128]{2,1,0:T(1,128)S(1)}, u32[]{:S(2)}, u32[]{:S(2)}) %all-to-all-start) | async-done | bytes 8224 | tf_op jit(solution)/shard_map/all_to_all | solution.py:175
  23.9 0.0 copy-start.4
  23.9 0.7 fusion.10
  24.6 96.1 %all-gather.2.cloned.1.call-done = bf16[4096,4096]{1,0:T(8,128)(2,1)} async-done(((bf16[32,4096]{1,0:T(8,128)(2,1)}), bf16[4096,4096]{1,0:T(8,128)(2,1)}) %all-gather.2.cloned.1.call-update) | async-done | bytes 33554448 | tf_op jit(solution)/shard_map/all_gather | solution.py:170
  120.7 18.0 %shard_map.93 = (bf16[1152,4096]{1,0:T(8,128)(2,1)}, f32[1152,192]{1,0:T(8,128)}, f32[1152,192]{1,0:T(8,128)}, bf16[1152,192]{1,0:T(8,128)(2,1)}, bf16[8,1152,512]{2,1,0:T(8,128)(2,1)}) custom-call(bf16[16,8,2,16,4096]{4,3,2,1,0:T(8,128)(2,1)} %bitcast.31, s32[8,1,256]{2,1,0:T(1,128)} %bitcast.41, bf16[2,192,4096]{2,1,0:T(8,128)(2,1)} %bitcast.33, ...), custom_call_target="tpu_custom_call" | custom-call | flops 8000000000 | bytes 42000000 | tf_op jit(solution)/shard_map/pallas_call | solution.py:107
  138.7 0.0 copy-done.4
  138.7 0.0 reduce-scatter.3.cloned.1.call-update
  138.7 0.0 reduce-scatter.5.cloned.1.call-start
  138.8 21.5 %shard_map.95 = (bf16[1152,4096]{1,0:T(8,128)(2,1)}, bf16[2,1152,192]{2,1,0:T(8,128)(2,1)}, bf16[8,1152,512]{2,1,0:T(8,128)(2,1)}) custom-call(bf16[16,8,2,16,4096]{4,3,2,1,0:T(8,128)(2,1)} %bitcast.32, s32[8,1,256]{2,1,0:T(1,128)} %bitcast.42, f32[8,1,256]{2,1,0:T(1,128)} %bitcast.40, f32[1152,192]{1,0:T(8,128)} %get-tuple-element.13.gate_ref, ...), custom_call_target="tpu_custom_call" | custom-call | flops 8000000000 | bytes 42000000 | tf_op jit(solution)/shard_map/pallas_call | solution.py:125
  160.3 0.0 reduce-scatter.5.cloned.1.call-update
  160.3 0.0 copy-start.3
  160.4 35.5 %reduce-scatter.3.cloned.1.call-done = bf16[1,1152,512]{2,1,0:T(8,128)(2,1)} async-done(((bf16[8,1152,512]{2,1,0:T(8,128)(2,1)}), bf16[1,1152,512]{2,1,0:T(8,128)(2,1)}) %reduce-scatter.3.cloned.1.call-update) | async-done | bytes 1179664 | tf_op jit(solution)/shard_map/reduce_scatter | solution.py:154
  195.9 7.3 %all-to-all-start.1 = ((bf16[16,72,512]{2,1,0:T(8,128)(2,1)}), bf16[16,72,512]{2,1,0:T(8,128)(2,1)S(1)}, u32[]{:S(2)}, u32[]{:S(2)}) async-start(bf16[16,72,512]{2,1,0:T(8,128)(2,1)} %bitcast.38), calls=%async_computation.2 | async-start | bytes 2359296 | tf_op jit(solution)/shard_map/all_to_all | solution.py:155
  203.1 1.4 copy.34.refs_1_
  204.6 50.9 %reduce-scatter.5.cloned.1.call-done = bf16[1,1152,512]{2,1,0:T(8,128)(2,1)} async-done(((bf16[8,1152,512]{2,1,0:T(8,128)(2,1)}), bf16[1,1152,512]{2,1,0:T(8,128)(2,1)}) %reduce-scatter.5.cloned.1.call-update) | async-done | bytes 1179664 | tf_op jit(solution)/shard_map/reduce_scatter | solution.py:154
  255.4 0.0 all-to-all-done.1.refs_0_
  255.4 0.0 copy-start
  255.4 7.3 %all-to-all-start.2 = ((bf16[16,72,512]{2,1,0:T(8,128)(2,1)}), bf16[16,72,512]{2,1,0:T(8,128)(2,1)S(1)}, u32[]{:S(2)}, u32[]{:S(2)}) async-start(bf16[16,72,512]{2,1,0:T(8,128)(2,1)} %bitcast.37), calls=%async_computation.4 | async-start | bytes 2359296 | tf_op jit(solution)/shard_map/all_to_all | solution.py:155
  262.7 0.0 copy-done.3
  262.7 0.0 copy-start.2
  262.7 7.2 %fusion.8 = bf16[1,192,4096]{2,1,0:T(8,128)(2,1)} fusion(bf16[1152,192]{1,0:T(8,128)(2,1)S(1)} %copy-done.3, bf16[1152,4096]{1,0:T(8,128)(2,1)} %get-tuple-element.19), kind=kOutput, calls=%fused_computation.5 | convolution fusion | flops 1812725760 | bytes 11452416 | tf_op jit(solution)/shard_map/rf,rd->fd/dot_general | solution.py:189
  269.9 0.0 copy-done
  269.9 0.0 copy-done.2
  269.9 9.4 %fusion.5 = bf16[1,2,192,4096]{3,2,1,0:T(8,128)(2,1)} fusion(bf16[2,1152,192]{2,1,0:T(8,128)(2,1)S(1)} %copy-done.2, bf16[1152,4096]{1,0:T(8,128)(2,1)} %get-tuple-element.17), kind=kOutput, calls=%fused_computation.3 | convolution fusion | flops 3625451520 | bytes 13467648 | tf_op jit(solution)/shard_map/crf,rd->cfd/dot_general | solution.py:190
  279.3 2.8 shard_map.94
  282.1 0.0 all-to-all-done.2.refs_0_
  282.1 0.0 copy-start.1
  282.1 1.0 copy-done.1
  283.1 2.8 shard_map.96
  (1 shorter events, 0.0 us)
Async XLA Ops:
  7.2 113.5 %all-gather.2.cloned.1.call-start = ((), (), s32[]{:S(2)}) async-start(), calls=%async_computation.5 | async-start | bytes 33816576 | tf_op jit(solution)/shard_map/all_gather | solution.py:170
  10.3 13.6 %all-to-all-start = ((f32[16,1,128]{2,1,0:T(1,128)}), f32[16,1,128]{2,1,0:T(1,128)S(1)}, u32[]{:S(2)}, u32[]{:S(2)}) async-start(f32[16,1,128]{2,1,0:T(1,128)} %bitcast.3), calls=%async_computation | async-start | bytes 16384 | tf_op jit(solution)/shard_map/all_to_all | solution.py:175
  17.7 178.1 %reduce-scatter.3.cloned.1.call-start = ((), (), s32[]{:S(2)}) async-start(), calls=%async_computation.6 | async-start | bytes 10616832 | tf_op jit(solution)/shard_map/reduce_scatter | solution.py:154
  23.9 114.8 %copy-start.4 = (f32[16,1,128]{2,1,0:T(1,128)}, f32[16,1,128]{2,1,0:T(1,128)S(1)}, u32[]{:S(2)}) copy-start(f32[16,1,128]{2,1,0:T(1,128)S(1)} %all-to-all-done) | copy-start | bytes 24580
  138.7 116.7 %reduce-scatter.5.cloned.1.call-start = ((), (), s32[]{:S(2)}) async-start(), calls=%async_computation.7 | async-start | bytes 10616832 | tf_op jit(solution)/shard_map/reduce_scatter | solution.py:154
  160.3 102.4 %copy-start.3 = (bf16[1152,192]{1,0:T(8,128)(2,1)S(1)}, bf16[1152,192]{1,0:T(8,128)(2,1)}, u32[]{:S(2)}) copy-start(bf16[1152,192]{1,0:T(8,128)(2,1)} %get-tuple-element.18) | copy-start | bytes 1327108
  195.9 59.6 %all-to-all-start.1 = ((bf16[16,72,512]{2,1,0:T(8,128)(2,1)}), bf16[16,72,512]{2,1,0:T(8,128)(2,1)S(1)}, u32[]{:S(2)}, u32[]{:S(2)}) async-start(bf16[16,72,512]{2,1,0:T(8,128)(2,1)} %bitcast.38), calls=%async_computation.2 | async-start | bytes 2359296 | tf_op jit(solution)/shard_map/all_to_all | solution.py:155
  255.4 14.5 %copy-start = (bf16[16,72,512]{2,1,0:T(8,128)(2,1)}, bf16[16,72,512]{2,1,0:T(8,128)(2,1)S(1)}, u32[]{:S(2)}) copy-start(bf16[16,72,512]{2,1,0:T(8,128)(2,1)S(1)} %all-to-all-done.1.refs_0_) | copy-start | bytes 3538948
  255.4 26.7 %all-to-all-start.2 = ((bf16[16,72,512]{2,1,0:T(8,128)(2,1)}), bf16[16,72,512]{2,1,0:T(8,128)(2,1)S(1)}, u32[]{:S(2)}, u32[]{:S(2)}) async-start(bf16[16,72,512]{2,1,0:T(8,128)(2,1)} %bitcast.37), calls=%async_computation.4 | async-start | bytes 2359296 | tf_op jit(solution)/shard_map/all_to_all | solution.py:155
  262.7 7.2 %copy-start.2 = (bf16[2,1152,192]{2,1,0:T(8,128)(2,1)S(1)}, bf16[2,1152,192]{2,1,0:T(8,128)(2,1)}, u32[]{:S(2)}) copy-start(bf16[2,1152,192]{2,1,0:T(8,128)(2,1)} %get-tuple-element.16) | copy-start | bytes 2654212
  282.1 1.0 copy-start.1
Sparse Core Ops, SparseCore 0:
  11.6 109.0 all-gather.1
  138.9 56.9 reduce-scatter.2
  198.3 57.0 reduce-scatter.4

commit v2 on v1

v2 whole, which is shorter than its diff:
```python
import jax
import jax.numpy as jnp
from jax import lax
from jax.experimental import pallas as pl
from jax.experimental.pallas import tpu as pltpu
from jax.sharding import PartitionSpec as P

EXPERTS = 16
CAP = 72
GROUPS = 16
TOK = 128
D = 4096
UNITS = 192
TENSOR = 8
SHARE = D // TENSOR
HALF = D // 2
DEPTH = TENSOR // 2
STEP_GROUPS = 4
PAIRS = STEP_GROUPS // 2
ROWS = STEP_GROUPS * CAP
STEPS = GROUPS // STEP_GROUPS
ALL_ROWS = GROUPS * CAP
F32 = jnp.float32
BF16 = jnp.bfloat16
VMEM_LIMIT = 56 * 1024 * 1024


def nt(a, b):
    return lax.dot_general(a, b, (((1,), (1,)), ((), ())), preferred_element_type=F32)


def nn(a, b):
    return lax.dot_general(a, b, (((1,), (0,)), ((), ())), preferred_element_type=F32)


def pick_kernel(x_ref, w_ref, o_ref):
    mask = w_ref[...] > 0.0
    earlier = lax.broadcasted_iota(jnp.int32, (TOK, TOK), 0) < lax.broadcasted_iota(jnp.int32, (TOK, TOK), 1)
    ones = jnp.where(mask, 1.0, 0.0).astype(BF16)
    slot = nn(ones, jnp.where(earlier, 1.0, 0.0).astype(BF16))
    slot = jnp.where(mask, slot, -1.0).astype(jnp.int32)
    x = x_ref[...]
    for e in range(EXPERTS):
        hit = lax.broadcasted_iota(jnp.int32, (CAP, TOK), 0) == slot[e : e + 1]
        o_ref[e] = nn(jnp.where(hit, 1.0, 0.0).astype(BF16), x).astype(BF16)


def forward_kernel(
    core_ref, own_ref, other_ref, wgu_ref, wd_ref, in_ref, gate_ref, up_ref, hid_ref, keep_ref, send_ref
):
    core = core_ref[0]
    in_ref[:, pl.ds(pl.multiple_of(core * HALF, HALF), HALF)] = own_ref[...]
    in_ref[:, pl.ds(pl.multiple_of((1 - core) * HALF, HALF), HALF)] = other_ref[...]
    rows = in_ref[...]
    gate = nt(rows, wgu_ref[0])
    up = nt(rows, wgu_ref[1])
    gate_ref[...] = gate
    up_ref[...] = up
    hidden = (gate * jax.nn.sigmoid(gate) * up).astype(BF16)
    hid_ref[...] = hidden
    for ref, parity in ((send_ref, 1 - core), (keep_ref, core)):
        for z in range(DEPTH):
            cols = pl.ds(pl.multiple_of((2 * z + parity) * SHARE, SHARE), SHARE)
            ref[:, SHARE * z : SHARE * (z + 1)] = nn(hidden, wd_ref[:, cols]).astype(BF16)


def backward_kernel(g_ref, row_ref, w_ref, gate_ref, up_ref, wgu_ref, wd_ref, cot_ref, dgu_ref, back_ref):
    for j in range(PAIRS):
        g = g_ref[2 * TOK * j : 2 * TOK * (j + 1), :]
        hit = lax.broadcasted_iota(jnp.int32, (2 * CAP, 2 * TOK), 0) == row_ref[j]
        onehot = jnp.where(hit, 1.0, 0.0).astype(BF16)
        weight = jnp.sum(jnp.where(hit, w_ref[j], 0.0), axis=1, keepdims=True)
        cot_ref[2 * CAP * j : 2 * CAP * (j + 1), :] = (nn(onehot, g) * weight).astype(BF16)
    dhid = nt(cot_ref[...], wd_ref[...])
    gate = gate_ref[...]
    up = up_ref[...]
    sig = jax.nn.sigmoid(gate)
    dgate = (dhid * up * sig * (1.0 + gate * (1.0 - sig))).astype(BF16)
    dup = (dhid * gate * sig).astype(BF16)
    dgu_ref[0] = dgate
    dgu_ref[1] = dup
    for c in range(TENSOR):
        cols = slice(SHARE * c, SHARE * (c + 1))
        back_ref[c] = (nn(dgate, wgu_ref[0, :, cols]) + nn(dup, wgu_ref[1, :, cols])).astype(BF16)


def own_places(w_ref):
    w = w_ref[...]
    mask = w > 0.0
    ones = jnp.where(mask, 1.0, 0.0)
    lower = lax.broadcasted_iota(jnp.int32, (TOK, TOK), 1) < lax.broadcasted_iota(jnp.int32, (TOK, TOK), 0)
    slot = nn(jnp.where(lower, 1.0, 0.0).astype(BF16), ones.astype(BF16))
    return w, ones, jnp.where(mask, slot, -1.0).astype(jnp.int32)


def combine_kernel(r_ref, w_ref, o_ref):
    _, ones, slot = own_places(w_ref)
    total = jnp.zeros(o_ref.shape, F32)
    for e in range(EXPERTS):
        hit = lax.broadcasted_iota(jnp.int32, (TOK, CAP), 1) == slot[:, e : e + 1]
        onehot = jnp.where(hit, 1.0, 0.0).astype(BF16)
        total += nn(onehot, r_ref[e]) * ones[:, e : e + 1]
    o_ref[...] = total.astype(BF16)


def depth_kernel(z_ref, r_ref, w_ref, o_ref):
    w, _, slot = own_places(w_ref)
    total = jnp.zeros((TOK, SHARE), F32)
    for e in range(EXPERTS):
        hit = lax.broadcasted_iota(jnp.int32, (TOK, CAP), 1) == slot[:, e : e + 1]
        onehot = jnp.where(hit, 1.0, 0.0).astype(BF16)
        total += nn(onehot, r_ref[e]) * w[:, e : e + 1]
    o_ref[...] = total.astype(BF16)


def params():
    return pltpu.CompilerParams(vmem_limit_bytes=VMEM_LIMIT, dimension_semantics=("arbitrary",))


def whole(shape):
    return pl.BlockSpec(shape, lambda i: (0,) * len(shape), pipeline_mode=pl.Buffered(1))


ROW_SPEC = pl.BlockSpec((PAIRS, 1, 2 * TOK), lambda i: (i, 0, 0))
WIDE_SPEC = pl.BlockSpec((ROWS, D), lambda i: (i, 0))
UNIT_SPEC = pl.BlockSpec((ROWS, UNITS), lambda i: (i, 0))
SHARE_SPEC = pl.BlockSpec((TENSOR, ROWS, SHARE), lambda i: (0, i, 0))


def pick(x_half, weight_rows):
    return pl.pallas_call(
        pick_kernel,
        out_shape=jax.ShapeDtypeStruct((EXPERTS, CAP, HALF), BF16),
        compiler_params=pltpu.CompilerParams(vmem_limit_bytes=VMEM_LIMIT),
        cost_estimate=pl.CostEstimate(flops=600_000_000, bytes_accessed=5_300_000, transcendentals=0),
    )(x_half, weight_rows)


def forward(core, own, other, wgu, wd):
    wide = pl.BlockSpec((ROWS, D), lambda i, _: (i, 0))
    half = pl.BlockSpec((ROWS, HALF), lambda i, _: (i, 0))
    units = pl.BlockSpec((ROWS, UNITS), lambda i, _: (i, 0))
    once = pl.Buffered(1)
    return pl.pallas_call(
        forward_kernel,
        grid_spec=pltpu.PrefetchScalarGridSpec(
            num_scalar_prefetch=1,
            grid=(STEPS,),
            in_specs=[
                half,
                half,
                pl.BlockSpec(wgu.shape, lambda i, _: (0, 0, 0), pipeline_mode=once),
                pl.BlockSpec(wd.shape, lambda i, _: (0, 0), pipeline_mode=once),
            ],
            out_specs=[wide, units, units, units, half, half],
        ),
        out_shape=[
            jax.ShapeDtypeStruct((ALL_ROWS, D), BF16),
            jax.ShapeDtypeStruct((ALL_ROWS, UNITS), F32),
            jax.ShapeDtypeStruct((ALL_ROWS, UNITS), F32),
            jax.ShapeDtypeStruct((ALL_ROWS, UNITS), BF16),
            jax.ShapeDtypeStruct((ALL_ROWS, HALF), BF16),
            jax.ShapeDtypeStruct((ALL_ROWS, HALF), BF16),
        ],
        compiler_params=params(),
        cost_estimate=pl.CostEstimate(flops=6_000_000_000, bytes_accessed=36_000_000, transcendentals=221184),
    )(core, own, other, wgu, wd)


def backward(gathered, row_of, weight, gate, up, wgu, wd):
    return pl.pallas_call(
        backward_kernel,
        grid=(STEPS,),
        in_specs=[
            pl.BlockSpec((STEP_GROUPS * TOK, D), lambda i: (i, 0)), ROW_SPEC, ROW_SPEC, UNIT_SPEC, UNIT_SPEC,
            whole(wgu.shape), whole(wd.shape),
        ],
        out_specs=[
            WIDE_SPEC, pl.BlockSpec((2, ROWS, UNITS), lambda i: (0, i, 0)), SHARE_SPEC,
        ],
        out_shape=[
            jax.ShapeDtypeStruct((ALL_ROWS, D), BF16),
            jax.ShapeDtypeStruct((2, ALL_ROWS, UNITS), BF16),
            jax.ShapeDtypeStruct((TENSOR, ALL_ROWS, SHARE), BF16),
        ],
        compiler_params=params(),
        cost_estimate=pl.CostEstimate(flops=8_000_000_000, bytes_accessed=42_000_000, transcendentals=221184),
    )(gathered, row_of, weight, gate, up, wgu, wd)


def combine(returned, own_weight):
    return pl.pallas_call(
        combine_kernel,
        out_shape=jax.ShapeDtypeStruct((TOK, SHARE), BF16),
        compiler_params=pltpu.CompilerParams(vmem_limit_bytes=VMEM_LIMIT),
        cost_estimate=pl.CostEstimate(flops=200_000_000, bytes_accessed=1_400_000, transcendentals=0),
    )(returned, own_weight)


def depth_parts(level, returned, own_weight):
    return pl.pallas_call(
        depth_kernel,
        grid_spec=pltpu.PrefetchScalarGridSpec(
            num_scalar_prefetch=1,
            grid=(DEPTH,),
            in_specs=[
                pl.BlockSpec((EXPERTS, CAP, SHARE), lambda d, z: (0, 0, (z[0] + d) % DEPTH)),
                pl.BlockSpec((TOK, EXPERTS), lambda d, z: (0, 0)),
            ],
            out_specs=pl.BlockSpec((None, TOK, SHARE), lambda d, z: (d, 0, 0)),
        ),
        out_shape=jax.ShapeDtypeStruct((DEPTH, TOK, SHARE), BF16),
        compiler_params=params(),
        cost_estimate=pl.CostEstimate(flops=800_000_000, bytes_accessed=5_300_000, transcendentals=0),
    )(level, returned, own_weight)


def over_experts(x):
    return lax.all_to_all(x, "expert", split_axis=0, concat_axis=0, tiled=True)


def swap_cores(x):
    return lax.ppermute(x, "tensor", [(t, t ^ 1) for t in range(TENSOR)])


def up_levels(x, d):
    return lax.ppermute(x, "tensor", [(t, (t + 2 * d) % TENSOR) for t in range(TENSOR)])


def on_device(tokens, expert_ids, gate_probs, grad_out, gate_up, down_proj):
    part = TOK // TENSOR
    member = lax.axis_index("tensor")
    core, level = member % 2, member // 2
    core_list, level_list = core.reshape(1).astype(jnp.int32), level.reshape(1).astype(jnp.int32)
    wgu, wd = gate_up[0], down_proj[0]

    mine = lax.dynamic_slice_in_dim(grad_out, member * part, part, 0)
    grad_rows = lax.all_gather(mine, ("expert", "tensor"), axis=0, tiled=True)

    named = expert_ids[:, :, None] == jnp.arange(EXPERTS, dtype=jnp.int32)
    own_weight = jnp.sum(jnp.where(named, gate_probs[:, :, None], 0.0), axis=1)
    weight_rows = own_weight.T
    x_half = lax.dynamic_slice_in_dim(tokens, core * HALF, HALF, 1)
    own_rows = over_experts(pick(x_half, weight_rows)).reshape(ALL_ROWS, HALF)
    other_rows = swap_cores(own_rows)
    weight_rows, own_rows = lax.optimization_barrier((weight_rows, own_rows))
    weight = over_experts(weight_rows)
    mask = weight > 0.0
    place = jnp.arange(TOK, dtype=jnp.int32)
    earlier = (place[:, None] < place[None, :]).astype(BF16)
    slot = jnp.dot(mask.astype(BF16), earlier, preferred_element_type=F32).astype(jnp.int32)
    offset = CAP * (jnp.arange(GROUPS, dtype=jnp.int32) % 2)
    row_of = jnp.where(mask, slot + offset[:, None], -1).reshape(GROUPS // 2, 1, 2 * TOK)
    weight = weight.reshape(GROUPS // 2, 1, 2 * TOK)

    inputs, gate, up, hidden, keep, send = forward(core_list, own_rows, other_rows, wgu, wd)
    pair_sum = (keep.astype(F32) + swap_cores(send).astype(F32)).astype(BF16)
    pair_sum, gate = lax.optimization_barrier((pair_sum, gate))
    out_back = over_experts(pair_sum.reshape(GROUPS, CAP, HALF))

    cot, dgu, partial_back = backward(grad_rows, row_of, weight, gate, up, wgu, wd)
    back_sum = lax.psum_scatter(partial_back, "tensor", scatter_dimension=0, tiled=False)
    grad_back = over_experts(back_sum.reshape(GROUPS, CAP, SHARE))
    grad_down = jnp.einsum("rf,rd->fd", hidden, cot, preferred_element_type=F32).astype(BF16)
    grad_gate_up = jnp.einsum("crf,rd->cfd", dgu, inputs, preferred_element_type=F32).astype(BF16)

    parts = depth_parts(level_list, out_back, own_weight)
    mixed = parts[0].astype(F32)
    for d in range(1, DEPTH):
        mixed += up_levels(parts[d], d).astype(F32)
    grad_tokens = combine(grad_back, own_weight)
    return (mixed.astype(BF16), grad_tokens, grad_gate_up[None], grad_down[None])


def solution(mesh):
    return jax.shard_map(
        on_device,
        mesh=mesh,
        in_specs=(
            P("expert", None),
            P("expert", None),
            P("expert", None),
            P("expert", None),
            P("expert", None, "tensor", None),
            P("expert", "tensor", None),
        ),
        out_specs=(
            P("expert", "tensor"),
            P("expert", "tensor"),
            P("expert", None, "tensor", None),
            P("expert", "tensor", None),
        ),
        check_vma=False,
    )
```

time: 293 us -> 282 us (0.962)
  waiting for transfers between devices: 189 us -> 85.2 us
  blocking collectives: 0 us -> 69.5 us
  other arithmetic: 2.04 us -> 11.5 us
  Pallas kernels: 45.2 us -> 50.5 us
  local copies, waits for them, and re-layouts: 3.48 us -> 8.23 us
    all_gather x1, waiting for transfers between devices: 96.1 us -> 0.01 us  [on_device(): grad_rows = lax.all_gather(mine, ('expert', 'tensor'), axis=0, tiled=True)]
    reduce_scatter x2 -> x1, waiting for transfers between devices: 86.4 us -> 0.01 us  [on_device(): lax.psum_scatter(partial_back, 'tensor', scatter_dimension=0, tiled=False)]
    all_to_all x0 -> x1, blocking collectives: none -> 69.5 us  [over_experts(): return lax.all_to_all(x, 'expert', split_axis=0, concat_axis=0, tiled=True)]
    all_to_all x3, waiting for transfers between devices: 6.07 us -> 71.7 us  [over_experts(): return lax.all_to_all(x, 'expert', split_axis=0, concat_axis=0, tiled=True)]
    ppermute x0 -> x5, waiting for transfers between devices: none -> 13.4 us  [the longest x2 7.91 us: swap_cores(): return lax.ppermute(x, 'tensor', [(t, t ^ 1) for t in range(TENSOR)])]
    convert_element_type x0 -> x2, other arithmetic: none -> 10.1 us  [the longest x1 8.52 us: on_device(): pair_sum = (keep.astype(F32) + swap_cores(send).astype(F32)).astype(BF16)]
    pallas_call x4 -> x5, Pallas kernels: 45.2 us -> 50.5 us  [the longest x1 21.5 us: backward(): pl.pallas_call(backward_kernel, grid=(STEPS,), in_specs=[pl.BlockSpec((ST...]
    ppermute x0 -> x5, starting transfers between devices: none -> 4.67 us  [the longest x3 4.31 us: up_levels(): lax.ppermute(x, 'tensor', [(t, (t + 2 * d) % TENSOR) for t in range(TENSO...]
  transfers between devices with their start and end apart: 6 -> 10, of which waited for: 4 -> 6; matrix products, arithmetic and copies ran while one was open for 7% -> 11% of each run, Pallas kernels for 8% -> 9%
where the time goes in v2:
time: 282 us; the launch traced here: 281 us
  waiting for transfers between devices  85.2 us (30%)
  blocking collectives  69.5 us (25%)
  Pallas kernels  50.5 us (18%)
  starting transfers between devices  24.8 us (9%)
  matrix products  17.4 us (6%)
  between operations  14.1 us (5%)
  other arithmetic  11.5 us (4%)
  local copies, waits for them, and re-layouts  8.23 us (3%)
    all_to_all x3, waiting for transfers between devices, over_experts(): return lax.all_to_all(x, 'expert', split_axis=0, concat_axis=0, tiled=True)  71.7 us
    all_to_all x1, blocking collectives, over_experts(): return lax.all_to_all(x, 'expert', split_axis=0, concat_axis=0, tiled=True)  69.5 us
    pallas_call x1, Pallas kernels, backward(): pl.pallas_call(backward_kernel, grid=(STEPS,), in_specs=[pl.BlockSpec((ST...  21.5 us
    all_to_all x3, starting transfers between devices, over_experts(): return lax.all_to_all(x, 'expert', split_axis=0, concat_axis=0, tiled=True)  20.1 us
    pallas_call x1, Pallas kernels, forward(): pl.pallas_call(forward_kernel, grid_spec=pltpu.PrefetchScalarGridSpec(num...  15.2 us
    dot_general x1, matrix products, on_device(): jnp.einsum('crf,rd->cfd', dgu, inputs, preferred_element_type=F32)  9.45 us
    convert_element_type x1, other arithmetic, on_device(): pair_sum = (keep.astype(F32) + swap_cores(send).astype(F32)).astype(BF16)  8.52 us
    ppermute x2, waiting for transfers between devices, swap_cores(): return lax.ppermute(x, 'tensor', [(t, t ^ 1) for t in range(TENSOR)])  7.91 us
  transfers between devices with their start and end apart: 10, of which 6 were waited for; matrix products, arithmetic and copies ran while one was open for 11% of the time, Pallas kernels for 9%

profile of v2, /device:TPU:2, one launch (start us, length us, event | category | flops | bytes accessed | tf_op | source)
XLA Modules:
  0.0 281.2 jit_solution(7760139740532289453)
XLA Ops:
  7.2 0.0 copy-start
  7.2 0.0 all-gather.2.cloned.1.call-start
  7.2 1.6 constant_dynamic-slice_fusion
  8.9 0.0 all-gather.2.cloned.1.call-update
  8.9 1.3 select_reduce_fusion
  10.2 0.0 copy-done
  10.2 0.8 constant_dynamic-slice_fusion.1.x_ref
  11.1 4.8 %shard_map.93 = bf16[16,72,2048]{2,1,0:T(8,128)(2,1)} custom-call(bf16[128,2048]{1,0:T(8,128)(2,1)} %constant_dynamic-slice_fusion.1.x_ref, f32[16,128]{1,0:T(8,128)} %bitcast.2.w_ref), custom_call_target="tpu_custom_call" | custom-call | flops 600000000 | bytes 5300000 | tf_op jit(solution)/shard_map/pallas_call | solution.py:131
  15.9 69.5 %all_to_all.24 = bf16[16,72,2048]{2,1,0:T(8,128)(2,1)S(1)} all-to-all(bf16[16,72,2048]{2,1,0:T(8,128)(2,1)} %shard_map.93), channel_id=1, replica_groups=mesh['expert'=16,'tensor'=8] {'expert'}, dimensions={0} | all-to-all | bytes 9437184 | tf_op jit(solution)/shard_map/all_to_all | solution.py:219
  85.5 0.0 copy-start.2
  85.5 0.0 collective-permute-start
  85.5 7.9 %collective-permute-done.other_ref = bf16[1152,2048]{1,0:T(8,128)(2,1)S(1)} collective-permute-done((bf16[1152,2048]{1,0:T(8,128)(2,1)S(1)}, bf16[1152,2048]{1,0:T(8,128)(2,1)S(1)}, u32[]{:S(2)}, u32[]{:S(2)}) %collective-permute-start) | collective-permute-done | bytes 4718624 | tf_op jit(solution)/shard_map/ppermute | solution.py:223
  93.4 0.0 copy-start.7
  93.4 2.1 copy-done.7
  95.5 0.0 copy-done.2
  95.5 15.2 %shard_map.94 = (bf16[1152,4096]{1,0:T(8,128)(2,1)}, f32[1152,192]{1,0:T(8,128)}, f32[1152,192]{1,0:T(8,128)}, bf16[1152,192]{1,0:T(8,128)(2,1)}, bf16[1152,2048...) custom-call(s32[1]{0:T(128)} %bitcast.1.core_ref, bf16[1152,2048]{1,0:T(8,128)(2,1)} %bitcast.44, bf16[1152,2048]{1,0:T(8,128)(2,1)} %copy-done.7, ...), custom_call_target="tpu_custom_call" | custom-call | flops 6000000000 | bytes 36000000 | tf_op jit(solution)/shard_map/pallas_call | solution.py:144
  110.7 0.4 collective-permute-start.1
  111.1 5.5 %all-to-all-start.2 = ((f32[16,1,128]{2,1,0:T(1,128)}), f32[16,1,128]{2,1,0:T(1,128)S(1)}, u32[]{:S(2)}, u32[]{:S(2)}) async-start(f32[16,1,128]{2,1,0:T(1,128)} %bitcast.12), calls=%async_computation.2 | async-start | bytes 16384 | tf_op jit(solution)/shard_map/all_to_all | solution.py:219
  116.6 0.0 reduce-scatter.2.cloned.1.call-start
  116.6 6.1 %all-to-all-done.2 = f32[16,1,128]{2,1,0:T(1,128)S(1)} async-done(((f32[16,1,128]{2,1,0:T(1,128)}), f32[16,1,128]{2,1,0:T(1,128)S(1)}, u32[]{:S(2)}, u32[]{:S(2)}) %all-to-all-start.2) | async-done | bytes 8224 | tf_op jit(solution)/shard_map/all_to_all | solution.py:219
  122.7 0.0 copy-start.6
  122.7 0.7 fusion.10
  123.4 0.0 collective-permute-done.1
  123.4 8.5 %add_convert_fusion = bf16[1152,2048]{1,0:T(8,128)(2,1)} fusion(bf16[1152,2048]{1,0:T(8,128)(2,1)} %collective-permute-done.1, bf16[1152,2048]{1,0:T(8,128)(2,1)} %get-tuple-element.18), kind=kLoop, calls=%fused_computation.2 | loop fusion | flops 9437184 | bytes 14155776 | tf_op jit(solution)/shard_map/convert_element_type | solution.py:257
  131.9 0.0 copy-done.6
  131.9 0.0 all-gather.2.cloned.1.call-done.g_ref
  131.9 21.5 %shard_map.96 = (bf16[1152,4096]{1,0:T(8,128)(2,1)}, bf16[2,1152,192]{2,1,0:T(8,128)(2,1)}, bf16[8,1152,512]{2,1,0:T(8,128)(2,1)}) custom-call(bf16[2048,4096]{1,0:T(8,128)(2,1)} %all-gather.2.cloned.1.call-done.g_ref, s32[8,1,256]{2,1,0:T(1,128)} %bitcast.52, f32[8,1,256]{2,1,0:T(1,128)} %bitcast.47, f32[1152,192]{1,0:T(8,128)} %get-tuple-element.23.gate_ref, ...), custom_call_target="tpu_custom_call" | custom-call | flops 8000000000 | bytes 42000000 | tf_op jit(solution)/shard_map/pallas_call | solution.py:171
  153.4 0.0 reduce-scatter.2.cloned.1.call-update
  153.5 5.8 %all-to-all-start.1 = ((bf16[16,72,2048]{2,1,0:T(8,128)(2,1)}), bf16[16,72,2048]{2,1,0:T(8,128)(2,1)}, u32[]{:S(2)}, u32[]{:S(2)}) async-start(bf16[16,72,2048]{2,1,0:T(8,128)(2,1)} %bitcast.42), calls=%async_computation.1 | async-start | bytes 9437184 | tf_op jit(solution)/shard_map/all_to_all | solution.py:219
  159.2 0.0 copy-start.5
  159.3 1.5 copy.32.w_ref
  160.7 65.7 %all-to-all-done.1.r_ref = bf16[16,72,2048]{2,1,0:T(8,128)(2,1)} async-done(((bf16[16,72,2048]{2,1,0:T(8,128)(2,1)}), bf16[16,72,2048]{2,1,0:T(8,128)(2,1)}, u32[]{:S(2)}, u32[]{:S(2)}) %all-to-all-start.1) | async-done | bytes 4718624 | tf_op jit(solution)/shard_map/all_to_all | solution.py:219
  226.4 6.1 %shard_map.95 = bf16[4,128,512]{2,1,0:T(8,128)(2,1)} custom-call(s32[1]{0:T(128)} %bitcast.z_ref, bf16[16,72,2048]{2,1,0:T(8,128)(2,1)} %all-to-all-done.1.r_ref, f32[128,16]{1,0:T(8,128)} %copy.32.w_ref), custom_call_target="tpu_custom_call" | custom-call | flops 800000000 | bytes 5300000 | tf_op jit(solution)/shard_map/pallas_call | solution.py:201
  232.5 1.1 slice_bitcast_fusion.2
  233.6 0.1 collective-permute-start.2
  233.7 3.2 %collective-permute-start.4 = (bf16[128,512]{1,0:T(8,128)(2,1)S(1)}, bf16[128,512]{1,0:T(8,128)(2,1)S(1)}, u32[]{:S(2)}, u32[]{:S(2)}) collective-permute-start(bf16[128,512]{1,0:T(8,128)(2,1)S(1)} %get-tuple-element.31), channel_id=1, source_target_pairs={{0,6},{1,7},{2,0},{3,1},{4,2},{5,3},{6,4},{7,5},{8,14},{9,15},{10,... | collective-permute-start | bytes 393224 | tf_op jit(solution)/shard_map/ppermute | solution.py:227
  236.9 1.0 collective-permute-start.3
  237.9 2.7 collective-permute-done.2
  240.6 0.5 collective-permute-done.4
  241.1 2.3 collective-permute-done.3
  243.4 1.6 fusion.13
  245.0 0.0 reduce-scatter.2.cloned.1.call-done
  245.0 8.8 %all-to-all-start.3 = ((bf16[16,72,512]{2,1,0:T(8,128)(2,1)}), bf16[16,72,512]{2,1,0:T(8,128)(2,1)S(1)}, u32[]{:S(2)}, u32[]{:S(2)}) async-start(bf16[16,72,512]{2,1,0:T(8,128)(2,1)} %bitcast.45), calls=%async_computation.4 | async-start | bytes 2359296 | tf_op jit(solution)/shard_map/all_to_all | solution.py:219
  253.8 0.0 copy-done.5
  253.8 0.0 copy-start.4
  253.8 7.2 %fusion.8 = bf16[1,192,4096]{2,1,0:T(8,128)(2,1)} fusion(bf16[1152,192]{1,0:T(8,128)(2,1)S(1)} %copy-done.5, bf16[1152,4096]{1,0:T(8,128)(2,1)} %get-tuple-element.29), kind=kOutput, calls=%fused_computation.6 | convolution fusion | flops 1812725760 | bytes 11452416 | tf_op jit(solution)/shard_map/rf,rd->fd/dot_general | solution.py:264
  261.0 0.0 copy-start.1
  261.0 0.0 copy-done.4
  261.0 9.5 %fusion.5 = bf16[1,2,192,4096]{3,2,1,0:T(8,128)(2,1)} fusion(bf16[2,1152,192]{2,1,0:T(8,128)(2,1)S(1)} %copy-done.4, bf16[1152,4096]{1,0:T(8,128)(2,1)} %get-tuple-element.27), kind=kOutput, calls=%fused_computation.4 | convolution fusion | flops 3625451520 | bytes 13467648 | tf_op jit(solution)/shard_map/crf,rd->cfd/dot_general | solution.py:265
  270.5 0.0 all-to-all-done.3.r_ref
  270.5 0.0 copy-start.3
  270.5 1.0 copy-done.3
  271.5 2.8 %shard_map.97 = bf16[128,512]{1,0:T(8,128)(2,1)} custom-call(bf16[16,72,512]{2,1,0:T(8,128)(2,1)} %copy-done.3, f32[128,16]{1,0:T(8,128)} %copy.32.w_ref), custom_call_target="tpu_custom_call" | custom-call | flops 200000000 | bytes 1400000 | tf_op jit(solution)/shard_map/pallas_call | solution.py:192
  274.3 0.0 copy-done.1
  (1 shorter events, 0.0 us)
Async XLA Ops:
  7.2 3.1 %copy-start = (bf16[128,4096]{1,0:T(8,128)(2,1)S(1)}, bf16[128,4096]{1,0:T(8,128)(2,1)}, u32[]{:S(2)}) copy-start(bf16[128,4096]{1,0:T(8,128)(2,1)} %param.6) | copy-start | bytes 3145732
  7.2 124.8 %all-gather.2.cloned.1.call-start = ((), (), s32[]{:S(2)}) async-start(), calls=%async_computation.5 | async-start | bytes 16908288 | tf_op jit(solution)/shard_map/all_gather | solution.py:238
  85.5 10.1 %copy-start.2 = (bf16[16,72,2048]{2,1,0:T(8,128)(2,1)}, bf16[16,72,2048]{2,1,0:T(8,128)(2,1)S(1)}, u32[]{:S(2)}) copy-start(bf16[16,72,2048]{2,1,0:T(8,128)(2,1)S(1)} %all_to_all.24) | copy-start | bytes 14155780
  85.5 7.9 %collective-permute-start = (bf16[1152,2048]{1,0:T(8,128)(2,1)S(1)}, bf16[1152,2048]{1,0:T(8,128)(2,1)S(1)}, u32[]{:S(2)}, u32[]{:S(2)}) collective-permute-start(bf16[1152,2048]{1,0:T(8,128)(2,1)S(1)} %bitcast.43), channel_id=1, source_target_pairs={{0,1},{1,0},{2,3},{3,2},{4,5},{5,4},{6,7},{7,6},{8,9},{9,8},{10,11... | collective-permute-start | bytes 14155784 | tf_op jit(solution)/shard_map/ppermute | solution.py:223
  93.4 2.1 copy-start.7
  110.7 12.7 %collective-permute-start.1 = (bf16[1152,2048]{1,0:T(8,128)(2,1)}, bf16[1152,2048]{1,0:T(8,128)(2,1)}, u32[]{:S(2)}, u32[]{:S(2)}) collective-permute-start(bf16[1152,2048]{1,0:T(8,128)(2,1)} %get-tuple-element.19), channel_id=1, source_target_pairs={{0,1},{1,0},{2,3},{3,2},{4,5},{5,4},{6,7},{7,6},{8,9},{9,8},{10,11... | collective-permute-start | bytes 14155784 | tf_op jit(solution)/shard_map/ppermute | solution.py:223
  111.1 11.6 %all-to-all-start.2 = ((f32[16,1,128]{2,1,0:T(1,128)}), f32[16,1,128]{2,1,0:T(1,128)S(1)}, u32[]{:S(2)}, u32[]{:S(2)}) async-start(f32[16,1,128]{2,1,0:T(1,128)} %bitcast.12), calls=%async_computation.2 | async-start | bytes 16384 | tf_op jit(solution)/shard_map/all_to_all | solution.py:219
  116.6 128.5 %reduce-scatter.2.cloned.1.call-start = ((), (), s32[]{:S(2)}) async-start(), calls=%async_computation.6 | async-start | bytes 10616832 | tf_op jit(solution)/shard_map/reduce_scatter | solution.py:262
  122.7 9.3 %copy-start.6 = (f32[16,1,128]{2,1,0:T(1,128)}, f32[16,1,128]{2,1,0:T(1,128)S(1)}, u32[]{:S(2)}) copy-start(f32[16,1,128]{2,1,0:T(1,128)S(1)} %all-to-all-done.2) | copy-start | bytes 24580
  153.5 73.0 %all-to-all-start.1 = ((bf16[16,72,2048]{2,1,0:T(8,128)(2,1)}), bf16[16,72,2048]{2,1,0:T(8,128)(2,1)}, u32[]{:S(2)}, u32[]{:S(2)}) async-start(bf16[16,72,2048]{2,1,0:T(8,128)(2,1)} %bitcast.42), calls=%async_computation.1 | async-start | bytes 9437184 | tf_op jit(solution)/shard_map/all_to_all | solution.py:219
  159.2 94.6 %copy-start.5 = (bf16[1152,192]{1,0:T(8,128)(2,1)S(1)}, bf16[1152,192]{1,0:T(8,128)(2,1)}, u32[]{:S(2)}) copy-start(bf16[1152,192]{1,0:T(8,128)(2,1)} %get-tuple-element.28) | copy-start | bytes 1327108
  233.6 7.0 %collective-permute-start.2 = (bf16[128,512]{1,0:T(8,128)(2,1)S(1)}, bf16[128,512]{1,0:T(8,128)(2,1)S(1)}, u32[]{:S(2)}, u32[]{:S(2)}) collective-permute-start(bf16[128,512]{1,0:T(8,128)(2,1)S(1)} %get-tuple-element.30), channel_id=1, source_target_pairs={{0,2},{1,3},{2,4},{3,5},{4,6},{5,7},{6,0},{7,1},{8,10},{9,11},{10,... | collective-permute-start | bytes 393224 | tf_op jit(solution)/shard_map/ppermute | solution.py:227
  233.7 7.4 %collective-permute-start.4 = (bf16[128,512]{1,0:T(8,128)(2,1)S(1)}, bf16[128,512]{1,0:T(8,128)(2,1)S(1)}, u32[]{:S(2)}, u32[]{:S(2)}) collective-permute-start(bf16[128,512]{1,0:T(8,128)(2,1)S(1)} %get-tuple-element.31), channel_id=1, source_target_pairs={{0,6},{1,7},{2,0},{3,1},{4,2},{5,3},{6,4},{7,5},{8,14},{9,15},{10,... | collective-permute-start | bytes 393224 | tf_op jit(solution)/shard_map/ppermute | solution.py:227
  236.9 6.5 %collective-permute-start.3 = (bf16[128,512]{1,0:T(8,128)(2,1)S(1)}, bf16[128,512]{1,0:T(8,128)(2,1)S(1)}, u32[]{:S(2)}, u32[]{:S(2)}) collective-permute-start(bf16[128,512]{1,0:T(8,128)(2,1)S(1)} %get-tuple-element.32), channel_id=1, source_target_pairs={{0,4},{1,5},{2,6},{3,7},{4,0},{5,1},{6,2},{7,3},{8,12},{9,13},{10,... | collective-permute-start | bytes 393224 | tf_op jit(solution)/shard_map/ppermute | solution.py:227
  245.0 25.5 %all-to-all-start.3 = ((bf16[16,72,512]{2,1,0:T(8,128)(2,1)}), bf16[16,72,512]{2,1,0:T(8,128)(2,1)S(1)}, u32[]{:S(2)}, u32[]{:S(2)}) async-start(bf16[16,72,512]{2,1,0:T(8,128)(2,1)} %bitcast.45), calls=%async_computation.4 | async-start | bytes 2359296 | tf_op jit(solution)/shard_map/all_to_all | solution.py:219
  253.8 7.2 %copy-start.4 = (bf16[2,1152,192]{2,1,0:T(8,128)(2,1)S(1)}, bf16[2,1152,192]{2,1,0:T(8,128)(2,1)}, u32[]{:S(2)}) copy-start(bf16[2,1152,192]{2,1,0:T(8,128)(2,1)} %get-tuple-element.26) | copy-start | bytes 2654212
  261.0 13.3 %copy-start.1 = (bf16[128,4096]{1,0:T(8,128)(2,1)S(1)}, bf16[128,4096]{1,0:T(8,128)(2,1)}, u32[]{:S(2)}) copy-start(bf16[128,4096]{1,0:T(8,128)(2,1)} %param.6) | copy-start | bytes 3145732
  270.5 1.0 copy-start.3
Sparse Core Ops, SparseCore 0:
  11.7 110.8 all-gather.1
  153.6 57.0 reduce-scatter.1

commit v3 on v2

--- a/solution.py
+++ b/solution.py
@@ -211,7 +211,7 @@
         ),
         out_shape=jax.ShapeDtypeStruct((DEPTH, TOK, SHARE), BF16),
         compiler_params=params(),
-        cost_estimate=pl.CostEstimate(flops=800_000_000, bytes_accessed=5_300_000, transcendentals=0),
+        cost_estimate=pl.CostEstimate(flops=170_000_000_000, bytes_accessed=5_300_000, transcendentals=0),
     )(level, returned, own_weight)
 
 
@@ -264,6 +264,7 @@
     grad_down = jnp.einsum("rf,rd->fd", hidden, cot, preferred_element_type=F32).astype(BF16)
     grad_gate_up = jnp.einsum("crf,rd->cfd", dgu, inputs, preferred_element_type=F32).astype(BF16)
 
+    out_back, _ = lax.optimization_barrier((out_back, back_sum))
     parts = depth_parts(level_list, out_back, own_weight)
     mixed = parts[0].astype(F32)
     for d in range(1, DEPTH):

time: 282 us -> 262 us (0.929)
  waiting for transfers between devices: 85.2 us -> 66.4 us
  matrix products: 17.4 us -> 13.7 us
    all_to_all x3, waiting for transfers between devices: 71.7 us -> 48.2 us  [over_experts(): return lax.all_to_all(x, 'expert', split_axis=0, concat_axis=0, tiled=True)]
    ppermute x2, waiting for transfers between devices: 7.91 us -> 12.4 us  [swap_cores(): return lax.ppermute(x, 'tensor', [(t, t ^ 1) for t in range(TENSOR)])]
    dot_general x1, matrix products: 9.45 us -> 5.73 us  [on_device(): jnp.einsum('crf,rd->cfd', dgu, inputs, preferred_element_type=F32)]
  transfers between devices with their start and end apart: 10 -> 10, of which waited for: 6 -> 7; matrix products, arithmetic and copies ran while one was open for 11% -> 11% of each run, Pallas kernels for 9% -> 18%
where the time goes in v3:
time: 262 us; the launch traced here: 260 us
  blocking collectives  69.5 us (27%)
  waiting for transfers between devices  66.4 us (25%)
  Pallas kernels  50.6 us (19%)
  starting transfers between devices  26.4 us (10%)
  between operations  14.1 us (5%)
  matrix products  13.7 us (5%)
  other arithmetic  11.5 us (4%)
  local copies, waits for them, and re-layouts  8.16 us (3%)
    all_to_all x1, blocking collectives, over_experts(): return lax.all_to_all(x, 'expert', split_axis=0, concat_axis=0, tiled=True)  69.5 us
    all_to_all x3, waiting for transfers between devices, over_experts(): return lax.all_to_all(x, 'expert', split_axis=0, concat_axis=0, tiled=True)  48.2 us
    pallas_call x1, Pallas kernels, backward(): pl.pallas_call(backward_kernel, grid=(STEPS,), in_specs=[pl.BlockSpec((ST...  21.5 us
    all_to_all x3, starting transfers between devices, over_experts(): return lax.all_to_all(x, 'expert', split_axis=0, concat_axis=0, tiled=True)  21.4 us
    pallas_call x1, Pallas kernels, forward(): pl.pallas_call(forward_kernel, grid_spec=pltpu.PrefetchScalarGridSpec(num...  15.2 us
    ppermute x2, waiting for transfers between devices, swap_cores(): return lax.ppermute(x, 'tensor', [(t, t ^ 1) for t in range(TENSOR)])  12.4 us
    convert_element_type x1, other arithmetic, on_device(): pair_sum = (keep.astype(F32) + swap_cores(send).astype(F32)).astype(BF16)  8.51 us
    dot_general x1, matrix products, on_device(): jnp.einsum('rf,rd->fd', hidden, cot, preferred_element_type=F32)  7.23 us
  transfers between devices with their start and end apart: 10, of which 7 were waited for; matrix products, arithmetic and copies ran while one was open for 11% of the time, Pallas kernels for 18%

profile of v3, /device:TPU:2, one launch (start us, length us, event | category | flops | bytes accessed | tf_op | source)
XLA Modules:
  0.0 260.3 jit_solution(16413945853516700692)
XLA Ops:
  7.2 0.0 copy-start
  7.2 0.0 all-gather.2.cloned.1.call-start
  7.2 1.6 constant_dynamic-slice_fusion
  8.9 0.0 all-gather.2.cloned.1.call-update
  8.9 1.3 select_reduce_fusion
  10.2 0.0 copy-done
  10.2 0.8 constant_dynamic-slice_fusion.1.x_ref
  11.1 4.8 %shard_map.93 = bf16[16,72,2048]{2,1,0:T(8,128)(2,1)} custom-call(bf16[128,2048]{1,0:T(8,128)(2,1)} %constant_dynamic-slice_fusion.1.x_ref, f32[16,128]{1,0:T(8,128)} %bitcast.2.w_ref), custom_call_target="tpu_custom_call" | custom-call | flops 600000000 | bytes 5300000 | tf_op jit(solution)/shard_map/pallas_call | solution.py:131
  15.9 69.5 %all_to_all.24 = bf16[16,72,2048]{2,1,0:T(8,128)(2,1)S(1)} all-to-all(bf16[16,72,2048]{2,1,0:T(8,128)(2,1)} %shard_map.93), channel_id=1, replica_groups=mesh['expert'=16,'tensor'=8] {'expert'}, dimensions={0} | all-to-all | bytes 9437184 | tf_op jit(solution)/shard_map/all_to_all | solution.py:219
  85.4 0.0 copy-start.3
  85.4 0.0 collective-permute-start
  85.5 7.9 %collective-permute-done.other_ref = bf16[1152,2048]{1,0:T(8,128)(2,1)S(1)} collective-permute-done((bf16[1152,2048]{1,0:T(8,128)(2,1)S(1)}, bf16[1152,2048]{1,0:T(8,128)(2,1)S(1)}, u32[]{:S(2)}, u32[]{:S(2)}) %collective-permute-start) | collective-permute-done | bytes 4718624 | tf_op jit(solution)/shard_map/ppermute | solution.py:223
  93.4 0.0 copy-start.8
  93.4 2.1 copy-done.8
  95.5 0.0 copy-done.3
  95.5 15.2 %shard_map.94 = (bf16[1152,4096]{1,0:T(8,128)(2,1)}, f32[1152,192]{1,0:T(8,128)}, f32[1152,192]{1,0:T(8,128)}, bf16[1152,192]{1,0:T(8,128)(2,1)}, bf16[1152,2048...) custom-call(s32[1]{0:T(128)} %bitcast.1.core_ref, bf16[1152,2048]{1,0:T(8,128)(2,1)} %bitcast.44, bf16[1152,2048]{1,0:T(8,128)(2,1)} %copy-done.8, ...), custom_call_target="tpu_custom_call" | custom-call | flops 6000000000 | bytes 36000000 | tf_op jit(solution)/shard_map/pallas_call | solution.py:144
  110.7 0.5 collective-permute-start.1
  111.2 5.4 %all-to-all-start.2 = ((f32[16,1,128]{2,1,0:T(1,128)}), f32[16,1,128]{2,1,0:T(1,128)S(1)}, u32[]{:S(2)}, u32[]{:S(2)}) async-start(f32[16,1,128]{2,1,0:T(1,128)} %bitcast.12), calls=%async_computation.2 | async-start | bytes 16384 | tf_op jit(solution)/shard_map/all_to_all | solution.py:219
  116.6 4.5 %collective-permute-done.1 = bf16[1152,2048]{1,0:T(8,128)(2,1)} collective-permute-done((bf16[1152,2048]{1,0:T(8,128)(2,1)}, bf16[1152,2048]{1,0:T(8,128)(2,1)}, u32[]{:S(2)}, u32[]{:S(2)}) %collective-permute-start.1) | collective-permute-done | bytes 4718624 | tf_op jit(solution)/shard_map/ppermute | solution.py:223
  121.1 8.5 %add_convert_fusion = bf16[1152,2048]{1,0:T(8,128)(2,1)} fusion(bf16[1152,2048]{1,0:T(8,128)(2,1)} %collective-permute-done.1, bf16[1152,2048]{1,0:T(8,128)(2,1)} %get-tuple-element.18), kind=kLoop, calls=%fused_computation.2 | loop fusion | flops 9437184 | bytes 14155776 | tf_op jit(solution)/shard_map/convert_element_type | solution.py:257
  129.6 0.0 all-to-all-done.2
  129.6 0.0 copy-start.7
  129.6 7.3 %all-to-all-start.1 = ((bf16[16,72,2048]{2,1,0:T(8,128)(2,1)}), bf16[16,72,2048]{2,1,0:T(8,128)(2,1)}, u32[]{:S(2)}, u32[]{:S(2)}) async-start(bf16[16,72,2048]{2,1,0:T(8,128)(2,1)} %bitcast.42), calls=%async_computation.1 | async-start | bytes 9437184 | tf_op jit(solution)/shard_map/all_to_all | solution.py:219
  136.9 0.0 reduce-scatter.2.cloned.1.call-start
  136.9 0.0 copy-done.7
  136.9 0.7 fusion.10
  137.7 0.0 all-gather.2.cloned.1.call-done.g_ref
  137.7 21.5 %shard_map.96 = (bf16[1152,4096]{1,0:T(8,128)(2,1)}, bf16[2,1152,192]{2,1,0:T(8,128)(2,1)}, bf16[8,1152,512]{2,1,0:T(8,128)(2,1)}) custom-call(bf16[2048,4096]{1,0:T(8,128)(2,1)} %all-gather.2.cloned.1.call-done.g_ref, s32[8,1,256]{2,1,0:T(1,128)} %bitcast.52, f32[8,1,256]{2,1,0:T(1,128)} %bitcast.47, f32[1152,192]{1,0:T(8,128)} %get-tuple-element.23.gate_ref, ...), custom_call_target="tpu_custom_call" | custom-call | flops 8000000000 | bytes 42000000 | tf_op jit(solution)/shard_map/pallas_call | solution.py:171
  159.2 0.0 reduce-scatter.2.cloned.1.call-update
  159.2 1.4 copy.32.w_ref
  160.6 44.8 %all-to-all-done.1.r_ref = bf16[16,72,2048]{2,1,0:T(8,128)(2,1)} async-done(((bf16[16,72,2048]{2,1,0:T(8,128)(2,1)}), bf16[16,72,2048]{2,1,0:T(8,128)(2,1)}, u32[]{:S(2)}, u32[]{:S(2)}) %all-to-all-start.1) | async-done | bytes 4718624 | tf_op jit(solution)/shard_map/all_to_all | solution.py:219
  205.4 0.0 copy-start.6
  205.4 6.2 %shard_map.95 = bf16[4,128,512]{2,1,0:T(8,128)(2,1)} custom-call(s32[1]{0:T(128)} %bitcast.z_ref, bf16[16,72,2048]{2,1,0:T(8,128)(2,1)} %all-to-all-done.1.r_ref, f32[128,16]{1,0:T(8,128)} %copy.32.w_ref), custom_call_target="tpu_custom_call" | custom-call | flops 170000007168 | bytes 5300000 | tf_op jit(solution)/shard_map/pallas_call | solution.py:201
  211.6 1.1 slice_bitcast_fusion.2
  212.6 0.1 collective-permute-start.2
  212.7 3.2 %collective-permute-start.4 = (bf16[128,512]{1,0:T(8,128)(2,1)S(1)}, bf16[128,512]{1,0:T(8,128)(2,1)S(1)}, u32[]{:S(2)}, u32[]{:S(2)}) collective-permute-start(bf16[128,512]{1,0:T(8,128)(2,1)S(1)} %get-tuple-element.31), channel_id=1, source_target_pairs={{0,6},{1,7},{2,0},{3,1},{4,2},{5,3},{6,4},{7,5},{8,14},{9,15},{10,... | collective-permute-start | bytes 393224 | tf_op jit(solution)/shard_map/ppermute | solution.py:227
  215.9 1.1 collective-permute-start.3
  217.0 2.6 collective-permute-done.2
  219.6 1.7 collective-permute-done.4
  221.3 1.5 collective-permute-done.3
  222.8 1.6 fusion.13
  224.4 0.0 reduce-scatter.2.cloned.1.call-done
  224.4 8.8 %all-to-all-start.3 = ((bf16[16,72,512]{2,1,0:T(8,128)(2,1)}), bf16[16,72,512]{2,1,0:T(8,128)(2,1)S(1)}, u32[]{:S(2)}, u32[]{:S(2)}) async-start(bf16[16,72,512]{2,1,0:T(8,128)(2,1)} %bitcast.45), calls=%async_computation.4 | async-start | bytes 2359296 | tf_op jit(solution)/shard_map/all_to_all | solution.py:219
  233.2 0.0 copy-done.6
  233.2 0.0 copy-start.2
  233.2 0.0 copy-start.5
  233.2 7.2 %fusion.8 = bf16[1,192,4096]{2,1,0:T(8,128)(2,1)} fusion(bf16[1152,192]{1,0:T(8,128)(2,1)S(1)} %copy-done.6, bf16[1152,4096]{1,0:T(8,128)(2,1)} %get-tuple-element.29), kind=kOutput, calls=%fused_computation.6 | convolution fusion | flops 1812725760 | bytes 11452416 | tf_op jit(solution)/shard_map/rf,rd->fd/dot_general | solution.py:264
  240.4 0.0 copy-start.1
  240.4 0.0 copy-done.2
  240.4 0.0 copy-done.5
  240.4 5.7 %fusion.5 = bf16[1,2,192,4096]{3,2,1,0:T(8,128)(2,1)} fusion(bf16[2,1152,192]{2,1,0:T(8,128)(2,1)S(1)} %copy-done.5, bf16[1152,4096]{1,0:T(8,128)(2,1)S(1)} %copy-done.2), kind=kOutput, calls=%fused_computation.4 | convolution fusion | flops 3625451520 | bytes 13467648 | tf_op jit(solution)/shard_map/crf,rd->cfd/dot_general | solution.py:265
  246.2 3.5 %all-to-all-done.3.r_ref = bf16[16,72,512]{2,1,0:T(8,128)(2,1)S(1)} async-done(((bf16[16,72,512]{2,1,0:T(8,128)(2,1)}), bf16[16,72,512]{2,1,0:T(8,128)(2,1)S(1)}, u32[]{:S(2)}, u32[]{:S(2)}) %all-to-all-start.3) | async-done | bytes 1179680 | tf_op jit(solution)/shard_map/all_to_all | solution.py:219
  249.6 0.0 copy-start.4
  249.6 1.0 copy-done.4
  250.7 2.8 %shard_map.97 = bf16[128,512]{1,0:T(8,128)(2,1)} custom-call(bf16[16,72,512]{2,1,0:T(8,128)(2,1)} %copy-done.4, f32[128,16]{1,0:T(8,128)} %copy.32.w_ref), custom_call_target="tpu_custom_call" | custom-call | flops 200000000 | bytes 1400000 | tf_op jit(solution)/shard_map/pallas_call | solution.py:192
  253.5 0.0 copy-done.1
  (1 shorter events, 0.0 us)
Async XLA Ops:
  7.2 3.1 %copy-start = (bf16[128,4096]{1,0:T(8,128)(2,1)S(1)}, bf16[128,4096]{1,0:T(8,128)(2,1)}, u32[]{:S(2)}) copy-start(bf16[128,4096]{1,0:T(8,128)(2,1)} %param.6) | copy-start | bytes 3145732
  7.2 130.5 %all-gather.2.cloned.1.call-start = ((), (), s32[]{:S(2)}) async-start(), calls=%async_computation.5 | async-start | bytes 16908288 | tf_op jit(solution)/shard_map/all_gather | solution.py:238
  85.4 10.1 %copy-start.3 = (bf16[16,72,2048]{2,1,0:T(8,128)(2,1)}, bf16[16,72,2048]{2,1,0:T(8,128)(2,1)S(1)}, u32[]{:S(2)}) copy-start(bf16[16,72,2048]{2,1,0:T(8,128)(2,1)S(1)} %all_to_all.24) | copy-start | bytes 14155780
  85.4 7.9 %collective-permute-start = (bf16[1152,2048]{1,0:T(8,128)(2,1)S(1)}, bf16[1152,2048]{1,0:T(8,128)(2,1)S(1)}, u32[]{:S(2)}, u32[]{:S(2)}) collective-permute-start(bf16[1152,2048]{1,0:T(8,128)(2,1)S(1)} %bitcast.43), channel_id=1, source_target_pairs={{0,1},{1,0},{2,3},{3,2},{4,5},{5,4},{6,7},{7,6},{8,9},{9,8},{10,11... | collective-permute-start | bytes 14155784 | tf_op jit(solution)/shard_map/ppermute | solution.py:223
  93.4 2.1 copy-start.8
  110.7 10.4 %collective-permute-start.1 = (bf16[1152,2048]{1,0:T(8,128)(2,1)}, bf16[1152,2048]{1,0:T(8,128)(2,1)}, u32[]{:S(2)}, u32[]{:S(2)}) collective-permute-start(bf16[1152,2048]{1,0:T(8,128)(2,1)} %get-tuple-element.19), channel_id=1, source_target_pairs={{0,1},{1,0},{2,3},{3,2},{4,5},{5,4},{6,7},{7,6},{8,9},{9,8},{10,11... | collective-permute-start | bytes 14155784 | tf_op jit(solution)/shard_map/ppermute | solution.py:223
  111.2 18.4 %all-to-all-start.2 = ((f32[16,1,128]{2,1,0:T(1,128)}), f32[16,1,128]{2,1,0:T(1,128)S(1)}, u32[]{:S(2)}, u32[]{:S(2)}) async-start(f32[16,1,128]{2,1,0:T(1,128)} %bitcast.12), calls=%async_computation.2 | async-start | bytes 16384 | tf_op jit(solution)/shard_map/all_to_all | solution.py:219
  129.6 7.3 %copy-start.7 = (f32[16,1,128]{2,1,0:T(1,128)}, f32[16,1,128]{2,1,0:T(1,128)S(1)}, u32[]{:S(2)}) copy-start(f32[16,1,128]{2,1,0:T(1,128)S(1)} %all-to-all-done.2) | copy-start | bytes 24580
  129.6 75.8 %all-to-all-start.1 = ((bf16[16,72,2048]{2,1,0:T(8,128)(2,1)}), bf16[16,72,2048]{2,1,0:T(8,128)(2,1)}, u32[]{:S(2)}, u32[]{:S(2)}) async-start(bf16[16,72,2048]{2,1,0:T(8,128)(2,1)} %bitcast.42), calls=%async_computation.1 | async-start | bytes 9437184 | tf_op jit(solution)/shard_map/all_to_all | solution.py:219
  136.9 87.5 %reduce-scatter.2.cloned.1.call-start = ((), (), s32[]{:S(2)}) async-start(), calls=%async_computation.6 | async-start | bytes 10616832 | tf_op jit(solution)/shard_map/reduce_scatter | solution.py:262
  205.4 27.8 %copy-start.6 = (bf16[1152,192]{1,0:T(8,128)(2,1)S(1)}, bf16[1152,192]{1,0:T(8,128)(2,1)}, u32[]{:S(2)}) copy-start(bf16[1152,192]{1,0:T(8,128)(2,1)} %get-tuple-element.28) | copy-start | bytes 1327108
  212.6 7.0 %collective-permute-start.2 = (bf16[128,512]{1,0:T(8,128)(2,1)S(1)}, bf16[128,512]{1,0:T(8,128)(2,1)S(1)}, u32[]{:S(2)}, u32[]{:S(2)}) collective-permute-start(bf16[128,512]{1,0:T(8,128)(2,1)S(1)} %get-tuple-element.30), channel_id=1, source_target_pairs={{0,2},{1,3},{2,4},{3,5},{4,6},{5,7},{6,0},{7,1},{8,10},{9,11},{10,... | collective-permute-start | bytes 393224 | tf_op jit(solution)/shard_map/ppermute | solution.py:227
  212.7 8.5 %collective-permute-start.4 = (bf16[128,512]{1,0:T(8,128)(2,1)S(1)}, bf16[128,512]{1,0:T(8,128)(2,1)S(1)}, u32[]{:S(2)}, u32[]{:S(2)}) collective-permute-start(bf16[128,512]{1,0:T(8,128)(2,1)S(1)} %get-tuple-element.31), channel_id=1, source_target_pairs={{0,6},{1,7},{2,0},{3,1},{4,2},{5,3},{6,4},{7,5},{8,14},{9,15},{10,... | collective-permute-start | bytes 393224 | tf_op jit(solution)/shard_map/ppermute | solution.py:227
  215.9 6.8 %collective-permute-start.3 = (bf16[128,512]{1,0:T(8,128)(2,1)S(1)}, bf16[128,512]{1,0:T(8,128)(2,1)S(1)}, u32[]{:S(2)}, u32[]{:S(2)}) collective-permute-start(bf16[128,512]{1,0:T(8,128)(2,1)S(1)} %get-tuple-element.32), channel_id=1, source_target_pairs={{0,4},{1,5},{2,6},{3,7},{4,0},{5,1},{6,2},{7,3},{8,12},{9,13},{10,... | collective-permute-start | bytes 393224 | tf_op jit(solution)/shard_map/ppermute | solution.py:227
  224.4 25.2 %all-to-all-start.3 = ((bf16[16,72,512]{2,1,0:T(8,128)(2,1)}), bf16[16,72,512]{2,1,0:T(8,128)(2,1)S(1)}, u32[]{:S(2)}, u32[]{:S(2)}) async-start(bf16[16,72,512]{2,1,0:T(8,128)(2,1)} %bitcast.45), calls=%async_computation.4 | async-start | bytes 2359296 | tf_op jit(solution)/shard_map/all_to_all | solution.py:219
  233.2 7.3 %copy-start.2 = (bf16[1152,4096]{1,0:T(8,128)(2,1)S(1)}, bf16[1152,4096]{1,0:T(8,128)(2,1)}, u32[]{:S(2)}) copy-start(bf16[1152,4096]{1,0:T(8,128)(2,1)} %get-tuple-element.27) | copy-start | bytes 28311556
  233.2 7.2 %copy-start.5 = (bf16[2,1152,192]{2,1,0:T(8,128)(2,1)S(1)}, bf16[2,1152,192]{2,1,0:T(8,128)(2,1)}, u32[]{:S(2)}) copy-start(bf16[2,1152,192]{2,1,0:T(8,128)(2,1)} %get-tuple-element.26) | copy-start | bytes 2654212
  240.4 13.1 %copy-start.1 = (bf16[128,4096]{1,0:T(8,128)(2,1)S(1)}, bf16[128,4096]{1,0:T(8,128)(2,1)}, u32[]{:S(2)}) copy-start(bf16[128,4096]{1,0:T(8,128)(2,1)} %param.6) | copy-start | bytes 3145732
  249.6 1.0 copy-start.4
Sparse Core Ops, SparseCore 0:
  11.7 110.9 all-gather.1
  159.3 58.8 reduce-scatter.1

commit v4 on v2

--- a/solution.py
+++ b/solution.py
@@ -11,6 +11,7 @@
 TOK = 128
 D = 4096
 UNITS = 192
+WIDE = 256
 TENSOR = 8
 SHARE = D // TENSOR
 HALF = D // 2
@@ -29,6 +30,10 @@
     return lax.dot_general(a, b, (((1,), (1,)), ((), ())), preferred_element_type=F32)
 
 
+def tn(a, b):
+    return lax.dot_general(a, b, (((0,), (0,)), ((), ())), preferred_element_type=F32)
+
+
 def nn(a, b):
     return lax.dot_general(a, b, (((1,), (0,)), ((), ())), preferred_element_type=F32)
 
@@ -45,9 +50,12 @@
         o_ref[e] = nn(jnp.where(hit, 1.0, 0.0).astype(BF16), x).astype(BF16)
 
 
-def forward_kernel(
-    core_ref, own_ref, other_ref, wgu_ref, wd_ref, in_ref, gate_ref, up_ref, hid_ref, keep_ref, send_ref
-):
+def lend_kernel(core_ref, after_ref, wgu_ref, wd_ref, o_ref):
+    o_ref[0:2] = wgu_ref[...]
+    o_ref[2] = wd_ref[...]
+
+
+def hidden_kernel(core_ref, own_ref, other_ref, wgu_ref, in_ref, gate_ref, up_ref, hid_ref):
     core = core_ref[0]
     in_ref[:, pl.ds(pl.multiple_of(core * HALF, HALF), HALF)] = own_ref[...]
     in_ref[:, pl.ds(pl.multiple_of((1 - core) * HALF, HALF), HALF)] = other_ref[...]
@@ -56,15 +64,19 @@
     up = nt(rows, wgu_ref[1])
     gate_ref[...] = gate
     up_ref[...] = up
-    hidden = (gate * jax.nn.sigmoid(gate) * up).astype(BF16)
-    hid_ref[...] = hidden
-    for ref, parity in ((send_ref, 1 - core), (keep_ref, core)):
-        for z in range(DEPTH):
-            cols = pl.ds(pl.multiple_of((2 * z + parity) * SHARE, SHARE), SHARE)
-            ref[:, SHARE * z : SHARE * (z + 1)] = nn(hidden, wd_ref[:, cols]).astype(BF16)
-
-
-def backward_kernel(g_ref, row_ref, w_ref, gate_ref, up_ref, wgu_ref, wd_ref, cot_ref, dgu_ref, back_ref):
+    hid_ref[:, :UNITS] = (gate * jax.nn.sigmoid(gate) * up).astype(BF16)
+    hid_ref[:, UNITS:] = jnp.zeros((ROWS, WIDE - UNITS), BF16)
+
+
+def out_kernel(core_ref, own_ref, other_ref, wd_ref, lent_ref, o_ref):
+    own, other = own_ref[:, :UNITS], other_ref[:, :UNITS]
+    for z in range(DEPTH):
+        cols = pl.ds(pl.multiple_of((2 * z + core_ref[0]) * SHARE, SHARE), SHARE)
+        share = slice(SHARE * z, SHARE * (z + 1))
+        o_ref[:, share] = (nn(own, wd_ref[:, cols]) + nn(other, lent_ref[:, share])).astype(BF16)
+
+
+def unit_grad_kernel(g_ref, row_ref, w_ref, gate_ref, up_ref, wd_ref, cot_ref, dgu_ref):
     for j in range(PAIRS):
         g = g_ref[2 * TOK * j : 2 * TOK * (j + 1), :]
         hit = lax.broadcasted_iota(jnp.int32, (2 * CAP, 2 * TOK), 0) == row_ref[j]
@@ -75,13 +87,26 @@
     gate = gate_ref[...]
     up = up_ref[...]
     sig = jax.nn.sigmoid(gate)
-    dgate = (dhid * up * sig * (1.0 + gate * (1.0 - sig))).astype(BF16)
-    dup = (dhid * gate * sig).astype(BF16)
-    dgu_ref[0] = dgate
-    dgu_ref[1] = dup
-    for c in range(TENSOR):
-        cols = slice(SHARE * c, SHARE * (c + 1))
-        back_ref[c] = (nn(dgate, wgu_ref[0, :, cols]) + nn(dup, wgu_ref[1, :, cols])).astype(BF16)
+    dgu_ref[:, :, UNITS:] = jnp.zeros((2, ROWS, WIDE - UNITS), BF16)
+    dgu_ref[0, :, :UNITS] = (dhid * up * sig * (1.0 + gate * (1.0 - sig))).astype(BF16)
+    dgu_ref[1, :, :UNITS] = (dhid * gate * sig).astype(BF16)
+
+
+def weight_grad_kernel(in_ref, cot_ref, dgu_ref, hid_ref, gu_ref, down_ref):
+    x = in_ref[...]
+    gu_ref[0] = tn(dgu_ref[0, :, :UNITS], x).astype(BF16)
+    gu_ref[1] = tn(dgu_ref[1, :, :UNITS], x).astype(BF16)
+    down_ref[...] = tn(hid_ref[:, :UNITS], cot_ref[...]).astype(BF16)
+
+
+def back_kernel(core_ref, own_ref, other_ref, wgu_ref, lent_ref, o_ref):
+    for z in range(DEPTH):
+        cols = pl.ds(pl.multiple_of((2 * z + core_ref[0]) * SHARE, SHARE), SHARE)
+        share = slice(SHARE * z, SHARE * (z + 1))
+        total = nn(own_ref[0, :, :UNITS], wgu_ref[0, :, cols]) + nn(own_ref[1, :, :UNITS], wgu_ref[1, :, cols])
+        total += nn(other_ref[0, :, :UNITS], lent_ref[0, :, share])
+        total += nn(other_ref[1, :, :UNITS], lent_ref[1, :, share])
+        o_ref[z] = total.astype(BF16)
 
 
 def own_places(w_ref):
@@ -118,13 +143,30 @@
 
 
 def whole(shape):
-    return pl.BlockSpec(shape, lambda i: (0,) * len(shape), pipeline_mode=pl.Buffered(1))
-
-
-ROW_SPEC = pl.BlockSpec((PAIRS, 1, 2 * TOK), lambda i: (i, 0, 0))
-WIDE_SPEC = pl.BlockSpec((ROWS, D), lambda i: (i, 0))
-UNIT_SPEC = pl.BlockSpec((ROWS, UNITS), lambda i: (i, 0))
-SHARE_SPEC = pl.BlockSpec((TENSOR, ROWS, SHARE), lambda i: (0, i, 0))
+    return pl.BlockSpec(shape, lambda *_: (0,) * len(shape), pipeline_mode=pl.Buffered(1))
+
+
+def by_rows(*shape):
+    return pl.BlockSpec(shape, lambda i, *_: (0,) * (len(shape) - 2) + (i, 0))
+
+
+def shaped(*shape, dtype=BF16):
+    return jax.ShapeDtypeStruct(shape, dtype)
+
+
+def stepped(kernel, scalars, steps, in_specs, out_specs, out_shape, flops, moved):
+    return pl.pallas_call(
+        kernel,
+        grid_spec=pltpu.PrefetchScalarGridSpec(
+            num_scalar_prefetch=scalars, grid=(steps,), in_specs=in_specs, out_specs=out_specs
+        ),
+        out_shape=out_shape,
+        compiler_params=params(),
+        cost_estimate=pl.CostEstimate(flops=flops, bytes_accessed=moved, transcendentals=0),
+    )
+
+
+ROW_SPEC = pl.BlockSpec((PAIRS, 1, 2 * TOK), lambda i, *_: (i, 0, 0))
 
 
 def pick(x_half, weight_rows):
@@ -136,56 +178,75 @@
     )(x_half, weight_rows)
 
 
-def forward(core, own, other, wgu, wd):
-    wide = pl.BlockSpec((ROWS, D), lambda i, _: (i, 0))
-    half = pl.BlockSpec((ROWS, HALF), lambda i, _: (i, 0))
-    units = pl.BlockSpec((ROWS, UNITS), lambda i, _: (i, 0))
-    once = pl.Buffered(1)
-    return pl.pallas_call(
-        forward_kernel,
-        grid_spec=pltpu.PrefetchScalarGridSpec(
-            num_scalar_prefetch=1,
-            grid=(STEPS,),
-            in_specs=[
-                half,
-                half,
-                pl.BlockSpec(wgu.shape, lambda i, _: (0, 0, 0), pipeline_mode=once),
-                pl.BlockSpec(wd.shape, lambda i, _: (0, 0), pipeline_mode=once),
-            ],
-            out_specs=[wide, units, units, units, half, half],
-        ),
-        out_shape=[
-            jax.ShapeDtypeStruct((ALL_ROWS, D), BF16),
-            jax.ShapeDtypeStruct((ALL_ROWS, UNITS), F32),
-            jax.ShapeDtypeStruct((ALL_ROWS, UNITS), F32),
-            jax.ShapeDtypeStruct((ALL_ROWS, UNITS), BF16),
-            jax.ShapeDtypeStruct((ALL_ROWS, HALF), BF16),
-            jax.ShapeDtypeStruct((ALL_ROWS, HALF), BF16),
-        ],
-        compiler_params=params(),
-        cost_estimate=pl.CostEstimate(flops=6_000_000_000, bytes_accessed=36_000_000, transcendentals=221184),
-    )(core, own, other, wgu, wd)
-
-
-def backward(gathered, row_of, weight, gate, up, wgu, wd):
-    return pl.pallas_call(
-        backward_kernel,
-        grid=(STEPS,),
-        in_specs=[
-            pl.BlockSpec((STEP_GROUPS * TOK, D), lambda i: (i, 0)), ROW_SPEC, ROW_SPEC, UNIT_SPEC, UNIT_SPEC,
-            whole(wgu.shape), whole(wd.shape),
-        ],
-        out_specs=[
-            WIDE_SPEC, pl.BlockSpec((2, ROWS, UNITS), lambda i: (0, i, 0)), SHARE_SPEC,
-        ],
-        out_shape=[
-            jax.ShapeDtypeStruct((ALL_ROWS, D), BF16),
-            jax.ShapeDtypeStruct((2, ALL_ROWS, UNITS), BF16),
-            jax.ShapeDtypeStruct((TENSOR, ALL_ROWS, SHARE), BF16),
-        ],
-        compiler_params=params(),
-        cost_estimate=pl.CostEstimate(flops=8_000_000_000, bytes_accessed=42_000_000, transcendentals=221184),
-    )(gathered, row_of, weight, gate, up, wgu, wd)
+def lend(other_core, after, wgu, wd):
+    return stepped(
+        lend_kernel, 1, DEPTH,
+        [
+            pl.BlockSpec(memory_space=pl.ANY),
+            pl.BlockSpec((2, UNITS, SHARE), lambda z, c: (0, 0, 2 * z + c[0])),
+            pl.BlockSpec((UNITS, SHARE), lambda z, c: (0, 2 * z + c[0])),
+        ],
+        pl.BlockSpec((3, UNITS, SHARE), lambda z, c: (0, 0, z)),
+        shaped(3, UNITS, HALF), 0, 4_700_000,
+    )(other_core, after, wgu, wd)
+
+
+def hidden_units(core, own, other, wgu):
+    return stepped(
+        hidden_kernel, 1, STEPS,
+        [by_rows(ROWS, HALF), by_rows(ROWS, HALF), whole(wgu.shape)],
+        [by_rows(ROWS, D), by_rows(ROWS, UNITS), by_rows(ROWS, UNITS), by_rows(ROWS, WIDE)],
+        [
+            shaped(ALL_ROWS, D), shaped(ALL_ROWS, UNITS, dtype=F32), shaped(ALL_ROWS, UNITS, dtype=F32),
+            shaped(ALL_ROWS, WIDE),
+        ],
+        4_000_000_000, 25_000_000,
+    )(core, own, other, wgu)
+
+
+def out_rows(core, own, other, wd, lent):
+    return stepped(
+        out_kernel, 1, STEPS,
+        [
+            by_rows(ROWS, WIDE), by_rows(ROWS, WIDE), whole(wd.shape),
+            pl.BlockSpec((None, UNITS, HALF), lambda *_: (2, 0, 0), pipeline_mode=pl.Buffered(1)),
+        ],
+        by_rows(ROWS, HALF), shaped(ALL_ROWS, HALF), 2_000_000_000, 8_000_000,
+    )(core, own, other, wd, lent)
+
+
+def unit_grads(grad_rows, row_of, weight, gate, up, wd):
+    return stepped(
+        unit_grad_kernel, 0, STEPS,
+        [
+            by_rows(STEP_GROUPS * TOK, D), ROW_SPEC, ROW_SPEC, by_rows(ROWS, UNITS), by_rows(ROWS, UNITS),
+            whole(wd.shape),
+        ],
+        [by_rows(ROWS, D), by_rows(2, ROWS, WIDE)],
+        [shaped(ALL_ROWS, D), shaped(2, ALL_ROWS, WIDE)],
+        4_000_000_000, 30_000_000,
+    )(grad_rows, row_of, weight, gate, up, wd)
+
+
+def back_rows(core, own, other, wgu, lent):
+    return stepped(
+        back_kernel, 1, STEPS,
+        [by_rows(2, ROWS, WIDE), by_rows(2, ROWS, WIDE), whole(wgu.shape), whole((2, UNITS, HALF))],
+        by_rows(DEPTH, ROWS, SHARE), shaped(DEPTH, ALL_ROWS, SHARE), 4_000_000_000, 10_000_000,
+    )(core, own, other, wgu, lent)
+
+
+def weight_grads(inputs, cot, dgu, hidden):
+    cols = pl.BlockSpec((ALL_ROWS, SHARE), lambda i: (0, i))
+    return stepped(
+        weight_grad_kernel, 0, TENSOR,
+        [cols, cols, whole(dgu.shape), whole(hidden.shape)],
+        [
+            pl.BlockSpec((2, UNITS, SHARE), lambda i: (0, 0, i)),
+            pl.BlockSpec((UNITS, SHARE), lambda i: (0, i)),
+        ],
+        [shaped(2, UNITS, D), shaped(UNITS, D)], 6_000_000_000, 25_000_000,
+    )(inputs, cot, dgu, hidden)
 
 
 def combine(returned, own_weight):
@@ -211,7 +272,7 @@
         ),
         out_shape=jax.ShapeDtypeStruct((DEPTH, TOK, SHARE), BF16),
         compiler_params=params(),
-        cost_estimate=pl.CostEstimate(flops=800_000_000, bytes_accessed=5_300_000, transcendentals=0),
+        cost_estimate=pl.CostEstimate(flops=130000000000, bytes_accessed=5_300_000, transcendentals=0),
     )(level, returned, own_weight)
 
 
@@ -241,7 +302,10 @@
     own_weight = jnp.sum(jnp.where(named, gate_probs[:, :, None], 0.0), axis=1)
     weight_rows = own_weight.T
     x_half = lax.dynamic_slice_in_dim(tokens, core * HALF, HALF, 1)
-    own_rows = over_experts(pick(x_half, weight_rows)).reshape(ALL_ROWS, HALF)
+    picked = pick(x_half, weight_rows)
+    own_rows = over_experts(picked).reshape(ALL_ROWS, HALF)
+    lent = swap_cores(lend(1 - core_list, picked, wgu, wd))
+    own_rows, lent = lax.optimization_barrier((own_rows, lent))
     other_rows = swap_cores(own_rows)
     weight_rows, own_rows = lax.optimization_barrier((weight_rows, own_rows))
     weight = over_experts(weight_rows)
@@ -253,17 +317,19 @@
     row_of = jnp.where(mask, slot + offset[:, None], -1).reshape(GROUPS // 2, 1, 2 * TOK)
     weight = weight.reshape(GROUPS // 2, 1, 2 * TOK)
 
-    inputs, gate, up, hidden, keep, send = forward(core_list, own_rows, other_rows, wgu, wd)
-    pair_sum = (keep.astype(F32) + swap_cores(send).astype(F32)).astype(BF16)
-    pair_sum, gate = lax.optimization_barrier((pair_sum, gate))
-    out_back = over_experts(pair_sum.reshape(GROUPS, CAP, HALF))
-
-    cot, dgu, partial_back = backward(grad_rows, row_of, weight, gate, up, wgu, wd)
-    back_sum = lax.psum_scatter(partial_back, "tensor", scatter_dimension=0, tiled=False)
+    inputs, gate, up, hidden = hidden_units(core_list, own_rows, other_rows, wgu)
+    pair_out = out_rows(core_list, hidden, swap_cores(hidden), wd, lent)
+    pair_out, gate = lax.optimization_barrier((pair_out, gate))
+    out_back = over_experts(pair_out.reshape(GROUPS, CAP, HALF))
+
+    cot, dgu = unit_grads(grad_rows, row_of, weight, gate, up, wd)
+    pair_back = back_rows(core_list, dgu, swap_cores(dgu), wgu, lent)
+    back_sum = lax.psum_scatter(
+        pair_back, "tensor", scatter_dimension=0, tiled=False,
+        axis_index_groups=[[2 * z + c for z in range(DEPTH)] for c in range(2)],
+    )
     grad_back = over_experts(back_sum.reshape(GROUPS, CAP, SHARE))
-    grad_down = jnp.einsum("rf,rd->fd", hidden, cot, preferred_element_type=F32).astype(BF16)
-    grad_gate_up = jnp.einsum("crf,rd->cfd", dgu, inputs, preferred_element_type=F32).astype(BF16)
-
+    grad_gate_up, grad_down = weight_grads(inputs, cot, dgu, hidden)
     parts = depth_parts(level_list, out_back, own_weight)
     mixed = parts[0].astype(F32)
     for d in range(1, DEPTH):

time: 282 us -> 266 us (0.943)
  blocking collectives: 69.5 us -> 0 us
  waiting for transfers between devices: 85.2 us -> 133 us
  Pallas kernels: 50.5 us -> 70 us
  matrix products: 17.4 us -> 0.74 us
  starting transfers between devices: 24.8 us -> 34 us
  other arithmetic: 11.5 us -> 2.95 us
    all_to_all x1 -> x0, blocking collectives: 69.5 us -> none  [over_experts(): return lax.all_to_all(x, 'expert', split_axis=0, concat_axis=0, tiled=True)]
    all_to_all x3 -> x4, waiting for transfers between devices: 71.7 us -> 95.6 us  [over_experts(): return lax.all_to_all(x, 'expert', split_axis=0, concat_axis=0, tiled=True)]
    pallas_call x2 -> x6, Pallas kernels: 36.7 us -> 56.2 us  [the longest x1 13.5 us: weight_grads(): stepped(weight_grad_kernel, 0, TENSOR, [cols, cols, whole(dgu.shape), who...]
    dot_general x2 -> x0, matrix products: 16.6 us -> none  [the longest x1 9.45 us: on_device(): jnp.einsum('crf,rd->cfd', dgu, inputs, preferred_element_type=F32)]
    reduce_scatter x1, waiting for transfers between devices: 0.01 us -> 12.1 us  [on_device(): lax.psum_scatter(pair_back, 'tensor', scatter_dimension=0, tiled=False, a...]
    all_to_all x3 -> x4, starting transfers between devices: 20.1 us -> 30.6 us  [over_experts(): return lax.all_to_all(x, 'expert', split_axis=0, concat_axis=0, tiled=True)]
    convert_element_type x1 -> x0, other arithmetic: 8.52 us -> none  [on_device(): pair_sum = (keep.astype(F32) + swap_cores(send).astype(F32)).astype(BF16)]
    ppermute x2 -> x4, waiting for transfers between devices: 7.91 us -> 14.3 us  [swap_cores(): return lax.ppermute(x, 'tensor', [(t, t ^ 1) for t in range(TENSOR)])]
  transfers between devices with their start and end apart: 10 -> 13, of which waited for: 6 -> 10; matrix products, arithmetic and copies ran while one was open for 11% -> 3% of each run, Pallas kernels for 9% -> 25%
where the time goes in v4:
time: 266 us; the launch traced here: 265 us
  waiting for transfers between devices  133 us (50%)
  Pallas kernels  70 us (26%)
  starting transfers between devices  34 us (13%)
  between operations  14.1 us (5%)
  local copies, waits for them, and re-layouts  9.91 us (4%)
  other arithmetic  2.95 us (1%)
    all_to_all x4, waiting for transfers between devices, over_experts(): return lax.all_to_all(x, 'expert', split_axis=0, concat_axis=0, tiled=True)  95.6 us
    all_to_all x4, starting transfers between devices, over_experts(): return lax.all_to_all(x, 'expert', split_axis=0, concat_axis=0, tiled=True)  30.6 us
    ppermute x4, waiting for transfers between devices, swap_cores(): return lax.ppermute(x, 'tensor', [(t, t ^ 1) for t in range(TENSOR)])  14.3 us
    pallas_call x1, Pallas kernels, weight_grads(): stepped(weight_grad_kernel, 0, TENSOR, [cols, cols, whole(dgu.shape), who...  13.5 us
    reduce_scatter x1, waiting for transfers between devices, on_device(): lax.psum_scatter(pair_back, 'tensor', scatter_dimension=0, tiled=False, a...  12.1 us
    pallas_call x1, Pallas kernels, unit_grads(): stepped(unit_grad_kernel, 0, STEPS, [by_rows(STEP_GROUPS * TOK, D), ROW_S...  11.8 us
    pallas_call x1, Pallas kernels, hidden_units(): stepped(hidden_kernel, 1, STEPS, [by_rows(ROWS, HALF), by_rows(ROWS, HALF...  11.2 us
    pallas_call x1, Pallas kernels, back_rows(): stepped(back_kernel, 1, STEPS, [by_rows(2, ROWS, WIDE), by_rows(2, ROWS,...  9.24 us
  transfers between devices with their start and end apart: 13, of which 10 were waited for; matrix products, arithmetic and copies ran while one was open for 3% of the time, Pallas kernels for 25%

profile of v4, /device:TPU:2, one launch (start us, length us, event | category | flops | bytes accessed | tf_op | source)
XLA Modules:
  0.0 265.0 jit_solution(4110845921668189142)
XLA Ops:
  7.2 0.0 copy-start
  7.2 0.0 all-gather.2.cloned.1.call-start
  7.2 1.6 constant_dynamic-slice_fusion
  8.9 0.0 all-gather.2.cloned.1.call-update
  8.9 1.3 select_reduce_fusion
  10.2 0.0 copy-done
  10.2 0.8 constant_dynamic-slice_fusion.1.x_ref
  11.1 4.8 %shard_map.93.after_ref = bf16[16,72,2048]{2,1,0:T(8,128)(2,1)} custom-call(bf16[128,2048]{1,0:T(8,128)(2,1)} %constant_dynamic-slice_fusion.1.x_ref, f32[16,128]{1,0:T(8,128)} %bitcast.2.w_ref), custom_call_target="tpu_custom_call" | custom-call | flops 600000000 | bytes 5300000 | tf_op jit(solution)/shard_map/pallas_call | solution.py:173
  15.9 7.5 %all-to-all-start = ((bf16[16,72,2048]{2,1,0:T(8,128)(2,1)}), bf16[16,72,2048]{2,1,0:T(8,128)(2,1)}, u32[]{:S(2)}, u32[]{:S(2)}) async-start(bf16[16,72,2048]{2,1,0:T(8,128)(2,1)} %shard_map.93.after_ref), calls=%async_computation | async-start | bytes 9437184 | tf_op jit(solution)/shard_map/all_to_all | solution.py:280
  23.4 3.9 %shard_map.94 = bf16[3,192,2048]{2,1,0:T(8,128)(2,1)} custom-call(s32[1]{0:T(128)S(6)} %sub.8.core_ref, bf16[16,72,2048]{2,1,0:T(8,128)(2,1)} %shard_map.93.after_ref, bf16[2,192,4096]{2,1,0:T(8,128)(2,1)} %bitcast.34, bf16[192,4096]{1,0:T(8,128)(2,1)} %bitcast.31), custom_call_target="tpu_custom_call" | custom-call | bytes 4700000 | tf_op jit(solution)/shard_map/pallas_call | solution.py:182
  27.3 0.0 collective-permute-start
  27.3 4.7 %collective-permute-done.lent_ref = bf16[3,192,2048]{2,1,0:T(8,128)(2,1)S(1)} collective-permute-done((bf16[3,192,2048]{2,1,0:T(8,128)(2,1)}, bf16[3,192,2048]{2,1,0:T(8,128)(2,1)S(1)}, u32[]{:S(2)}, u32[]{:S(2)}) %collective-permute-start) | collective-permute-done | bytes 2359328 | tf_op jit(solution)/shard_map/ppermute | solution.py:284
  32.0 0.0 copy-start.3
  32.0 59.0 %all-to-all-done = bf16[16,72,2048]{2,1,0:T(8,128)(2,1)} async-done(((bf16[16,72,2048]{2,1,0:T(8,128)(2,1)}), bf16[16,72,2048]{2,1,0:T(8,128)(2,1)}, u32[]{:S(2)}, u32[]{:S(2)}) %all-to-all-start) | async-done | bytes 4718624 | tf_op jit(solution)/shard_map/all_to_all | solution.py:280
  91.0 0.0 collective-permute-start.1
  91.0 8.1 %collective-permute-done.1.other_ref = bf16[1152,2048]{1,0:T(8,128)(2,1)S(1)} collective-permute-done((bf16[1152,2048]{1,0:T(8,128)(2,1)}, bf16[1152,2048]{1,0:T(8,128)(2,1)S(1)}, u32[]{:S(2)}, u32[]{:S(2)}) %collective-permute-start.1) | collective-permute-done | bytes 4718624 | tf_op jit(solution)/shard_map/ppermute | solution.py:284
  99.1 0.0 copy-start.6
  99.1 2.1 copy-done.6
  101.2 11.2 %shard_map.95 = (bf16[1152,4096]{1,0:T(8,128)(2,1)}, f32[1152,192]{1,0:T(8,128)}, f32[1152,192]{1,0:T(8,128)}, bf16[1152,256]{1,0:T(8,128)(2,1)}) custom-call(s32[1]{0:T(128)} %bitcast.1.core_ref, bf16[1152,2048]{1,0:T(8,128)(2,1)} %bitcast.3.own_ref, bf16[1152,2048]{1,0:T(8,128)(2,1)} %copy-done.6, bf16[2,192,4096]{2,1,0:T(8,128)(2,1)} %bitcast.35), custom_call_target="tpu_custom_call" | custom-call | flops 4000000000 | bytes 25000000 | tf_op jit(solution)/shard_map/pallas_call | solution.py:195
  112.4 0.0 copy-done.3
  112.4 0.1 collective-permute-start.2
  112.5 8.6 %all-to-all-start.2 = ((f32[16,1,128]{2,1,0:T(1,128)}), f32[16,1,128]{2,1,0:T(1,128)S(1)}, u32[]{:S(2)}, u32[]{:S(2)}) async-start(f32[16,1,128]{2,1,0:T(1,128)} %bitcast.12), calls=%async_computation.2 | async-start | bytes 16384 | tf_op jit(solution)/shard_map/all_to_all | solution.py:280
  121.2 0.0 collective-permute-done.2.other_ref
  121.2 0.0 copy-start.4
  121.2 0.8 copy-done.4
  122.0 6.6 %shard_map.96 = bf16[1152,2048]{1,0:T(8,128)(2,1)} custom-call(s32[1]{0:T(128)} %bitcast.1.core_ref, bf16[1152,256]{1,0:T(8,128)(2,1)} %get-tuple-element.20.own_ref.hid_ref, bf16[1152,256]{1,0:T(8,128)(2,1)} %copy-done.4, bf16[192,4096]{1,0:T(8,128)(2,1)} %bitcast.32, bf16[3,192,2048]{2,1,0:T(8,128)(2,1)} %copy-done.3), custom_call_target="tpu_custom_call" | custom-call | flops 2000000000 | bytes 8000000 | tf_op jit(solution)/shard_map/pallas_call | solution.py:208
  128.6 0.0 all-to-all-done.2
  128.6 0.0 copy-start.5
  128.6 7.3 %all-to-all-start.1 = ((bf16[16,72,2048]{2,1,0:T(8,128)(2,1)}), bf16[16,72,2048]{2,1,0:T(8,128)(2,1)}, u32[]{:S(2)}, u32[]{:S(2)}) async-start(bf16[16,72,2048]{2,1,0:T(8,128)(2,1)} %bitcast.30), calls=%async_computation.1 | async-start | bytes 9437184 | tf_op jit(solution)/shard_map/all_to_all | solution.py:280
  135.9 0.0 reduce-scatter.2.cloned.1.call-start
  135.9 0.0 copy-done.5
  135.9 0.7 fusion.1
  136.7 4.6 %all-gather.2.cloned.1.call-done.g_ref = bf16[2048,4096]{1,0:T(8,128)(2,1)} async-done(((bf16[16,4096]{1,0:T(8,128)(2,1)}), bf16[2048,4096]{1,0:T(8,128)(2,1)}) %all-gather.2.cloned.1.call-update) | async-done | bytes 16777232 | tf_op jit(solution)/shard_map/all_gather | solution.py:299
  141.3 11.8 %shard_map.98 = (bf16[1152,4096]{1,0:T(8,128)(2,1)}, bf16[2,1152,256]{2,1,0:T(8,128)(2,1)}) custom-call(bf16[2048,4096]{1,0:T(8,128)(2,1)} %all-gather.2.cloned.1.call-done.g_ref, s32[8,1,256]{2,1,0:T(1,128)} %bitcast.40, f32[8,1,256]{2,1,0:T(1,128)} %bitcast.39, f32[1152,192]{1,0:T(8,128)} %get-tuple-element.25.gate_ref, ...), custom_call_target="tpu_custom_call" | custom-call | flops 4000000000 | bytes 30000000 | tf_op jit(solution)/shard_map/pallas_call | solution.py:219
  153.1 0.3 collective-permute-start.6
  153.4 1.4 copy.29.w_ref
  154.8 1.4 collective-permute-done.6.other_ref
  156.2 0.0 copy-start.7
  156.2 1.0 copy-done.7
  157.2 9.2 %shard_map.99 = bf16[4,1152,512]{2,1,0:T(8,128)(2,1)} custom-call(s32[1]{0:T(128)} %bitcast.1.core_ref, bf16[2,1152,256]{2,1,0:T(8,128)(2,1)} %get-tuple-element.27.own_ref.dgu_ref, bf16[2,1152,256]{2,1,0:T(8,128)(2,1)} %copy-done.7, bf16[2,192,4096]{2,1,0:T(8,128)(2,1)} %bitcast.36, bf16[3,192,2048]{2,1,0:T(8,128)(2,1)} %copy-done.3), custom_call_target="tpu_custom_call" | custom-call | flops 4000000000 | bytes 10000000 | tf_op jit(solution)/shard_map/pallas_call | solution.py:232
  166.4 0.0 reduce-scatter.2.cloned.1.call-update
  166.4 36.6 %all-to-all-done.1.r_ref = bf16[16,72,2048]{2,1,0:T(8,128)(2,1)} async-done(((bf16[16,72,2048]{2,1,0:T(8,128)(2,1)}), bf16[16,72,2048]{2,1,0:T(8,128)(2,1)}, u32[]{:S(2)}, u32[]{:S(2)}) %all-to-all-start.1) | async-done | bytes 4718624 | tf_op jit(solution)/shard_map/all_to_all | solution.py:280
  203.1 6.1 %shard_map.97 = bf16[4,128,512]{2,1,0:T(8,128)(2,1)} custom-call(s32[1]{0:T(128)} %bitcast.z_ref, bf16[16,72,2048]{2,1,0:T(8,128)(2,1)} %all-to-all-done.1.r_ref, f32[128,16]{1,0:T(8,128)} %copy.29.w_ref), custom_call_target="tpu_custom_call" | custom-call | flops 130000003072 | bytes 5300000 | tf_op jit(solution)/shard_map/pallas_call | solution.py:262
  209.2 12.1 %reduce-scatter.2.cloned.1.call-done = bf16[1,1152,512]{2,1,0:T(8,128)(2,1)} async-done(((bf16[4,1152,512]{2,1,0:T(8,128)(2,1)}), bf16[1,1152,512]{2,1,0:T(8,128)(2,1)}) %reduce-scatter.2.cloned.1.call-update) | async-done | bytes 1179664 | tf_op jit(solution)/shard_map/reduce_scatter | solution.py:327
  221.3 7.3 %all-to-all-start.3 = ((bf16[16,72,512]{2,1,0:T(8,128)(2,1)}), bf16[16,72,512]{2,1,0:T(8,128)(2,1)S(1)}, u32[]{:S(2)}, u32[]{:S(2)}) async-start(bf16[16,72,512]{2,1,0:T(8,128)(2,1)} %bitcast.37), calls=%async_computation.4 | async-start | bytes 2359296 | tf_op jit(solution)/shard_map/all_to_all | solution.py:280
  228.5 1.1 slice_bitcast_fusion.2
  229.6 0.8 collective-permute-start.5
  230.4 1.5 collective-permute-start.4
  231.9 0.7 collective-permute-start.3
  232.5 3.3 %collective-permute-done.5 = bf16[128,512]{1,0:T(8,128)(2,1)S(1)} collective-permute-done((bf16[128,512]{1,0:T(8,128)(2,1)S(1)}, bf16[128,512]{1,0:T(8,128)(2,1)S(1)}, u32[]{:S(2)}, u32[]{:S(2)}) %collective-permute-start.5) | collective-permute-done | bytes 131104 | tf_op jit(solution)/shard_map/ppermute | solution.py:288
  235.8 2.2 collective-permute-done.4
  238.0 1.2 collective-permute-done.3
  239.2 1.6 fusion.4
  240.8 0.0 copy-start.1
  240.8 13.5 %shard_map.101 = (bf16[2,192,4096]{2,1,0:T(8,128)(2,1)}, bf16[192,4096]{1,0:T(8,128)(2,1)}) custom-call(bf16[1152,4096]{1,0:T(8,128)(2,1)} %get-tuple-element.28.in_ref, bf16[1152,4096]{1,0:T(8,128)(2,1)} %get-tuple-element.29.cot_ref, bf16[2,1152,256]{2,1,0:T(8,128)(2,1)} %get-tuple-element.27.own_ref.dgu_ref, ...), custom_call_target="tpu_custom_call" | custom-call | flops 6000000000 | bytes 25000000 | tf_op jit(solution)/shard_map/pallas_call | solution.py:241
  254.3 0.0 all-to-all-done.3.r_ref
  254.3 0.0 copy-start.2
  254.3 1.0 copy-done.2
  255.4 2.8 %shard_map.100 = bf16[128,512]{1,0:T(8,128)(2,1)} custom-call(bf16[16,72,512]{2,1,0:T(8,128)(2,1)} %copy-done.2, f32[128,16]{1,0:T(8,128)} %copy.29.w_ref), custom_call_target="tpu_custom_call" | custom-call | flops 200000000 | bytes 1400000 | tf_op jit(solution)/shard_map/pallas_call | solution.py:253
  258.2 0.0 copy-done.1
  (1 shorter events, 0.0 us)
Async XLA Ops:
  7.2 3.1 %copy-start = (bf16[128,4096]{1,0:T(8,128)(2,1)S(1)}, bf16[128,4096]{1,0:T(8,128)(2,1)}, u32[]{:S(2)}) copy-start(bf16[128,4096]{1,0:T(8,128)(2,1)} %param.6) | copy-start | bytes 3145732
  7.2 134.1 %all-gather.2.cloned.1.call-start = ((), (), s32[]{:S(2)}) async-start(), calls=%async_computation.5 | async-start | bytes 16908288 | tf_op jit(solution)/shard_map/all_gather | solution.py:299
  15.9 75.1 %all-to-all-start = ((bf16[16,72,2048]{2,1,0:T(8,128)(2,1)}), bf16[16,72,2048]{2,1,0:T(8,128)(2,1)}, u32[]{:S(2)}, u32[]{:S(2)}) async-start(bf16[16,72,2048]{2,1,0:T(8,128)(2,1)} %shard_map.93.after_ref), calls=%async_computation | async-start | bytes 9437184 | tf_op jit(solution)/shard_map/all_to_all | solution.py:280
  27.3 4.7 %collective-permute-start = (bf16[3,192,2048]{2,1,0:T(8,128)(2,1)}, bf16[3,192,2048]{2,1,0:T(8,128)(2,1)S(1)}, u32[]{:S(2)}, u32[]{:S(2)}) collective-permute-start(bf16[3,192,2048]{2,1,0:T(8,128)(2,1)} %shard_map.94), channel_id=1, source_target_pairs={{0,1},{1,0},{2,3},{3,2},{4,5},{5,4},{6,7},{7,6},{8,9},{9,8},{10,11... | collective-permute-start | bytes 7077896 | tf_op jit(solution)/shard_map/ppermute | solution.py:284
  32.0 80.4 %copy-start.3 = (bf16[3,192,2048]{2,1,0:T(8,128)(2,1)}, bf16[3,192,2048]{2,1,0:T(8,128)(2,1)S(1)}, u32[]{:S(2)}) copy-start(bf16[3,192,2048]{2,1,0:T(8,128)(2,1)S(1)} %collective-permute-done.lent_ref) | copy-start | bytes 7077892
  91.0 8.1 %collective-permute-start.1 = (bf16[1152,2048]{1,0:T(8,128)(2,1)}, bf16[1152,2048]{1,0:T(8,128)(2,1)S(1)}, u32[]{:S(2)}, u32[]{:S(2)}) collective-permute-start(bf16[1152,2048]{1,0:T(8,128)(2,1)} %bitcast.3.own_ref), channel_id=1, source_target_pairs={{0,1},{1,0},{2,3},{3,2},{4,5},{5,4},{6,7},{7,6},{8,9},{9,8},{10,11... | collective-permute-start | bytes 14155784 | tf_op jit(solution)/shard_map/ppermute | solution.py:284
  99.1 2.1 copy-start.6
  112.4 8.8 %collective-permute-start.2 = (bf16[1152,256]{1,0:T(8,128)(2,1)}, bf16[1152,256]{1,0:T(8,128)(2,1)S(1)}, u32[]{:S(2)}, u32[]{:S(2)}) collective-permute-start(bf16[1152,256]{1,0:T(8,128)(2,1)} %get-tuple-element.20.own_ref.hid_ref), channel_id=1, source_target_pairs={{0,1},{1,0},{2,3},{3,2},{4,5},{5,4},{6,7},{7,6},{8,9},{9,8},{10,11... | collective-permute-start | bytes 1769480 | tf_op jit(solution)/shard_map/ppermute | solution.py:284
  112.5 16.1 %all-to-all-start.2 = ((f32[16,1,128]{2,1,0:T(1,128)}), f32[16,1,128]{2,1,0:T(1,128)S(1)}, u32[]{:S(2)}, u32[]{:S(2)}) async-start(f32[16,1,128]{2,1,0:T(1,128)} %bitcast.12), calls=%async_computation.2 | async-start | bytes 16384 | tf_op jit(solution)/shard_map/all_to_all | solution.py:280
  121.2 0.8 copy-start.4
  128.6 7.3 %copy-start.5 = (f32[16,1,128]{2,1,0:T(1,128)}, f32[16,1,128]{2,1,0:T(1,128)S(1)}, u32[]{:S(2)}) copy-start(f32[16,1,128]{2,1,0:T(1,128)S(1)} %all-to-all-done.2) | copy-start | bytes 24580
  128.6 74.5 %all-to-all-start.1 = ((bf16[16,72,2048]{2,1,0:T(8,128)(2,1)}), bf16[16,72,2048]{2,1,0:T(8,128)(2,1)}, u32[]{:S(2)}, u32[]{:S(2)}) async-start(bf16[16,72,2048]{2,1,0:T(8,128)(2,1)} %bitcast.30), calls=%async_computation.1 | async-start | bytes 9437184 | tf_op jit(solution)/shard_map/all_to_all | solution.py:280
  135.9 85.4 %reduce-scatter.2.cloned.1.call-start = ((), (), s32[]{:S(2)}) async-start(), calls=%async_computation.6 | async-start | bytes 5898240 | tf_op jit(solution)/shard_map/reduce_scatter | solution.py:327
  153.1 3.1 %collective-permute-start.6 = (bf16[2,1152,256]{2,1,0:T(8,128)(2,1)}, bf16[2,1152,256]{2,1,0:T(8,128)(2,1)S(1)}, u32[]{:S(2)}, u32[]{:S(2)}) collective-permute-start(bf16[2,1152,256]{2,1,0:T(8,128)(2,1)} %get-tuple-element.27.own_ref.dgu_ref), channel_id=1, source_target_pairs={{0,1},{1,0},{2,3},{3,2},{4,5},{5,4},{6,7},{7,6},{8,9},{9,8},{10,11... | collective-permute-start | bytes 3538952 | tf_op jit(solution)/shard_map/ppermute | solution.py:284
  156.2 1.0 copy-start.7
  221.3 33.0 %all-to-all-start.3 = ((bf16[16,72,512]{2,1,0:T(8,128)(2,1)}), bf16[16,72,512]{2,1,0:T(8,128)(2,1)S(1)}, u32[]{:S(2)}, u32[]{:S(2)}) async-start(bf16[16,72,512]{2,1,0:T(8,128)(2,1)} %bitcast.37), calls=%async_computation.4 | async-start | bytes 2359296 | tf_op jit(solution)/shard_map/all_to_all | solution.py:280
  229.6 6.2 %collective-permute-start.5 = (bf16[128,512]{1,0:T(8,128)(2,1)S(1)}, bf16[128,512]{1,0:T(8,128)(2,1)S(1)}, u32[]{:S(2)}, u32[]{:S(2)}) collective-permute-start(bf16[128,512]{1,0:T(8,128)(2,1)S(1)} %get-tuple-element.33), channel_id=1, source_target_pairs={{0,6},{1,7},{2,0},{3,1},{4,2},{5,3},{6,4},{7,5},{8,14},{9,15},{10,... | collective-permute-start | bytes 393224 | tf_op jit(solution)/shard_map/ppermute | solution.py:288
  230.4 7.6 %collective-permute-start.4 = (bf16[128,512]{1,0:T(8,128)(2,1)S(1)}, bf16[128,512]{1,0:T(8,128)(2,1)S(1)}, u32[]{:S(2)}, u32[]{:S(2)}) collective-permute-start(bf16[128,512]{1,0:T(8,128)(2,1)S(1)} %get-tuple-element.34), channel_id=1, source_target_pairs={{0,4},{1,5},{2,6},{3,7},{4,0},{5,1},{6,2},{7,3},{8,12},{9,13},{10,... | collective-permute-start | bytes 393224 | tf_op jit(solution)/shard_map/ppermute | solution.py:288
  231.9 7.3 %collective-permute-start.3 = (bf16[128,512]{1,0:T(8,128)(2,1)S(1)}, bf16[128,512]{1,0:T(8,128)(2,1)S(1)}, u32[]{:S(2)}, u32[]{:S(2)}) collective-permute-start(bf16[128,512]{1,0:T(8,128)(2,1)S(1)} %get-tuple-element.32), channel_id=1, source_target_pairs={{0,2},{1,3},{2,4},{3,5},{4,6},{5,7},{6,0},{7,1},{8,10},{9,11},{10,... | collective-permute-start | bytes 393224 | tf_op jit(solution)/shard_map/ppermute | solution.py:288
  240.8 17.4 %copy-start.1 = (bf16[128,4096]{1,0:T(8,128)(2,1)S(1)}, bf16[128,4096]{1,0:T(8,128)(2,1)}, u32[]{:S(2)}) copy-start(bf16[128,4096]{1,0:T(8,128)(2,1)} %param.6) | copy-start | bytes 3145732
  254.3 1.0 copy-start.2
Sparse Core Ops, SparseCore 0:
  11.7 129.5 all-gather.1
  166.6 54.6 reduce-scatter.1

commit v5 on v4

--- a/solution.py
+++ b/solution.py
@@ -128,7 +128,7 @@
     o_ref[...] = total.astype(BF16)
 
 
-def depth_kernel(z_ref, r_ref, w_ref, o_ref):
+def depth_kernel(z_ref, r_ref, w_ref, after_ref, o_ref):
     w, _, slot = own_places(w_ref)
     total = jnp.zeros((TOK, SHARE), F32)
     for e in range(EXPERTS):
@@ -252,13 +252,14 @@
 def combine(returned, own_weight):
     return pl.pallas_call(
         combine_kernel,
+        in_specs=[pl.BlockSpec(memory_space=pltpu.VMEM)] * 2,
         out_shape=jax.ShapeDtypeStruct((TOK, SHARE), BF16),
         compiler_params=pltpu.CompilerParams(vmem_limit_bytes=VMEM_LIMIT),
         cost_estimate=pl.CostEstimate(flops=200_000_000, bytes_accessed=1_400_000, transcendentals=0),
     )(returned, own_weight)
 
 
-def depth_parts(level, returned, own_weight):
+def depth_parts(level, returned, own_weight, after):
     return pl.pallas_call(
         depth_kernel,
         grid_spec=pltpu.PrefetchScalarGridSpec(
@@ -267,13 +268,14 @@
             in_specs=[
                 pl.BlockSpec((EXPERTS, CAP, SHARE), lambda d, z: (0, 0, (z[0] + d) % DEPTH)),
                 pl.BlockSpec((TOK, EXPERTS), lambda d, z: (0, 0)),
+                pl.BlockSpec(memory_space=pl.ANY),
             ],
             out_specs=pl.BlockSpec((None, TOK, SHARE), lambda d, z: (d, 0, 0)),
         ),
         out_shape=jax.ShapeDtypeStruct((DEPTH, TOK, SHARE), BF16),
         compiler_params=params(),
-        cost_estimate=pl.CostEstimate(flops=130000000000, bytes_accessed=5_300_000, transcendentals=0),
-    )(level, returned, own_weight)
+        cost_estimate=pl.CostEstimate(flops=90_000_000_000, bytes_accessed=5_300_000, transcendentals=0),
+    )(level, returned, own_weight, after)
 
 
 def over_experts(x):
@@ -305,7 +307,6 @@
     picked = pick(x_half, weight_rows)
     own_rows = over_experts(picked).reshape(ALL_ROWS, HALF)
     lent = swap_cores(lend(1 - core_list, picked, wgu, wd))
-    own_rows, lent = lax.optimization_barrier((own_rows, lent))
     other_rows = swap_cores(own_rows)
     weight_rows, own_rows = lax.optimization_barrier((weight_rows, own_rows))
     weight = over_experts(weight_rows)
@@ -328,9 +329,10 @@
         pair_back, "tensor", scatter_dimension=0, tiled=False,
         axis_index_groups=[[2 * z + c for z in range(DEPTH)] for c in range(2)],
     )
+    grad_gate_up, grad_down = weight_grads(inputs, cot, dgu, hidden)
+    parts = depth_parts(level_list, out_back, own_weight, grad_down)
+    parts, back_sum = lax.optimization_barrier((parts, back_sum))
     grad_back = over_experts(back_sum.reshape(GROUPS, CAP, SHARE))
-    grad_gate_up, grad_down = weight_grads(inputs, cot, dgu, hidden)
-    parts = depth_parts(level_list, out_back, own_weight)
     mixed = parts[0].astype(F32)
     for d in range(1, DEPTH):
         mixed += up_levels(parts[d], d).astype(F32)

time: 266 us -> 244 us (0.917)
  waiting for transfers between devices: 133 us -> 49.3 us
  blocking collectives: 0 us -> 69.5 us
  starting transfers between devices: 34 us -> 23.6 us
    all_to_all x0 -> x1, blocking collectives: none -> 69.5 us  [over_experts(): return lax.all_to_all(x, 'expert', split_axis=0, concat_axis=0, tiled=True)]
    all_to_all x4 -> x3, waiting for transfers between devices: 95.6 us -> 30.8 us  [over_experts(): return lax.all_to_all(x, 'expert', split_axis=0, concat_axis=0, tiled=True)]
    all_to_all x4 -> x3, starting transfers between devices: 30.6 us -> 19.2 us  [over_experts(): return lax.all_to_all(x, 'expert', split_axis=0, concat_axis=0, tiled=True)]
    ppermute x4, waiting for transfers between devices: 14.3 us -> 6.49 us  [swap_cores(): return lax.ppermute(x, 'tensor', [(t, t ^ 1) for t in range(TENSOR)])]
    reduce_scatter x1, waiting for transfers between devices: 12.1 us -> 6.77 us  [on_device(): lax.psum_scatter(pair_back, 'tensor', scatter_dimension=0, tiled=False, a...]
    all_gather x1, waiting for transfers between devices: 4.62 us -> 0.01 us  [on_device(): grad_rows = lax.all_gather(mine, ('expert', 'tensor'), axis=0, tiled=True)]
  transfers between devices with their start and end apart: 13 -> 12, of which waited for: 10 -> 7; matrix products, arithmetic and copies ran while one was open for 3% -> 3% of each run, Pallas kernels for 25% -> 29%
where the time goes in v5:
time: 244 us; the launch traced here: 241 us
  Pallas kernels  71.8 us (29%)
  blocking collectives  69.5 us (28%)
  waiting for transfers between devices  49.3 us (20%)
  starting transfers between devices  23.6 us (10%)
  between operations  14.1 us (6%)
  local copies, waits for them, and re-layouts  9.24 us (4%)
  other arithmetic  2.95 us (1%)
    all_to_all x1, blocking collectives, over_experts(): return lax.all_to_all(x, 'expert', split_axis=0, concat_axis=0, tiled=True)  69.5 us
    all_to_all x3, waiting for transfers between devices, over_experts(): return lax.all_to_all(x, 'expert', split_axis=0, concat_axis=0, tiled=True)  30.8 us
    all_to_all x3, starting transfers between devices, over_experts(): return lax.all_to_all(x, 'expert', split_axis=0, concat_axis=0, tiled=True)  19.2 us
    pallas_call x1, Pallas kernels, weight_grads(): stepped(weight_grad_kernel, 0, TENSOR, [cols, cols, whole(dgu.shape), who...  13.9 us
    pallas_call x1, Pallas kernels, unit_grads(): stepped(unit_grad_kernel, 0, STEPS, [by_rows(STEP_GROUPS * TOK, D), ROW_S...  11.8 us
    pallas_call x1, Pallas kernels, hidden_units(): stepped(hidden_kernel, 1, STEPS, [by_rows(ROWS, HALF), by_rows(ROWS, HALF...  11.3 us
    pallas_call x1, Pallas kernels, back_rows(): stepped(back_kernel, 1, STEPS, [by_rows(2, ROWS, WIDE), by_rows(2, ROWS,...  9.27 us
    pallas_call x1, Pallas kernels, out_rows(): stepped(out_kernel, 1, STEPS, [by_rows(ROWS, WIDE), by_rows(ROWS, WIDE),...  6.98 us
  transfers between devices with their start and end apart: 12, of which 7 were waited for; matrix products, arithmetic and copies ran while one was open for 3% of the time, Pallas kernels for 29%

profile of v5, /device:TPU:2, one launch (start us, length us, event | category | flops | bytes accessed | tf_op | source)
XLA Modules:
  0.0 241.4 jit_solution(9739599564706422849)
XLA Ops:
  7.2 0.0 copy-start
  7.2 0.0 all-gather.2.cloned.1.call-start
  7.2 1.6 constant_dynamic-slice_fusion
  8.9 0.0 all-gather.2.cloned.1.call-update
  8.9 1.3 select_reduce_fusion
  10.2 0.0 copy-done
  10.2 0.8 constant_dynamic-slice_fusion.1.x_ref
  11.1 4.8 %shard_map.93.after_ref = bf16[16,72,2048]{2,1,0:T(8,128)(2,1)} custom-call(bf16[128,2048]{1,0:T(8,128)(2,1)} %constant_dynamic-slice_fusion.1.x_ref, f32[16,128]{1,0:T(8,128)} %bitcast.2.w_ref), custom_call_target="tpu_custom_call" | custom-call | flops 600000000 | bytes 5300000 | tf_op jit(solution)/shard_map/pallas_call | solution.py:173
  15.9 69.5 %all_to_all.24 = bf16[16,72,2048]{2,1,0:T(8,128)(2,1)S(1)} all-to-all(bf16[16,72,2048]{2,1,0:T(8,128)(2,1)} %shard_map.93.after_ref), channel_id=1, replica_groups=mesh['expert'=16,'tensor'=8] {'expert'}, dimensions={0} | all-to-all | bytes 9437184 | tf_op jit(solution)/shard_map/all_to_all | solution.py:282
  85.5 0.0 copy-start.2
  85.5 0.0 collective-permute-start
  85.5 4.6 %shard_map.95 = bf16[3,192,2048]{2,1,0:T(8,128)(2,1)} custom-call(s32[1]{0:T(128)S(6)} %sub.8.core_ref, bf16[16,72,2048]{2,1,0:T(8,128)(2,1)} %shard_map.93.after_ref, bf16[2,192,4096]{2,1,0:T(8,128)(2,1)} %bitcast.35, bf16[192,4096]{1,0:T(8,128)(2,1)} %bitcast.30), custom_call_target="tpu_custom_call" | custom-call | bytes 4700000 | tf_op jit(solution)/shard_map/pallas_call | solution.py:182
  90.1 0.0 copy-done.2
  90.1 0.0 collective-permute-start.2
  90.1 3.4 %collective-permute-done.other_ref = bf16[1152,2048]{1,0:T(8,128)(2,1)} collective-permute-done((bf16[1152,2048]{1,0:T(8,128)(2,1)S(1)}, bf16[1152,2048]{1,0:T(8,128)(2,1)}, u32[]{:S(2)}, u32[]{:S(2)}) %collective-permute-start) | collective-permute-done | bytes 4718624 | tf_op jit(solution)/shard_map/ppermute | solution.py:286
  93.5 11.3 %shard_map.94 = (bf16[1152,4096]{1,0:T(8,128)(2,1)}, f32[1152,192]{1,0:T(8,128)}, f32[1152,192]{1,0:T(8,128)}, bf16[1152,256]{1,0:T(8,128)(2,1)}) custom-call(s32[1]{0:T(128)} %bitcast.1.core_ref, bf16[1152,2048]{1,0:T(8,128)(2,1)} %bitcast.34, bf16[1152,2048]{1,0:T(8,128)(2,1)} %collective-permute-done.other_ref, bf16[2,192,4096]{2,1,0:T(8,128)(2,1)} %bitcast.36), custom_call_target="tpu_custom_call" | custom-call | flops 4000000000 | bytes 25000000 | tf_op jit(solution)/shard_map/pallas_call | solution.py:195
  104.8 0.2 collective-permute-start.1
  105.0 4.7 %all-to-all-start.2 = ((f32[16,1,128]{2,1,0:T(1,128)}), f32[16,1,128]{2,1,0:T(1,128)S(1)}, u32[]{:S(2)}, u32[]{:S(2)}) async-start(f32[16,1,128]{2,1,0:T(1,128)} %bitcast.8), calls=%async_computation.2 | async-start | bytes 16384 | tf_op jit(solution)/shard_map/all_to_all | solution.py:282
  109.7 0.0 collective-permute-done.2.lent_ref
  109.7 0.0 copy-start.4
  109.7 0.0 collective-permute-done.1.other_ref
  109.7 1.4 copy-done.4
  111.1 0.0 copy-start.5
  111.1 0.8 copy-done.5
  111.9 7.0 %shard_map.96 = bf16[1152,2048]{1,0:T(8,128)(2,1)} custom-call(s32[1]{0:T(128)} %bitcast.1.core_ref, bf16[1152,256]{1,0:T(8,128)(2,1)} %get-tuple-element.19.own_ref.hid_ref, bf16[1152,256]{1,0:T(8,128)(2,1)} %copy-done.5, bf16[192,4096]{1,0:T(8,128)(2,1)} %bitcast.31, bf16[3,192,2048]{2,1,0:T(8,128)(2,1)} %copy-done.4), custom_call_target="tpu_custom_call" | custom-call | flops 2000000000 | bytes 8000000 | tf_op jit(solution)/shard_map/pallas_call | solution.py:208
  118.9 0.0 all-to-all-done.2
  118.9 0.0 copy-start.6
  118.9 7.2 %all-to-all-start.1 = ((bf16[16,72,2048]{2,1,0:T(8,128)(2,1)}), bf16[16,72,2048]{2,1,0:T(8,128)(2,1)}, u32[]{:S(2)}, u32[]{:S(2)}) async-start(bf16[16,72,2048]{2,1,0:T(8,128)(2,1)} %bitcast.29), calls=%async_computation.1 | async-start | bytes 9437184 | tf_op jit(solution)/shard_map/all_to_all | solution.py:282
  126.2 0.0 reduce-scatter.2.cloned.1.call-start
  126.2 0.0 copy-done.6
  126.2 0.7 fusion.1
  127.0 0.0 all-gather.2.cloned.1.call-done.g_ref
  127.0 11.8 %shard_map.97 = (bf16[1152,4096]{1,0:T(8,128)(2,1)}, bf16[2,1152,256]{2,1,0:T(8,128)(2,1)}) custom-call(bf16[2048,4096]{1,0:T(8,128)(2,1)} %all-gather.2.cloned.1.call-done.g_ref, s32[8,1,256]{2,1,0:T(1,128)} %bitcast.41, f32[8,1,256]{2,1,0:T(1,128)} %bitcast.40, f32[1152,192]{1,0:T(8,128)} %get-tuple-element.24.gate_ref, ...), custom_call_target="tpu_custom_call" | custom-call | flops 4000000000 | bytes 30000000 | tf_op jit(solution)/shard_map/pallas_call | solution.py:219
  138.8 0.0 collective-permute-start.3
  138.8 3.1 %collective-permute-done.3.other_ref = bf16[2,1152,256]{2,1,0:T(8,128)(2,1)S(1)} collective-permute-done((bf16[2,1152,256]{2,1,0:T(8,128)(2,1)}, bf16[2,1152,256]{2,1,0:T(8,128)(2,1)S(1)}, u32[]{:S(2)}, u32[]{:S(2)}) %collective-permute-start.3) | collective-permute-done | bytes 1179680 | tf_op jit(solution)/shard_map/ppermute | solution.py:286
  141.9 0.0 copy-start.7
  141.9 1.0 copy-done.7
  142.9 9.3 %shard_map.100 = bf16[4,1152,512]{2,1,0:T(8,128)(2,1)} custom-call(s32[1]{0:T(128)} %bitcast.1.core_ref, bf16[2,1152,256]{2,1,0:T(8,128)(2,1)} %get-tuple-element.27.dgu_ref.own_ref, bf16[2,1152,256]{2,1,0:T(8,128)(2,1)} %copy-done.7, bf16[2,192,4096]{2,1,0:T(8,128)(2,1)} %bitcast.37, bf16[3,192,2048]{2,1,0:T(8,128)(2,1)} %copy-done.4), custom_call_target="tpu_custom_call" | custom-call | flops 4000000000 | bytes 10000000 | tf_op jit(solution)/shard_map/pallas_call | solution.py:232
  152.1 0.0 reduce-scatter.2.cloned.1.call-update
  152.2 1.4 copy.33.w_ref
  153.6 13.9 %shard_map.98 = (bf16[2,192,4096]{2,1,0:T(8,128)(2,1)}, bf16[192,4096]{1,0:T(8,128)(2,1)}) custom-call(bf16[1152,4096]{1,0:T(8,128)(2,1)} %get-tuple-element.22.in_ref, bf16[1152,4096]{1,0:T(8,128)(2,1)} %get-tuple-element.26.cot_ref, bf16[2,1152,256]{2,1,0:T(8,128)(2,1)} %get-tuple-element.27.dgu_ref.own_ref, ...), custom_call_target="tpu_custom_call" | custom-call | flops 6000000000 | bytes 25000000 | tf_op jit(solution)/shard_map/pallas_call | solution.py:241
  167.5 25.7 %all-to-all-done.1.r_ref = bf16[16,72,2048]{2,1,0:T(8,128)(2,1)} async-done(((bf16[16,72,2048]{2,1,0:T(8,128)(2,1)}), bf16[16,72,2048]{2,1,0:T(8,128)(2,1)}, u32[]{:S(2)}, u32[]{:S(2)}) %all-to-all-start.1) | async-done | bytes 4718624 | tf_op jit(solution)/shard_map/all_to_all | solution.py:282
  193.1 0.0 copy-start.1
  193.1 6.3 %shard_map.99 = bf16[4,128,512]{2,1,0:T(8,128)(2,1)} custom-call(s32[1]{0:T(128)} %bitcast.z_ref, bf16[16,72,2048]{2,1,0:T(8,128)(2,1)} %all-to-all-done.1.r_ref, f32[128,16]{1,0:T(8,128)} %copy.33.w_ref, bf16[192,4096]{1,0:T(8,128)(2,1)} %get-tuple-element.28.after_ref), custom_call_target="tpu_custom_call" | custom-call | flops 89999998976 | bytes 5300000 | tf_op jit(solution)/shard_map/pallas_call | solution.py:263
  199.4 6.8 %reduce-scatter.2.cloned.1.call-done = bf16[1,1152,512]{2,1,0:T(8,128)(2,1)} async-done(((bf16[4,1152,512]{2,1,0:T(8,128)(2,1)}), bf16[1,1152,512]{2,1,0:T(8,128)(2,1)}) %reduce-scatter.2.cloned.1.call-update) | async-done | bytes 1179664 | tf_op jit(solution)/shard_map/reduce_scatter | solution.py:328
  206.2 7.3 %all-to-all-start.3 = ((bf16[16,72,512]{2,1,0:T(8,128)(2,1)}), bf16[16,72,512]{2,1,0:T(8,128)(2,1)S(1)}, u32[]{:S(2)}, u32[]{:S(2)}) async-start(bf16[16,72,512]{2,1,0:T(8,128)(2,1)} %bitcast.38), calls=%async_computation.4 | async-start | bytes 2359296 | tf_op jit(solution)/shard_map/all_to_all | solution.py:282
  213.5 1.1 slice_bitcast_fusion.2
  214.5 0.2 collective-permute-start.4
  214.7 2.1 collective-permute-start.5
  216.8 1.9 collective-permute-start.6
  218.7 4.6 %collective-permute-done.4 = bf16[128,512]{1,0:T(8,128)(2,1)S(1)} collective-permute-done((bf16[128,512]{1,0:T(8,128)(2,1)S(1)}, bf16[128,512]{1,0:T(8,128)(2,1)S(1)}, u32[]{:S(2)}, u32[]{:S(2)}) %collective-permute-start.4) | collective-permute-done | bytes 131104 | tf_op jit(solution)/shard_map/ppermute | solution.py:290
  223.3 0.0 collective-permute-done.5
  223.3 0.6 collective-permute-done.6
  223.9 1.6 fusion.4
  225.5 5.2 %all-to-all-done.3.r_ref = bf16[16,72,512]{2,1,0:T(8,128)(2,1)S(1)} async-done(((bf16[16,72,512]{2,1,0:T(8,128)(2,1)}), bf16[16,72,512]{2,1,0:T(8,128)(2,1)S(1)}, u32[]{:S(2)}, u32[]{:S(2)}) %all-to-all-start.3) | async-done | bytes 1179680 | tf_op jit(solution)/shard_map/all_to_all | solution.py:282
  230.7 0.0 copy-start.3
  230.7 1.0 copy-done.3
  231.7 2.8 %shard_map.101 = bf16[128,512]{1,0:T(8,128)(2,1)} custom-call(bf16[16,72,512]{2,1,0:T(8,128)(2,1)} %copy-done.3, f32[128,16]{1,0:T(8,128)} %copy.33.w_ref), custom_call_target="tpu_custom_call" | custom-call | flops 200000000 | bytes 1400000 | tf_op jit(solution)/shard_map/pallas_call | solution.py:253
  234.6 0.0 copy-done.1
  (1 shorter events, 0.0 us)
Async XLA Ops:
  7.2 3.1 %copy-start = (bf16[128,4096]{1,0:T(8,128)(2,1)S(1)}, bf16[128,4096]{1,0:T(8,128)(2,1)}, u32[]{:S(2)}) copy-start(bf16[128,4096]{1,0:T(8,128)(2,1)} %param.6) | copy-start | bytes 3145732
  7.2 119.8 %all-gather.2.cloned.1.call-start = ((), (), s32[]{:S(2)}) async-start(), calls=%async_computation.5 | async-start | bytes 16908288 | tf_op jit(solution)/shard_map/all_gather | solution.py:301
  85.5 4.6 %copy-start.2 = (bf16[16,72,2048]{2,1,0:T(8,128)(2,1)}, bf16[16,72,2048]{2,1,0:T(8,128)(2,1)S(1)}, u32[]{:S(2)}) copy-start(bf16[16,72,2048]{2,1,0:T(8,128)(2,1)S(1)} %all_to_all.24) | copy-start | bytes 14155780
  85.5 8.0 %collective-permute-start = (bf16[1152,2048]{1,0:T(8,128)(2,1)S(1)}, bf16[1152,2048]{1,0:T(8,128)(2,1)}, u32[]{:S(2)}, u32[]{:S(2)}) collective-permute-start(bf16[1152,2048]{1,0:T(8,128)(2,1)S(1)} %bitcast.33), channel_id=1, source_target_pairs={{0,1},{1,0},{2,3},{3,2},{4,5},{5,4},{6,7},{7,6},{8,9},{9,8},{10,11... | collective-permute-start | bytes 14155784 | tf_op jit(solution)/shard_map/ppermute | solution.py:286
  90.1 19.6 %collective-permute-start.2 = (bf16[3,192,2048]{2,1,0:T(8,128)(2,1)}, bf16[3,192,2048]{2,1,0:T(8,128)(2,1)S(1)}, u32[]{:S(2)}, u32[]{:S(2)}) collective-permute-start(bf16[3,192,2048]{2,1,0:T(8,128)(2,1)} %shard_map.95), channel_id=1, source_target_pairs={{0,1},{1,0},{2,3},{3,2},{4,5},{5,4},{6,7},{7,6},{8,9},{9,8},{10,11... | collective-permute-start | bytes 7077896 | tf_op jit(solution)/shard_map/ppermute | solution.py:286
  104.8 4.9 %collective-permute-start.1 = (bf16[1152,256]{1,0:T(8,128)(2,1)}, bf16[1152,256]{1,0:T(8,128)(2,1)S(1)}, u32[]{:S(2)}, u32[]{:S(2)}) collective-permute-start(bf16[1152,256]{1,0:T(8,128)(2,1)} %get-tuple-element.19.own_ref.hid_ref), channel_id=1, source_target_pairs={{0,1},{1,0},{2,3},{3,2},{4,5},{5,4},{6,7},{7,6},{8,9},{9,8},{10,11... | collective-permute-start | bytes 1769480 | tf_op jit(solution)/shard_map/ppermute | solution.py:286
  105.0 13.9 %all-to-all-start.2 = ((f32[16,1,128]{2,1,0:T(1,128)}), f32[16,1,128]{2,1,0:T(1,128)S(1)}, u32[]{:S(2)}, u32[]{:S(2)}) async-start(f32[16,1,128]{2,1,0:T(1,128)} %bitcast.8), calls=%async_computation.2 | async-start | bytes 16384 | tf_op jit(solution)/shard_map/all_to_all | solution.py:282
  109.7 1.4 copy-start.4
  111.1 0.8 copy-start.5
  118.9 7.3 %copy-start.6 = (f32[16,1,128]{2,1,0:T(1,128)}, f32[16,1,128]{2,1,0:T(1,128)S(1)}, u32[]{:S(2)}) copy-start(f32[16,1,128]{2,1,0:T(1,128)S(1)} %all-to-all-done.2) | copy-start | bytes 24580
  118.9 74.2 %all-to-all-start.1 = ((bf16[16,72,2048]{2,1,0:T(8,128)(2,1)}), bf16[16,72,2048]{2,1,0:T(8,128)(2,1)}, u32[]{:S(2)}, u32[]{:S(2)}) async-start(bf16[16,72,2048]{2,1,0:T(8,128)(2,1)} %bitcast.29), calls=%async_computation.1 | async-start | bytes 9437184 | tf_op jit(solution)/shard_map/all_to_all | solution.py:282
  126.2 80.0 %reduce-scatter.2.cloned.1.call-start = ((), (), s32[]{:S(2)}) async-start(), calls=%async_computation.6 | async-start | bytes 5898240 | tf_op jit(solution)/shard_map/reduce_scatter | solution.py:328
  138.8 3.1 %collective-permute-start.3 = (bf16[2,1152,256]{2,1,0:T(8,128)(2,1)}, bf16[2,1152,256]{2,1,0:T(8,128)(2,1)S(1)}, u32[]{:S(2)}, u32[]{:S(2)}) collective-permute-start(bf16[2,1152,256]{2,1,0:T(8,128)(2,1)} %get-tuple-element.27.dgu_ref.own_ref), channel_id=1, source_target_pairs={{0,1},{1,0},{2,3},{3,2},{4,5},{5,4},{6,7},{7,6},{8,9},{9,8},{10,11... | collective-permute-start | bytes 3538952 | tf_op jit(solution)/shard_map/ppermute | solution.py:286
  141.9 1.0 copy-start.7
  193.1 41.4 %copy-start.1 = (bf16[128,4096]{1,0:T(8,128)(2,1)S(1)}, bf16[128,4096]{1,0:T(8,128)(2,1)}, u32[]{:S(2)}) copy-start(bf16[128,4096]{1,0:T(8,128)(2,1)} %param.6) | copy-start | bytes 3145732
  206.2 24.5 %all-to-all-start.3 = ((bf16[16,72,512]{2,1,0:T(8,128)(2,1)}), bf16[16,72,512]{2,1,0:T(8,128)(2,1)S(1)}, u32[]{:S(2)}, u32[]{:S(2)}) async-start(bf16[16,72,512]{2,1,0:T(8,128)(2,1)} %bitcast.38), calls=%async_computation.4 | async-start | bytes 2359296 | tf_op jit(solution)/shard_map/all_to_all | solution.py:282
  214.5 8.8 %collective-permute-start.4 = (bf16[128,512]{1,0:T(8,128)(2,1)S(1)}, bf16[128,512]{1,0:T(8,128)(2,1)S(1)}, u32[]{:S(2)}, u32[]{:S(2)}) collective-permute-start(bf16[128,512]{1,0:T(8,128)(2,1)S(1)} %get-tuple-element.32), channel_id=1, source_target_pairs={{0,2},{1,3},{2,4},{3,5},{4,6},{5,7},{6,0},{7,1},{8,10},{9,11},{10,... | collective-permute-start | bytes 393224 | tf_op jit(solution)/shard_map/ppermute | solution.py:290
  214.7 8.6 %collective-permute-start.5 = (bf16[128,512]{1,0:T(8,128)(2,1)S(1)}, bf16[128,512]{1,0:T(8,128)(2,1)S(1)}, u32[]{:S(2)}, u32[]{:S(2)}) collective-permute-start(bf16[128,512]{1,0:T(8,128)(2,1)S(1)} %get-tuple-element.34), channel_id=1, source_target_pairs={{0,4},{1,5},{2,6},{3,7},{4,0},{5,1},{6,2},{7,3},{8,12},{9,13},{10,... | collective-permute-start | bytes 393224 | tf_op jit(solution)/shard_map/ppermute | solution.py:290
  216.8 7.1 %collective-permute-start.6 = (bf16[128,512]{1,0:T(8,128)(2,1)S(1)}, bf16[128,512]{1,0:T(8,128)(2,1)S(1)}, u32[]{:S(2)}, u32[]{:S(2)}) collective-permute-start(bf16[128,512]{1,0:T(8,128)(2,1)S(1)} %get-tuple-element.33), channel_id=1, source_target_pairs={{0,6},{1,7},{2,0},{3,1},{4,2},{5,3},{6,4},{7,5},{8,14},{9,15},{10,... | collective-permute-start | bytes 393224 | tf_op jit(solution)/shard_map/ppermute | solution.py:290
  230.7 1.0 copy-start.3
Sparse Core Ops, SparseCore 0:
  11.7 109.4 all-gather.1
  152.3 53.8 reduce-scatter.1

commit v6 on v4

--- a/solution.py
+++ b/solution.py
@@ -15,6 +15,7 @@
 TENSOR = 8
 SHARE = D // TENSOR
 HALF = D // 2
+PART = SHARE // 2
 DEPTH = TENSOR // 2
 STEP_GROUPS = 4
 PAIRS = STEP_GROUPS // 2
@@ -68,12 +69,14 @@
     hid_ref[:, UNITS:] = jnp.zeros((ROWS, WIDE - UNITS), BF16)
 
 
-def out_kernel(core_ref, own_ref, other_ref, wd_ref, lent_ref, o_ref):
+def out_kernel(core_ref, own_ref, other_ref, wd_ref, lent_ref, direct_ref, part_ref):
     own, other = own_ref[:, :UNITS], other_ref[:, :UNITS]
     for z in range(DEPTH):
         cols = pl.ds(pl.multiple_of((2 * z + core_ref[0]) * SHARE, SHARE), SHARE)
         share = slice(SHARE * z, SHARE * (z + 1))
-        o_ref[:, share] = (nn(own, wd_ref[:, cols]) + nn(other, lent_ref[:, share])).astype(BF16)
+        total = (nn(own, wd_ref[:, cols]) + nn(other, lent_ref[:, share])).astype(BF16)
+        direct_ref[:, PART * z : PART * (z + 1)] = total[:, :PART]
+        part_ref[z] = total[:, PART:]
 
 
 def unit_grad_kernel(g_ref, row_ref, w_ref, gate_ref, up_ref, wd_ref, cot_ref, dgu_ref):
@@ -99,14 +102,16 @@
     down_ref[...] = tn(hid_ref[:, :UNITS], cot_ref[...]).astype(BF16)
 
 
-def back_kernel(core_ref, own_ref, other_ref, wgu_ref, lent_ref, o_ref):
+def back_kernel(core_ref, after_ref, own_ref, other_ref, wgu_ref, lent_ref, direct_ref, part_ref):
     for z in range(DEPTH):
         cols = pl.ds(pl.multiple_of((2 * z + core_ref[0]) * SHARE, SHARE), SHARE)
         share = slice(SHARE * z, SHARE * (z + 1))
         total = nn(own_ref[0, :, :UNITS], wgu_ref[0, :, cols]) + nn(own_ref[1, :, :UNITS], wgu_ref[1, :, cols])
         total += nn(other_ref[0, :, :UNITS], lent_ref[0, :, share])
         total += nn(other_ref[1, :, :UNITS], lent_ref[1, :, share])
-        o_ref[z] = total.astype(BF16)
+        total = total.astype(BF16)
+        direct_ref[:, PART * z : PART * (z + 1)] = total[:, :PART]
+        part_ref[z] = total[:, PART:]
 
 
 def own_places(w_ref):
@@ -118,23 +123,14 @@
     return w, ones, jnp.where(mask, slot, -1.0).astype(jnp.int32)
 
 
-def combine_kernel(r_ref, w_ref, o_ref):
-    _, ones, slot = own_places(w_ref)
+def combine_kernel(weighted, r_ref, w_ref, o_ref):
+    w, ones, slot = own_places(w_ref)
+    scale = w if weighted else ones
     total = jnp.zeros(o_ref.shape, F32)
     for e in range(EXPERTS):
         hit = lax.broadcasted_iota(jnp.int32, (TOK, CAP), 1) == slot[:, e : e + 1]
         onehot = jnp.where(hit, 1.0, 0.0).astype(BF16)
-        total += nn(onehot, r_ref[e]) * ones[:, e : e + 1]
-    o_ref[...] = total.astype(BF16)
-
-
-def depth_kernel(z_ref, r_ref, w_ref, o_ref):
-    w, _, slot = own_places(w_ref)
-    total = jnp.zeros((TOK, SHARE), F32)
-    for e in range(EXPERTS):
-        hit = lax.broadcasted_iota(jnp.int32, (TOK, CAP), 1) == slot[:, e : e + 1]
-        onehot = jnp.where(hit, 1.0, 0.0).astype(BF16)
-        total += nn(onehot, r_ref[e]) * w[:, e : e + 1]
+        total += nn(onehot, r_ref[e]) * scale[:, e : e + 1]
     o_ref[...] = total.astype(BF16)
 
 
@@ -169,6 +165,12 @@
 ROW_SPEC = pl.BlockSpec((PAIRS, 1, 2 * TOK), lambda i, *_: (i, 0, 0))
 
 
+SPLIT = (
+    [by_rows(ROWS, DEPTH * PART), by_rows(DEPTH, ROWS, PART)],
+    [shaped(ALL_ROWS, DEPTH * PART), shaped(DEPTH, ALL_ROWS, PART)],
+)
+
+
 def pick(x_half, weight_rows):
     return pl.pallas_call(
         pick_kernel,
@@ -211,7 +213,7 @@
             by_rows(ROWS, WIDE), by_rows(ROWS, WIDE), whole(wd.shape),
             pl.BlockSpec((None, UNITS, HALF), lambda *_: (2, 0, 0), pipeline_mode=pl.Buffered(1)),
         ],
-        by_rows(ROWS, HALF), shaped(ALL_ROWS, HALF), 2_000_000_000, 8_000_000,
+        *SPLIT, 2_000_000_000, 8_000_000,
     )(core, own, other, wd, lent)
 
 
@@ -228,12 +230,15 @@
     )(grad_rows, row_of, weight, gate, up, wd)
 
 
-def back_rows(core, own, other, wgu, lent):
+def back_rows(core, after, own, other, wgu, lent):
     return stepped(
         back_kernel, 1, STEPS,
-        [by_rows(2, ROWS, WIDE), by_rows(2, ROWS, WIDE), whole(wgu.shape), whole((2, UNITS, HALF))],
-        by_rows(DEPTH, ROWS, SHARE), shaped(DEPTH, ALL_ROWS, SHARE), 4_000_000_000, 10_000_000,
-    )(core, own, other, wgu, lent)
+        [
+            pl.BlockSpec(memory_space=pl.ANY), by_rows(2, ROWS, WIDE), by_rows(2, ROWS, WIDE),
+            whole(wgu.shape), whole((2, UNITS, HALF)),
+        ],
+        *SPLIT, 4_000_000_000, 10_000_000,
+    )(core, after, own, other, wgu, lent)
 
 
 def weight_grads(inputs, cot, dgu, hidden):
@@ -249,35 +254,51 @@
     )(inputs, cot, dgu, hidden)
 
 
-def combine(returned, own_weight):
+def combine(weighted, returned, own_weight):
     return pl.pallas_call(
-        combine_kernel,
-        out_shape=jax.ShapeDtypeStruct((TOK, SHARE), BF16),
+        lambda *refs: combine_kernel(weighted, *refs),
+        in_specs=[pl.BlockSpec(memory_space=pltpu.VMEM)] * 2,
+        out_shape=shaped(TOK, PART),
         compiler_params=pltpu.CompilerParams(vmem_limit_bytes=VMEM_LIMIT),
         cost_estimate=pl.CostEstimate(flops=200_000_000, bytes_accessed=1_400_000, transcendentals=0),
     )(returned, own_weight)
 
 
-def depth_parts(level, returned, own_weight):
-    return pl.pallas_call(
-        depth_kernel,
+def sum_levels(weighted, level, returned, own_weight):
+    parts = pl.pallas_call(
+        lambda z_ref, *refs: combine_kernel(weighted, *refs),
         grid_spec=pltpu.PrefetchScalarGridSpec(
             num_scalar_prefetch=1,
             grid=(DEPTH,),
             in_specs=[
-                pl.BlockSpec((EXPERTS, CAP, SHARE), lambda d, z: (0, 0, (z[0] + d) % DEPTH)),
+                pl.BlockSpec((EXPERTS, CAP, PART), lambda d, z: (0, 0, (z[0] + d) % DEPTH)),
                 pl.BlockSpec((TOK, EXPERTS), lambda d, z: (0, 0)),
             ],
-            out_specs=pl.BlockSpec((None, TOK, SHARE), lambda d, z: (d, 0, 0)),
+            out_specs=pl.BlockSpec((None, TOK, PART), lambda d, z: (d, 0, 0)),
         ),
-        out_shape=jax.ShapeDtypeStruct((DEPTH, TOK, SHARE), BF16),
+        out_shape=shaped(DEPTH, TOK, PART),
         compiler_params=params(),
-        cost_estimate=pl.CostEstimate(flops=130000000000, bytes_accessed=5_300_000, transcendentals=0),
+        cost_estimate=pl.CostEstimate(flops=1_000_000_000, bytes_accessed=2_600_000, transcendentals=0),
     )(level, returned, own_weight)
+    total = parts[0].astype(F32)
+    for d in range(1, DEPTH):
+        total += up_levels(parts[d], d).astype(F32)
+    return total.astype(BF16)
+
+
+def sum_over_depth(x):
+    return lax.psum_scatter(
+        x, "tensor", scatter_dimension=0, tiled=False,
+        axis_index_groups=[[2 * z + c for z in range(DEPTH)] for c in range(2)],
+    )
 
 
 def over_experts(x):
     return lax.all_to_all(x, "expert", split_axis=0, concat_axis=0, tiled=True)
+
+
+def return_rows(x):
+    return over_experts(x.reshape(GROUPS, CAP, x.shape[-1]))
 
 
 def swap_cores(x):
@@ -305,7 +326,6 @@
     picked = pick(x_half, weight_rows)
     own_rows = over_experts(picked).reshape(ALL_ROWS, HALF)
     lent = swap_cores(lend(1 - core_list, picked, wgu, wd))
-    own_rows, lent = lax.optimization_barrier((own_rows, lent))
     other_rows = swap_cores(own_rows)
     weight_rows, own_rows = lax.optimization_barrier((weight_rows, own_rows))
     weight = over_experts(weight_rows)
@@ -318,24 +338,30 @@
     weight = weight.reshape(GROUPS // 2, 1, 2 * TOK)
 
     inputs, gate, up, hidden = hidden_units(core_list, own_rows, other_rows, wgu)
-    pair_out = out_rows(core_list, hidden, swap_cores(hidden), wd, lent)
-    pair_out, gate = lax.optimization_barrier((pair_out, gate))
-    out_back = over_experts(pair_out.reshape(GROUPS, CAP, HALF))
+    out_direct, out_part = out_rows(core_list, hidden, swap_cores(hidden), wd, lent)
+    out_direct, gate = lax.optimization_barrier((out_direct, gate))
+    out_sum = sum_over_depth(out_part)
+    out_direct = return_rows(out_direct)
 
     cot, dgu = unit_grads(grad_rows, row_of, weight, gate, up, wd)
-    pair_back = back_rows(core_list, dgu, swap_cores(dgu), wgu, lent)
-    back_sum = lax.psum_scatter(
-        pair_back, "tensor", scatter_dimension=0, tiled=False,
-        axis_index_groups=[[2 * z + c for z in range(DEPTH)] for c in range(2)],
-    )
-    grad_back = over_experts(back_sum.reshape(GROUPS, CAP, SHARE))
+    back_direct, back_part = back_rows(core_list, out_direct, dgu, swap_cores(dgu), wgu, lent)
+    back_sum = sum_over_depth(back_part)
     grad_gate_up, grad_down = weight_grads(inputs, cot, dgu, hidden)
-    parts = depth_parts(level_list, out_back, own_weight)
-    mixed = parts[0].astype(F32)
-    for d in range(1, DEPTH):
-        mixed += up_levels(parts[d], d).astype(F32)
-    grad_tokens = combine(grad_back, own_weight)
-    return (mixed.astype(BF16), grad_tokens, grad_gate_up[None], grad_down[None])
+
+    out_sum, out_direct = lax.optimization_barrier((out_sum, out_direct))
+    out_sum = return_rows(out_sum)
+    back_direct, out_sum = lax.optimization_barrier((back_direct, out_sum))
+    back_direct = return_rows(back_direct)
+    back_sum, back_direct = lax.optimization_barrier((back_sum, back_direct))
+    back_sum = return_rows(back_sum)
+
+    mixed = jnp.concatenate(
+        [sum_levels(True, level_list, out_direct, own_weight), combine(True, out_sum, own_weight)], axis=1
+    )
+    grad_tokens = jnp.concatenate(
+        [sum_levels(False, level_list, back_direct, own_weight), combine(False, back_sum, own_weight)], axis=1
+    )
+    return (mixed, grad_tokens, grad_gate_up[None], grad_down[None])
 
 
 def solution(mesh):

time: 266 us -> 266 us (level)
  waiting for transfers between devices: 133 us -> 37.2 us
  blocking collectives: 0 us -> 88.5 us
  Pallas kernels: 70 us -> 77.8 us
    all_to_all x0 -> x2, blocking collectives: none -> 88.5 us  [over_experts(): return lax.all_to_all(x, 'expert', split_axis=0, concat_axis=0, tiled=True)]
    all_to_all x4, waiting for transfers between devices: 95.6 us -> 22.8 us  [over_experts(): return lax.all_to_all(x, 'expert', split_axis=0, concat_axis=0, tiled=True)]
    reduce_scatter x1 -> x2, waiting for transfers between devices: 12.1 us -> 0.03 us  [sum_over_depth(): lax.psum_scatter(x, 'tensor', scatter_dimension=0, tiled=False, axis_inde...]
    ppermute x4, waiting for transfers between devices: 14.3 us -> 5.52 us  [swap_cores(): return lax.ppermute(x, 'tensor', [(t, t ^ 1) for t in range(TENSOR)])]
    all_to_all x4, starting transfers between devices: 30.6 us -> 22.4 us  [over_experts(): return lax.all_to_all(x, 'expert', split_axis=0, concat_axis=0, tiled=True)]
    pallas_call x3 -> x5, Pallas kernels: 18.2 us -> 24.8 us  [the longest x2 10.6 us: sum_levels(): pl.pallas_call(lambda z_ref, *refs: combine_kernel(weighted, *refs), grid...]
    ppermute x3 -> x6, starting transfers between devices: 2.94 us -> 8.67 us  [up_levels(): lax.ppermute(x, 'tensor', [(t, (t + 2 * d) % TENSOR) for t in range(TENSO...]
    all_gather x1, waiting for transfers between devices: 4.62 us -> 0.01 us  [on_device(): grad_rows = lax.all_gather(mine, ('expert', 'tensor'), axis=0, tiled=True)]
  transfers between devices with their start and end apart: 13 -> 17, of which waited for: 10 -> 10; matrix products, arithmetic and copies ran while one was open for 3% -> 3% of each run, Pallas kernels for 25% -> 28%
where the time goes in v6:
time: 266 us; the launch traced here: 264 us
  blocking collectives  88.5 us (33%)
  Pallas kernels  77.8 us (29%)
  waiting for transfers between devices  37.2 us (14%)
  starting transfers between devices  31.4 us (12%)
  between operations  15.6 us (6%)
  local copies, waits for them, and re-layouts  8.05 us (3%)
  other arithmetic  5.24 us (2%)
    all_to_all x2, blocking collectives, over_experts(): return lax.all_to_all(x, 'expert', split_axis=0, concat_axis=0, tiled=True)  88.5 us
    all_to_all x4, waiting for transfers between devices, over_experts(): return lax.all_to_all(x, 'expert', split_axis=0, concat_axis=0, tiled=True)  22.8 us
    all_to_all x4, starting transfers between devices, over_experts(): return lax.all_to_all(x, 'expert', split_axis=0, concat_axis=0, tiled=True)  22.4 us
    pallas_call x1, Pallas kernels, weight_grads(): stepped(weight_grad_kernel, 0, TENSOR, [cols, cols, whole(dgu.shape), who...  13.4 us
    pallas_call x1, Pallas kernels, unit_grads(): stepped(unit_grad_kernel, 0, STEPS, [by_rows(STEP_GROUPS * TOK, D), ROW_S...  11.9 us
    pallas_call x1, Pallas kernels, hidden_units(): stepped(hidden_kernel, 1, STEPS, [by_rows(ROWS, HALF), by_rows(ROWS, HALF...  11.4 us
    pallas_call x2, Pallas kernels, sum_levels(): pl.pallas_call(lambda z_ref, *refs: combine_kernel(weighted, *refs), grid...  10.6 us
    pallas_call x1, Pallas kernels, back_rows(): stepped(back_kernel, 1, STEPS, [pl.BlockSpec(memory_space=pl.ANY), by_row...  9.25 us
  transfers between devices with their start and end apart: 17, of which 10 were waited for; matrix products, arithmetic and copies ran while one was open for 3% of the time, Pallas kernels for 28%

profile of v6, /device:TPU:2, one launch (start us, length us, event | category | flops | bytes accessed | tf_op | source)
XLA Modules:
  0.0 264.5 jit_solution(2985300381346172504)
XLA Ops:
  8.0 0.0 copy-start
  8.0 0.0 all-gather.2.cloned.1.call-start
  8.1 1.6 constant_dynamic-slice_fusion
  9.7 0.0 all-gather.2.cloned.1.call-update
  9.7 0.0 reduce-scatter.3.cloned.1.call-start
  9.8 1.3 select_reduce_fusion
  11.1 0.8 constant_dynamic-slice_fusion.1.x_ref
  12.0 4.8 %shard_map.93.after_ref = bf16[16,72,2048]{2,1,0:T(8,128)(2,1)} custom-call(bf16[128,2048]{1,0:T(8,128)(2,1)} %constant_dynamic-slice_fusion.1.x_ref, f32[16,128]{1,0:T(8,128)} %bitcast.2.w_ref), custom_call_target="tpu_custom_call" | custom-call | flops 600000000 | bytes 5300000 | tf_op jit(solution)/shard_map/pallas_call | solution.py:175
  16.8 69.5 %all_to_all.34 = bf16[16,72,2048]{2,1,0:T(8,128)(2,1)S(1)} all-to-all(bf16[16,72,2048]{2,1,0:T(8,128)(2,1)} %shard_map.93.after_ref), channel_id=1, replica_groups=mesh['expert'=16,'tensor'=8] {'expert'}, dimensions={0} | all-to-all | bytes 9437184 | tf_op jit(solution)/shard_map/all_to_all | solution.py:297
  86.3 0.0 collective-permute-start
  86.3 4.6 %shard_map.95 = bf16[3,192,2048]{2,1,0:T(8,128)(2,1)} custom-call(s32[1]{0:T(128)S(6)} %sub.8.core_ref, bf16[16,72,2048]{2,1,0:T(8,128)(2,1)} %shard_map.93.after_ref, bf16[2,192,4096]{2,1,0:T(8,128)(2,1)} %bitcast.50, bf16[192,4096]{1,0:T(8,128)(2,1)} %bitcast.45), custom_call_target="tpu_custom_call" | custom-call | bytes 4700000 | tf_op jit(solution)/shard_map/pallas_call | solution.py:184
  90.9 0.0 collective-permute-start.2
  90.9 3.4 %collective-permute-done.other_ref = bf16[1152,2048]{1,0:T(8,128)(2,1)} collective-permute-done((bf16[1152,2048]{1,0:T(8,128)(2,1)S(1)}, bf16[1152,2048]{1,0:T(8,128)(2,1)}, u32[]{:S(2)}, u32[]{:S(2)}) %collective-permute-start) | collective-permute-done | bytes 4718624 | tf_op jit(solution)/shard_map/ppermute | solution.py:305
  94.4 11.4 %shard_map.94 = (bf16[1152,4096]{1,0:T(8,128)(2,1)}, f32[1152,192]{1,0:T(8,128)}, f32[1152,192]{1,0:T(8,128)}, bf16[1152,256]{1,0:T(8,128)(2,1)}) custom-call(s32[1]{0:T(128)} %bitcast.1.core_ref, bf16[1152,2048]{1,0:T(8,128)(2,1)} %bitcast.49, bf16[1152,2048]{1,0:T(8,128)(2,1)} %collective-permute-done.other_ref, bf16[2,192,4096]{2,1,0:T(8,128)(2,1)} %bitcast.51), custom_call_target="tpu_custom_call" | custom-call | flops 4000000000 | bytes 25000000 | tf_op jit(solution)/shard_map/pallas_call | solution.py:197
  105.8 0.2 collective-permute-start.1
  105.9 0.0 collective-permute-done.2.lent_ref
  105.9 2.1 collective-permute-done.1.other_ref
  108.0 0.8 copy-done.8
  108.8 6.9 %shard_map.96 = (bf16[1152,1024]{1,0:T(8,128)(2,1)}, bf16[4,1152,256]{2,1,0:T(8,128)(2,1)}) custom-call(s32[1]{0:T(128)} %bitcast.1.core_ref, bf16[1152,256]{1,0:T(8,128)(2,1)} %get-tuple-element.27.own_ref.hid_ref, bf16[1152,256]{1,0:T(8,128)(2,1)} %copy-done.8, bf16[192,4096]{1,0:T(8,128)(2,1)} %bitcast.46, bf16[3,192,2048]{2,1,0:T(8,128)(2,1)} %copy-done.7), custom_call_target="tpu_custom_call" | custom-call | flops 2000000000 | bytes 8000000 | tf_op jit(solution)/shard_map/pallas_call | solution.py:210
  115.7 0.0 reduce-scatter.3.cloned.1.call-update
  115.7 4.9 %all-to-all-start.2 = ((f32[16,1,128]{2,1,0:T(1,128)}), f32[16,1,128]{2,1,0:T(1,128)S(1)}, u32[]{:S(2)}, u32[]{:S(2)}) async-start(f32[16,1,128]{2,1,0:T(1,128)} %bitcast.13), calls=%async_computation.3 | async-start | bytes 16384 | tf_op jit(solution)/shard_map/all_to_all | solution.py:297
  120.6 6.1 %all-to-all-done.2 = f32[16,1,128]{2,1,0:T(1,128)S(1)} async-done(((f32[16,1,128]{2,1,0:T(1,128)}), f32[16,1,128]{2,1,0:T(1,128)S(1)}, u32[]{:S(2)}, u32[]{:S(2)}) %all-to-all-start.2) | async-done | bytes 8224 | tf_op jit(solution)/shard_map/all_to_all | solution.py:297
  126.7 5.0 %all-to-all-start.1 = ((bf16[16,72,1024]{2,1,0:T(8,128)(2,1)}), bf16[16,72,1024]{2,1,0:T(8,128)(2,1)S(1)}, u32[]{:S(2)}, u32[]{:S(2)}) async-start(bf16[16,72,1024]{2,1,0:T(8,128)(2,1)} %bitcast.53), calls=%async_computation.2 | async-start | bytes 4718592 | tf_op jit(solution)/shard_map/all_to_all | solution.py:297
  131.7 0.0 reduce-scatter.5.cloned.1.call-start
  131.8 0.7 fusion.1
  132.5 11.9 %shard_map.98 = (bf16[1152,4096]{1,0:T(8,128)(2,1)}, bf16[2,1152,256]{2,1,0:T(8,128)(2,1)}) custom-call(bf16[2048,4096]{1,0:T(8,128)(2,1)} %all-gather.2.cloned.1.call-done.g_ref, s32[8,1,256]{2,1,0:T(1,128)} %bitcast.58, f32[8,1,256]{2,1,0:T(1,128)} %bitcast.57, f32[1152,192]{1,0:T(8,128)} %get-tuple-element.34.gate_ref, ...), custom_call_target="tpu_custom_call" | custom-call | flops 4000000000 | bytes 30000000 | tf_op jit(solution)/shard_map/pallas_call | solution.py:221
  144.4 0.0 collective-permute-start.6
  144.4 16.7 %all-to-all-done.1.refs_0_.after_ref = bf16[16,72,1024]{2,1,0:T(8,128)(2,1)S(1)} async-done(((bf16[16,72,1024]{2,1,0:T(8,128)(2,1)}), bf16[16,72,1024]{2,1,0:T(8,128)(2,1)S(1)}, u32[]{:S(2)}, u32[]{:S(2)}) %all-to-all-start.1) | async-done | bytes 2359328 | tf_op jit(solution)/shard_map/all_to_all | solution.py:297
  161.1 0.0 collective-permute-done.6.other_ref
  161.1 1.4 copy-done.4
  162.6 9.2 %shard_map.99 = (bf16[1152,1024]{1,0:T(8,128)(2,1)}, bf16[4,1152,256]{2,1,0:T(8,128)(2,1)}) custom-call(s32[1]{0:T(128)} %bitcast.1.core_ref, bf16[16,72,1024]{2,1,0:T(8,128)(2,1)} %copy-done.4, bf16[2,1152,256]{2,1,0:T(8,128)(2,1)} %get-tuple-element.36.own_ref.dgu_ref, bf16[2,1152,256]{2,1,0:T(8,128)(2,1)} %collective-permute-done.6.other_ref, ...), custom_call_target="tpu_custom_call" | custom-call | flops 4000000000 | bytes 10000000 | tf_op jit(solution)/shard_map/pallas_call | solution.py:234
  171.8 0.0 reduce-scatter.5.cloned.1.call-update
  171.8 0.0 reduce-scatter.3.cloned.1.call-done
  171.9 18.9 %all_to_all.35.refs_0_ = bf16[16,72,256]{2,1,0:T(8,128)(2,1)} all-to-all(bf16[16,72,256]{2,1,0:T(8,128)(2,1)} %bitcast.55), channel_id=1, replica_groups=mesh['expert'=16,'tensor'=8] {'expert'}, dimensions={0} | all-to-all | bytes 1179648 | tf_op jit(solution)/shard_map/all_to_all | solution.py:297
  190.8 5.0 %all-to-all-start.4 = ((bf16[16,72,1024]{2,1,0:T(8,128)(2,1)}), bf16[16,72,1024]{2,1,0:T(8,128)(2,1)S(1)}, u32[]{:S(2)}, u32[]{:S(2)}) async-start(bf16[16,72,1024]{2,1,0:T(8,128)(2,1)} %bitcast.20), calls=%async_computation.6 | async-start | bytes 4718592 | tf_op jit(solution)/shard_map/all_to_all | solution.py:297
  195.8 1.4 copy.29.refs_1_
  197.2 5.4 %shard_map.97 = bf16[4,128,256]{2,1,0:T(8,128)(2,1)} custom-call(s32[1]{0:T(128)} %bitcast.z_ref, bf16[16,72,1024]{2,1,0:T(8,128)(2,1)} %copy-done.4, f32[128,16]{1,0:T(8,128)} %copy.29.refs_1_), custom_call_target="tpu_custom_call" | custom-call | flops 1000000000 | bytes 2600000 | tf_op jit(solution)/shard_map/pallas_call | solution.py:268
  202.6 0.9 slice_bitcast_fusion.6
  203.5 4.6 %collective-permute-start.5 = (bf16[128,256]{1,0:T(8,128)(2,1)S(1)}, bf16[128,256]{1,0:T(8,128)(2,1)S(1)}, u32[]{:S(2)}, u32[]{:S(2)}) collective-permute-start(bf16[128,256]{1,0:T(8,128)(2,1)S(1)} %get-tuple-element.52), channel_id=1, source_target_pairs={{0,6},{1,7},{2,0},{3,1},{4,2},{5,3},{6,4},{7,5},{8,14},{9,15},{10,... | collective-permute-start | bytes 196616 | tf_op jit(solution)/shard_map/ppermute | solution.py:309
  208.1 0.0 collective-permute-start.4
  208.1 1.0 collective-permute-start.3
  209.1 1.5 collective-permute-done.5
  210.6 3.4 %collective-permute-done.4 = bf16[128,256]{1,0:T(8,128)(2,1)S(1)} collective-permute-done((bf16[128,256]{1,0:T(8,128)(2,1)S(1)}, bf16[128,256]{1,0:T(8,128)(2,1)S(1)}, u32[]{:S(2)}, u32[]{:S(2)}) %collective-permute-start.4) | collective-permute-done | bytes 65568 | tf_op jit(solution)/shard_map/ppermute | solution.py:309
  214.0 0.3 collective-permute-done.3
  214.3 0.9 fusion.7
  215.2 13.4 %shard_map.103 = (bf16[2,192,4096]{2,1,0:T(8,128)(2,1)}, bf16[192,4096]{1,0:T(8,128)(2,1)}) custom-call(bf16[1152,4096]{1,0:T(8,128)(2,1)} %get-tuple-element.44.in_ref, bf16[1152,4096]{1,0:T(8,128)(2,1)} %get-tuple-element.45.cot_ref, bf16[2,1152,256]{2,1,0:T(8,128)(2,1)} %get-tuple-element.36.own_ref.dgu_ref, ...), custom_call_target="tpu_custom_call" | custom-call | flops 6000000000 | bytes 25000000 | tf_op jit(solution)/shard_map/pallas_call | solution.py:246
  228.6 2.5 shard_map.100
  231.1 0.0 all-to-all-done.4.refs_0_
  231.1 0.0 copy-start.5
  231.1 7.6 %all-to-all-start.5 = ((bf16[16,72,256]{2,1,0:T(8,128)(2,1)}), bf16[16,72,256]{2,1,0:T(8,128)(2,1)}, u32[]{:S(2)}, u32[]{:S(2)}) async-start(bf16[16,72,256]{2,1,0:T(8,128)(2,1)} %bitcast.54), calls=%async_computation.7 | async-start | bytes 1179648 | tf_op jit(solution)/shard_map/all_to_all | solution.py:297
  238.7 0.0 copy-start.1
  238.7 5.2 %shard_map.101 = bf16[4,128,256]{2,1,0:T(8,128)(2,1)} custom-call(s32[1]{0:T(128)} %bitcast.z_ref, bf16[16,72,1024]{2,1,0:T(8,128)(2,1)} %copy-done.3, f32[128,16]{1,0:T(8,128)} %copy.29.refs_1_), custom_call_target="tpu_custom_call" | custom-call | flops 1000000000 | bytes 2600000 | tf_op jit(solution)/shard_map/pallas_call | solution.py:268
  243.9 0.9 slice_bitcast_fusion.2
  244.8 0.9 collective-permute-start.9
  245.8 0.9 collective-permute-start.8
  246.6 1.3 collective-permute-start.7
  247.9 0.7 pad_maximum_fusion
  248.6 0.6 collective-permute-done.9
  249.2 2.4 collective-permute-done.8
  251.5 0.7 collective-permute-done.7
  252.2 0.9 fusion.4
  253.1 0.0 all-to-all-done.5.refs_0_
  253.1 2.4 shard_map.102
  255.6 1.5 pad_maximum_fusion.1
  (16 shorter events, 0.0 us)
Async XLA Ops:
  8.0 3.1 %copy-start = (bf16[128,4096]{1,0:T(8,128)(2,1)S(1)}, bf16[128,4096]{1,0:T(8,128)(2,1)}, u32[]{:S(2)}) copy-start(bf16[128,4096]{1,0:T(8,128)(2,1)} %param.6) | copy-start | bytes 3145732
  8.0 124.5 %all-gather.2.cloned.1.call-start = ((), (), s32[]{:S(2)}) async-start(), calls=%async_computation.9 | async-start | bytes 16908288 | tf_op jit(solution)/shard_map/all_gather | solution.py:320
  9.7 162.1 %reduce-scatter.3.cloned.1.call-start = ((), (), s32[]{:S(2)}) async-start(), calls=%async_computation.8 | async-start | bytes 2949120 | tf_op jit(solution)/shard_map/reduce_scatter | solution.py:290
  86.3 4.6 %copy-start.2 = (bf16[16,72,2048]{2,1,0:T(8,128)(2,1)}, bf16[16,72,2048]{2,1,0:T(8,128)(2,1)S(1)}, u32[]{:S(2)}) copy-start(bf16[16,72,2048]{2,1,0:T(8,128)(2,1)S(1)} %all_to_all.34) | copy-start | bytes 14155780
  86.3 8.0 %collective-permute-start = (bf16[1152,2048]{1,0:T(8,128)(2,1)S(1)}, bf16[1152,2048]{1,0:T(8,128)(2,1)}, u32[]{:S(2)}, u32[]{:S(2)}) collective-permute-start(bf16[1152,2048]{1,0:T(8,128)(2,1)S(1)} %bitcast.48), channel_id=1, source_target_pairs={{0,1},{1,0},{2,3},{3,2},{4,5},{5,4},{6,7},{7,6},{8,9},{9,8},{10,11... | collective-permute-start | bytes 14155784 | tf_op jit(solution)/shard_map/ppermute | solution.py:305
  90.9 15.0 %collective-permute-start.2 = (bf16[3,192,2048]{2,1,0:T(8,128)(2,1)}, bf16[3,192,2048]{2,1,0:T(8,128)(2,1)S(1)}, u32[]{:S(2)}, u32[]{:S(2)}) collective-permute-start(bf16[3,192,2048]{2,1,0:T(8,128)(2,1)} %shard_map.95), channel_id=1, source_target_pairs={{0,1},{1,0},{2,3},{3,2},{4,5},{5,4},{6,7},{7,6},{8,9},{9,8},{10,11... | collective-permute-start | bytes 7077896 | tf_op jit(solution)/shard_map/ppermute | solution.py:305
  105.8 2.3 collective-permute-start.1
  105.9 2.1 copy-start.7
  108.0 0.8 copy-start.8
  115.7 11.0 %all-to-all-start.2 = ((f32[16,1,128]{2,1,0:T(1,128)}), f32[16,1,128]{2,1,0:T(1,128)S(1)}, u32[]{:S(2)}, u32[]{:S(2)}) async-start(f32[16,1,128]{2,1,0:T(1,128)} %bitcast.13), calls=%async_computation.3 | async-start | bytes 16384 | tf_op jit(solution)/shard_map/all_to_all | solution.py:297
  126.7 5.0 %copy-start.6 = (f32[16,1,128]{2,1,0:T(1,128)}, f32[16,1,128]{2,1,0:T(1,128)S(1)}, u32[]{:S(2)}) copy-start(f32[16,1,128]{2,1,0:T(1,128)S(1)} %all-to-all-done.2) | copy-start | bytes 24580
  126.7 34.4 %all-to-all-start.1 = ((bf16[16,72,1024]{2,1,0:T(8,128)(2,1)}), bf16[16,72,1024]{2,1,0:T(8,128)(2,1)S(1)}, u32[]{:S(2)}, u32[]{:S(2)}) async-start(bf16[16,72,1024]{2,1,0:T(8,128)(2,1)} %bitcast.53), calls=%async_computation.2 | async-start | bytes 4718592 | tf_op jit(solution)/shard_map/all_to_all | solution.py:297
  131.7 99.4 %reduce-scatter.5.cloned.1.call-start = ((), (), s32[]{:S(2)}) async-start(), calls=%async_computation.10 | async-start | bytes 2949120 | tf_op jit(solution)/shard_map/reduce_scatter | solution.py:290
  144.4 16.7 %collective-permute-start.6 = (bf16[2,1152,256]{2,1,0:T(8,128)(2,1)}, bf16[2,1152,256]{2,1,0:T(8,128)(2,1)}, u32[]{:S(2)}, u32[]{:S(2)}) collective-permute-start(bf16[2,1152,256]{2,1,0:T(8,128)(2,1)} %get-tuple-element.36.own_ref.dgu_ref), channel_id=1, source_target_pairs={{0,1},{1,0},{2,3},{3,2},{4,5},{5,4},{6,7},{7,6},{8,9},{9,8},{10,11... | collective-permute-start | bytes 3538952 | tf_op jit(solution)/shard_map/ppermute | solution.py:305
  161.1 1.5 copy-start.4
  190.8 40.3 %all-to-all-start.4 = ((bf16[16,72,1024]{2,1,0:T(8,128)(2,1)}), bf16[16,72,1024]{2,1,0:T(8,128)(2,1)S(1)}, u32[]{:S(2)}, u32[]{:S(2)}) async-start(bf16[16,72,1024]{2,1,0:T(8,128)(2,1)} %bitcast.20), calls=%async_computation.6 | async-start | bytes 4718592 | tf_op jit(solution)/shard_map/all_to_all | solution.py:297
  203.5 7.1 %collective-permute-start.5 = (bf16[128,256]{1,0:T(8,128)(2,1)S(1)}, bf16[128,256]{1,0:T(8,128)(2,1)S(1)}, u32[]{:S(2)}, u32[]{:S(2)}) collective-permute-start(bf16[128,256]{1,0:T(8,128)(2,1)S(1)} %get-tuple-element.52), channel_id=1, source_target_pairs={{0,6},{1,7},{2,0},{3,1},{4,2},{5,3},{6,4},{7,5},{8,14},{9,15},{10,... | collective-permute-start | bytes 196616 | tf_op jit(solution)/shard_map/ppermute | solution.py:309
  208.1 5.9 %collective-permute-start.4 = (bf16[128,256]{1,0:T(8,128)(2,1)S(1)}, bf16[128,256]{1,0:T(8,128)(2,1)S(1)}, u32[]{:S(2)}, u32[]{:S(2)}) collective-permute-start(bf16[128,256]{1,0:T(8,128)(2,1)S(1)} %get-tuple-element.53), channel_id=1, source_target_pairs={{0,4},{1,5},{2,6},{3,7},{4,0},{5,1},{6,2},{7,3},{8,12},{9,13},{10,... | collective-permute-start | bytes 196616 | tf_op jit(solution)/shard_map/ppermute | solution.py:309
  208.1 6.2 %collective-permute-start.3 = (bf16[128,256]{1,0:T(8,128)(2,1)S(1)}, bf16[128,256]{1,0:T(8,128)(2,1)S(1)}, u32[]{:S(2)}, u32[]{:S(2)}) collective-permute-start(bf16[128,256]{1,0:T(8,128)(2,1)S(1)} %get-tuple-element.51), channel_id=1, source_target_pairs={{0,2},{1,3},{2,4},{3,5},{4,6},{5,7},{6,0},{7,1},{8,10},{9,11},{10,... | collective-permute-start | bytes 196616 | tf_op jit(solution)/shard_map/ppermute | solution.py:309
  231.1 7.6 %copy-start.3 = (bf16[16,72,1024]{2,1,0:T(8,128)(2,1)}, bf16[16,72,1024]{2,1,0:T(8,128)(2,1)S(1)}, u32[]{:S(2)}) copy-start(bf16[16,72,1024]{2,1,0:T(8,128)(2,1)S(1)} %all-to-all-done.4.refs_0_) | copy-start | bytes 7077892
  231.1 16.8 %copy-start.5 = (bf16[128,256]{1,0:T(8,128)(2,1)S(1)}, bf16[128,256]{1,0:T(8,128)(2,1)}, u32[]{:S(2)}) copy-start(bf16[128,256]{1,0:T(8,128)(2,1)} %shard_map.100) | copy-start | bytes 196612
  231.1 22.0 %all-to-all-start.5 = ((bf16[16,72,256]{2,1,0:T(8,128)(2,1)}), bf16[16,72,256]{2,1,0:T(8,128)(2,1)}, u32[]{:S(2)}, u32[]{:S(2)}) async-start(bf16[16,72,256]{2,1,0:T(8,128)(2,1)} %bitcast.54), calls=%async_computation.7 | async-start | bytes 1179648 | tf_op jit(solution)/shard_map/all_to_all | solution.py:297
  238.7 18.3 %copy-start.1 = (bf16[128,4096]{1,0:T(8,128)(2,1)S(1)}, bf16[128,4096]{1,0:T(8,128)(2,1)}, u32[]{:S(2)}) copy-start(bf16[128,4096]{1,0:T(8,128)(2,1)} %param.6) | copy-start | bytes 3145732
  244.8 4.3 %collective-permute-start.9 = (bf16[128,256]{1,0:T(8,128)(2,1)S(1)}, bf16[128,256]{1,0:T(8,128)(2,1)S(1)}, u32[]{:S(2)}, u32[]{:S(2)}) collective-permute-start(bf16[128,256]{1,0:T(8,128)(2,1)S(1)} %get-tuple-element.49), channel_id=1, source_target_pairs={{0,6},{1,7},{2,0},{3,1},{4,2},{5,3},{6,4},{7,5},{8,14},{9,15},{10,... | collective-permute-start | bytes 196616 | tf_op jit(solution)/shard_map/ppermute | solution.py:309
  245.8 5.8 %collective-permute-start.8 = (bf16[128,256]{1,0:T(8,128)(2,1)S(1)}, bf16[128,256]{1,0:T(8,128)(2,1)S(1)}, u32[]{:S(2)}, u32[]{:S(2)}) collective-permute-start(bf16[128,256]{1,0:T(8,128)(2,1)S(1)} %get-tuple-element.50), channel_id=1, source_target_pairs={{0,4},{1,5},{2,6},{3,7},{4,0},{5,1},{6,2},{7,3},{8,12},{9,13},{10,... | collective-permute-start | bytes 196616 | tf_op jit(solution)/shard_map/ppermute | solution.py:309
  246.6 5.6 %collective-permute-start.7 = (bf16[128,256]{1,0:T(8,128)(2,1)S(1)}, bf16[128,256]{1,0:T(8,128)(2,1)S(1)}, u32[]{:S(2)}, u32[]{:S(2)}) collective-permute-start(bf16[128,256]{1,0:T(8,128)(2,1)S(1)} %get-tuple-element.48), channel_id=1, source_target_pairs={{0,2},{1,3},{2,4},{3,5},{4,6},{5,7},{6,0},{7,1},{8,10},{9,11},{10,... | collective-permute-start | bytes 196616 | tf_op jit(solution)/shard_map/ppermute | solution.py:309
Sparse Core Ops, SparseCore 0:
  12.6 109.5 all-gather.1
Sparse Core Ops, SparseCore 1:
  115.8 32.2 reduce-scatter.2
  171.9 35.1 reduce-scatter.4

commit v7 on v5

--- a/solution.py
+++ b/solution.py
@@ -55,13 +55,12 @@
     o_ref[2] = wd_ref[...]
 
 
-def hidden_kernel(core_ref, own_ref, other_ref, wgu_ref, in_ref, gate_ref, up_ref, hid_ref):
-    core = core_ref[0]
-    in_ref[:, pl.ds(pl.multiple_of(core * HALF, HALF), HALF)] = own_ref[...]
-    in_ref[:, pl.ds(pl.multiple_of((1 - core) * HALF, HALF), HALF)] = other_ref[...]
-    rows = in_ref[...]
-    gate = nt(rows, wgu_ref[0])
-    up = nt(rows, wgu_ref[1])
+def hidden_kernel(core_ref, own_ref, other_ref, wgu_ref, gate_ref, up_ref, hid_ref):
+    mine = pl.ds(pl.multiple_of(core_ref[0] * HALF, HALF), HALF)
+    theirs = pl.ds(pl.multiple_of((1 - core_ref[0]) * HALF, HALF), HALF)
+    own, other = own_ref[...], other_ref[...]
+    gate = nt(own, wgu_ref[0, :, mine]) + nt(other, wgu_ref[0, :, theirs])
+    up = nt(own, wgu_ref[1, :, mine]) + nt(other, wgu_ref[1, :, theirs])
     gate_ref[...] = gate
     up_ref[...] = up
     hid_ref[:, :UNITS] = (gate * jax.nn.sigmoid(gate) * up).astype(BF16)
@@ -92,11 +91,21 @@
     dgu_ref[1, :, :UNITS] = (dhid * gate * sig).astype(BF16)
 
 
-def weight_grad_kernel(in_ref, cot_ref, dgu_ref, hid_ref, gu_ref, down_ref):
-    x = in_ref[...]
-    gu_ref[0] = tn(dgu_ref[0, :, :UNITS], x).astype(BF16)
-    gu_ref[1] = tn(dgu_ref[1, :, :UNITS], x).astype(BF16)
+def weight_grad_kernel(core_ref, own_ref, other_ref, cot_ref, dgu_ref, hid_ref, gu_ref, down_ref):
     down_ref[...] = tn(hid_ref[:, :UNITS], cot_ref[...]).astype(BF16)
+    owned = pl.program_id(0) // DEPTH == core_ref[0]
+
+    def write(x):
+        gu_ref[0] = tn(dgu_ref[0, :, :UNITS], x).astype(BF16)
+        gu_ref[1] = tn(dgu_ref[1, :, :UNITS], x).astype(BF16)
+
+    @pl.when(owned)
+    def _():
+        write(own_ref[...])
+
+    @pl.when(jnp.logical_not(owned))
+    def _():
+        write(other_ref[...])
 
 
 def back_kernel(core_ref, own_ref, other_ref, wgu_ref, lent_ref, o_ref):
@@ -195,12 +204,12 @@
     return stepped(
         hidden_kernel, 1, STEPS,
         [by_rows(ROWS, HALF), by_rows(ROWS, HALF), whole(wgu.shape)],
-        [by_rows(ROWS, D), by_rows(ROWS, UNITS), by_rows(ROWS, UNITS), by_rows(ROWS, WIDE)],
-        [
-            shaped(ALL_ROWS, D), shaped(ALL_ROWS, UNITS, dtype=F32), shaped(ALL_ROWS, UNITS, dtype=F32),
+        [by_rows(ROWS, UNITS), by_rows(ROWS, UNITS), by_rows(ROWS, WIDE)],
+        [
+            shaped(ALL_ROWS, UNITS, dtype=F32), shaped(ALL_ROWS, UNITS, dtype=F32),
             shaped(ALL_ROWS, WIDE),
         ],
-        4_000_000_000, 25_000_000,
+        4_000_000_000, 15_000_000,
     )(core, own, other, wgu)
 
 
@@ -236,17 +245,25 @@
     )(core, own, other, wgu, lent)
 
 
-def weight_grads(inputs, cot, dgu, hidden):
-    cols = pl.BlockSpec((ALL_ROWS, SHARE), lambda i: (0, i))
-    return stepped(
-        weight_grad_kernel, 0, TENSOR,
-        [cols, cols, whole(dgu.shape), whole(hidden.shape)],
-        [
-            pl.BlockSpec((2, UNITS, SHARE), lambda i: (0, 0, i)),
-            pl.BlockSpec((UNITS, SHARE), lambda i: (0, i)),
+def weight_grads(core, own, other, cot, dgu, hidden):
+    def block(first):
+        return lambda i, c: (0, jnp.clip(i - DEPTH * (c[0] if first else 1 - c[0]), 0, DEPTH - 1))
+
+    return stepped(
+        weight_grad_kernel, 1, TENSOR,
+        [
+            pl.BlockSpec((ALL_ROWS, SHARE), block(True)),
+            pl.BlockSpec((ALL_ROWS, SHARE), block(False)),
+            pl.BlockSpec((ALL_ROWS, SHARE), lambda i, c: (0, i)),
+            whole(dgu.shape),
+            whole(hidden.shape),
+        ],
+        [
+            pl.BlockSpec((2, UNITS, SHARE), lambda i, c: (0, 0, i)),
+            pl.BlockSpec((UNITS, SHARE), lambda i, c: (0, i)),
         ],
         [shaped(2, UNITS, D), shaped(UNITS, D)], 6_000_000_000, 25_000_000,
-    )(inputs, cot, dgu, hidden)
+    )(core, own, other, cot, dgu, hidden)
 
 
 def combine(returned, own_weight):
@@ -318,7 +335,7 @@
     row_of = jnp.where(mask, slot + offset[:, None], -1).reshape(GROUPS // 2, 1, 2 * TOK)
     weight = weight.reshape(GROUPS // 2, 1, 2 * TOK)
 
-    inputs, gate, up, hidden = hidden_units(core_list, own_rows, other_rows, wgu)
+    gate, up, hidden = hidden_units(core_list, own_rows, other_rows, wgu)
     pair_out = out_rows(core_list, hidden, swap_cores(hidden), wd, lent)
     pair_out, gate = lax.optimization_barrier((pair_out, gate))
     out_back = over_experts(pair_out.reshape(GROUPS, CAP, HALF))
@@ -329,7 +346,7 @@
         pair_back, "tensor", scatter_dimension=0, tiled=False,
         axis_index_groups=[[2 * z + c for z in range(DEPTH)] for c in range(2)],
     )
-    grad_gate_up, grad_down = weight_grads(inputs, cot, dgu, hidden)
+    grad_gate_up, grad_down = weight_grads(core_list, own_rows, other_rows, cot, dgu, hidden)
     parts = depth_parts(level_list, out_back, own_weight, grad_down)
     parts, back_sum = lax.optimization_barrier((parts, back_sum))
     grad_back = over_experts(back_sum.reshape(GROUPS, CAP, SHARE))

time: 244 us -> 243 us (level)
  no operation moved by 1% of the time
where the time goes in v7:
time: 243 us; the launch traced here: 240 us
  Pallas kernels  71.8 us (30%)
  blocking collectives  69.5 us (29%)
  waiting for transfers between devices  48.2 us (20%)
  starting transfers between devices  23.7 us (10%)
  between operations  14.1 us (6%)
  local copies, waits for them, and re-layouts  9.24 us (4%)
  other arithmetic  2.95 us (1%)
    all_to_all x1, blocking collectives, over_experts(): return lax.all_to_all(x, 'expert', split_axis=0, concat_axis=0, tiled=True)  69.5 us
    all_to_all x3, waiting for transfers between devices, over_experts(): return lax.all_to_all(x, 'expert', split_axis=0, concat_axis=0, tiled=True)  29.4 us
    all_to_all x3, starting transfers between devices, over_experts(): return lax.all_to_all(x, 'expert', split_axis=0, concat_axis=0, tiled=True)  19.1 us
    pallas_call x1, Pallas kernels, weight_grads(): stepped(weight_grad_kernel, 1, TENSOR, [pl.BlockSpec((ALL_ROWS, SHARE), b...  15.2 us
    pallas_call x1, Pallas kernels, unit_grads(): stepped(unit_grad_kernel, 0, STEPS, [by_rows(STEP_GROUPS * TOK, D), ROW_S...  11.9 us
    pallas_call x1, Pallas kernels, hidden_units(): stepped(hidden_kernel, 1, STEPS, [by_rows(ROWS, HALF), by_rows(ROWS, HALF...  10 us
    pallas_call x1, Pallas kernels, back_rows(): stepped(back_kernel, 1, STEPS, [by_rows(2, ROWS, WIDE), by_rows(2, ROWS,...  9.27 us
    reduce_scatter x1, waiting for transfers between devices, on_device(): lax.psum_scatter(pair_back, 'tensor', scatter_dimension=0, tiled=False, a...  7.01 us
  transfers between devices with their start and end apart: 12, of which 7 were waited for; matrix products, arithmetic and copies ran while one was open for 3% of the time, Pallas kernels for 29%

profile of v7, /device:TPU:2, one launch (start us, length us, event | category | flops | bytes accessed | tf_op | source)
XLA Modules:
  0.0 240.2 jit_solution(15830855941881865909)
XLA Ops:
  7.2 0.0 copy-start
  7.2 0.0 all-gather.2.cloned.1.call-start
  7.2 1.6 constant_dynamic-slice_fusion
  8.9 0.0 all-gather.2.cloned.1.call-update
  8.9 1.3 select_reduce_fusion
  10.2 0.0 copy-done
  10.2 0.8 constant_dynamic-slice_fusion.1.x_ref
  11.1 4.8 %shard_map.93.after_ref = bf16[16,72,2048]{2,1,0:T(8,128)(2,1)} custom-call(bf16[128,2048]{1,0:T(8,128)(2,1)} %constant_dynamic-slice_fusion.1.x_ref, f32[16,128]{1,0:T(8,128)} %bitcast.2.w_ref), custom_call_target="tpu_custom_call" | custom-call | flops 600000000 | bytes 5300000 | tf_op jit(solution)/shard_map/pallas_call | solution.py:182
  15.9 69.5 %all_to_all.24 = bf16[16,72,2048]{2,1,0:T(8,128)(2,1)S(1)} all-to-all(bf16[16,72,2048]{2,1,0:T(8,128)(2,1)} %shard_map.93.after_ref), channel_id=1, replica_groups=mesh['expert'=16,'tensor'=8] {'expert'}, dimensions={0} | all-to-all | bytes 9437184 | tf_op jit(solution)/shard_map/all_to_all | solution.py:299
  85.5 0.0 copy-start.2
  85.5 0.0 collective-permute-start
  85.5 4.6 %shard_map.95 = bf16[3,192,2048]{2,1,0:T(8,128)(2,1)} custom-call(s32[1]{0:T(128)S(6)} %sub.8.core_ref, bf16[16,72,2048]{2,1,0:T(8,128)(2,1)} %shard_map.93.after_ref, bf16[2,192,4096]{2,1,0:T(8,128)(2,1)} %bitcast.36, bf16[192,4096]{1,0:T(8,128)(2,1)} %bitcast.30), custom_call_target="tpu_custom_call" | custom-call | bytes 4700000 | tf_op jit(solution)/shard_map/pallas_call | solution.py:191
  90.1 0.0 copy-done.2
  90.1 0.0 collective-permute-start.2
  90.1 3.4 %collective-permute-done.other_ref = bf16[1152,2048]{1,0:T(8,128)(2,1)} collective-permute-done((bf16[1152,2048]{1,0:T(8,128)(2,1)S(1)}, bf16[1152,2048]{1,0:T(8,128)(2,1)}, u32[]{:S(2)}, u32[]{:S(2)}) %collective-permute-start) | collective-permute-done | bytes 4718624 | tf_op jit(solution)/shard_map/ppermute | solution.py:303
  93.5 10.0 %shard_map.94 = (f32[1152,192]{1,0:T(8,128)}, f32[1152,192]{1,0:T(8,128)}, bf16[1152,256]{1,0:T(8,128)(2,1)}) custom-call(s32[1]{0:T(128)} %bitcast.1.core_ref, bf16[1152,2048]{1,0:T(8,128)(2,1)} %bitcast.34, bf16[1152,2048]{1,0:T(8,128)(2,1)} %collective-permute-done.other_ref, bf16[2,192,4096]{2,1,0:T(8,128)(2,1)} %bitcast.37), custom_call_target="tpu_custom_call" | custom-call | flops 4000000000 | bytes 15000000 | tf_op jit(solution)/shard_map/pallas_call | solution.py:204
  103.5 0.3 collective-permute-start.1
  103.9 4.6 %all-to-all-start.2 = ((f32[16,1,128]{2,1,0:T(1,128)}), f32[16,1,128]{2,1,0:T(1,128)S(1)}, u32[]{:S(2)}, u32[]{:S(2)}) async-start(f32[16,1,128]{2,1,0:T(1,128)} %bitcast.8), calls=%async_computation.2 | async-start | bytes 16384 | tf_op jit(solution)/shard_map/all_to_all | solution.py:299
  108.5 0.0 collective-permute-done.2.lent_ref
  108.5 0.0 copy-start.4
  108.5 0.0 collective-permute-done.1.other_ref
  108.5 1.4 copy-done.4
  109.9 0.0 copy-start.5
  109.9 0.8 copy-done.5
  110.7 6.8 %shard_map.96 = bf16[1152,2048]{1,0:T(8,128)(2,1)} custom-call(s32[1]{0:T(128)} %bitcast.1.core_ref, bf16[1152,256]{1,0:T(8,128)(2,1)} %get-tuple-element.18.own_ref.hid_ref, bf16[1152,256]{1,0:T(8,128)(2,1)} %copy-done.5, bf16[192,4096]{1,0:T(8,128)(2,1)} %bitcast.31, bf16[3,192,2048]{2,1,0:T(8,128)(2,1)} %copy-done.4), custom_call_target="tpu_custom_call" | custom-call | flops 2000000000 | bytes 8000000 | tf_op jit(solution)/shard_map/pallas_call | solution.py:217
  117.5 0.0 all-to-all-done.2
  117.5 0.0 copy-start.6
  117.5 7.3 %all-to-all-start.1 = ((bf16[16,72,2048]{2,1,0:T(8,128)(2,1)}), bf16[16,72,2048]{2,1,0:T(8,128)(2,1)}, u32[]{:S(2)}, u32[]{:S(2)}) async-start(bf16[16,72,2048]{2,1,0:T(8,128)(2,1)} %bitcast.29), calls=%async_computation.1 | async-start | bytes 9437184 | tf_op jit(solution)/shard_map/all_to_all | solution.py:299
  124.8 0.0 reduce-scatter.2.cloned.1.call-start
  124.8 0.0 copy-done.6
  124.8 0.7 fusion.1
  125.6 0.0 all-gather.2.cloned.1.call-done.g_ref
  125.6 11.9 %shard_map.97 = (bf16[1152,4096]{1,0:T(8,128)(2,1)}, bf16[2,1152,256]{2,1,0:T(8,128)(2,1)}) custom-call(bf16[2048,4096]{1,0:T(8,128)(2,1)} %all-gather.2.cloned.1.call-done.g_ref, s32[8,1,256]{2,1,0:T(1,128)} %bitcast.42, f32[8,1,256]{2,1,0:T(1,128)} %bitcast.41, f32[1152,192]{1,0:T(8,128)} %get-tuple-element.22.gate_ref, ...), custom_call_target="tpu_custom_call" | custom-call | flops 4000000000 | bytes 30000000 | tf_op jit(solution)/shard_map/pallas_call | solution.py:228
  137.5 0.0 collective-permute-start.3
  137.5 3.1 %collective-permute-done.3.other_ref = bf16[2,1152,256]{2,1,0:T(8,128)(2,1)S(1)} collective-permute-done((bf16[2,1152,256]{2,1,0:T(8,128)(2,1)}, bf16[2,1152,256]{2,1,0:T(8,128)(2,1)S(1)}, u32[]{:S(2)}, u32[]{:S(2)}) %collective-permute-start.3) | collective-permute-done | bytes 1179680 | tf_op jit(solution)/shard_map/ppermute | solution.py:303
  140.6 0.0 copy-start.7
  140.6 1.0 copy-done.7
  141.6 9.3 %shard_map.100 = bf16[4,1152,512]{2,1,0:T(8,128)(2,1)} custom-call(s32[1]{0:T(128)} %bitcast.1.core_ref, bf16[2,1152,256]{2,1,0:T(8,128)(2,1)} %get-tuple-element.25.dgu_ref.own_ref, bf16[2,1152,256]{2,1,0:T(8,128)(2,1)} %copy-done.7, bf16[2,192,4096]{2,1,0:T(8,128)(2,1)} %bitcast.38, bf16[3,192,2048]{2,1,0:T(8,128)(2,1)} %copy-done.4), custom_call_target="tpu_custom_call" | custom-call | flops 4000000000 | bytes 10000000 | tf_op jit(solution)/shard_map/pallas_call | solution.py:241
  150.9 0.0 reduce-scatter.2.cloned.1.call-update
  150.9 1.4 copy.33.w_ref
  152.3 15.2 %shard_map.98 = (bf16[2,192,4096]{2,1,0:T(8,128)(2,1)}, bf16[192,4096]{1,0:T(8,128)(2,1)}) custom-call(s32[1]{0:T(128)} %bitcast.1.core_ref, bf16[1152,2048]{1,0:T(8,128)(2,1)} %bitcast.35, bf16[1152,2048]{1,0:T(8,128)(2,1)} %collective-permute-done.other_ref, bf16[1152,4096]{1,0:T(8,128)(2,1)} %get-tuple-element.24.cot_ref, ...), custom_call_target="tpu_custom_call" | custom-call | flops 6000000000 | bytes 25000000 | tf_op jit(solution)/shard_map/pallas_call | solution.py:252
  167.5 24.2 %all-to-all-done.1.r_ref = bf16[16,72,2048]{2,1,0:T(8,128)(2,1)} async-done(((bf16[16,72,2048]{2,1,0:T(8,128)(2,1)}), bf16[16,72,2048]{2,1,0:T(8,128)(2,1)}, u32[]{:S(2)}, u32[]{:S(2)}) %all-to-all-start.1) | async-done | bytes 4718624 | tf_op jit(solution)/shard_map/all_to_all | solution.py:299
  191.7 0.0 copy-start.1
  191.7 6.3 %shard_map.99 = bf16[4,128,512]{2,1,0:T(8,128)(2,1)} custom-call(s32[1]{0:T(128)} %bitcast.z_ref, bf16[16,72,2048]{2,1,0:T(8,128)(2,1)} %all-to-all-done.1.r_ref, f32[128,16]{1,0:T(8,128)} %copy.33.w_ref, bf16[192,4096]{1,0:T(8,128)(2,1)} %get-tuple-element.26.after_ref), custom_call_target="tpu_custom_call" | custom-call | flops 89999998976 | bytes 5300000 | tf_op jit(solution)/shard_map/pallas_call | solution.py:280
  198.0 7.0 %reduce-scatter.2.cloned.1.call-done = bf16[1,1152,512]{2,1,0:T(8,128)(2,1)} async-done(((bf16[4,1152,512]{2,1,0:T(8,128)(2,1)}), bf16[1,1152,512]{2,1,0:T(8,128)(2,1)}) %reduce-scatter.2.cloned.1.call-update) | async-done | bytes 1179664 | tf_op jit(solution)/shard_map/reduce_scatter | solution.py:345
  205.0 7.3 %all-to-all-start.3 = ((bf16[16,72,512]{2,1,0:T(8,128)(2,1)}), bf16[16,72,512]{2,1,0:T(8,128)(2,1)S(1)}, u32[]{:S(2)}, u32[]{:S(2)}) async-start(bf16[16,72,512]{2,1,0:T(8,128)(2,1)} %bitcast.39), calls=%async_computation.4 | async-start | bytes 2359296 | tf_op jit(solution)/shard_map/all_to_all | solution.py:299
  212.3 1.1 slice_bitcast_fusion.2
  213.3 0.2 collective-permute-start.4
  213.6 2.1 collective-permute-start.5
  215.6 1.9 collective-permute-start.6
  217.5 4.7 %collective-permute-done.4 = bf16[128,512]{1,0:T(8,128)(2,1)S(1)} collective-permute-done((bf16[128,512]{1,0:T(8,128)(2,1)S(1)}, bf16[128,512]{1,0:T(8,128)(2,1)S(1)}, u32[]{:S(2)}, u32[]{:S(2)}) %collective-permute-start.4) | collective-permute-done | bytes 131104 | tf_op jit(solution)/shard_map/ppermute | solution.py:307
  222.2 0.0 collective-permute-done.5
  222.2 0.6 collective-permute-done.6
  222.7 1.6 fusion.4
  224.4 5.2 %all-to-all-done.3.r_ref = bf16[16,72,512]{2,1,0:T(8,128)(2,1)S(1)} async-done(((bf16[16,72,512]{2,1,0:T(8,128)(2,1)}), bf16[16,72,512]{2,1,0:T(8,128)(2,1)S(1)}, u32[]{:S(2)}, u32[]{:S(2)}) %all-to-all-start.3) | async-done | bytes 1179680 | tf_op jit(solution)/shard_map/all_to_all | solution.py:299
  229.5 0.0 copy-start.3
  229.5 1.0 copy-done.3
  230.6 2.8 %shard_map.101 = bf16[128,512]{1,0:T(8,128)(2,1)} custom-call(bf16[16,72,512]{2,1,0:T(8,128)(2,1)} %copy-done.3, f32[128,16]{1,0:T(8,128)} %copy.33.w_ref), custom_call_target="tpu_custom_call" | custom-call | flops 200000000 | bytes 1400000 | tf_op jit(solution)/shard_map/pallas_call | solution.py:270
  233.4 0.0 copy-done.1
  (1 shorter events, 0.0 us)
Async XLA Ops:
  7.2 3.1 %copy-start = (bf16[128,4096]{1,0:T(8,128)(2,1)S(1)}, bf16[128,4096]{1,0:T(8,128)(2,1)}, u32[]{:S(2)}) copy-start(bf16[128,4096]{1,0:T(8,128)(2,1)} %param.6) | copy-start | bytes 3145732
  7.2 118.4 %all-gather.2.cloned.1.call-start = ((), (), s32[]{:S(2)}) async-start(), calls=%async_computation.5 | async-start | bytes 16908288 | tf_op jit(solution)/shard_map/all_gather | solution.py:318
  85.5 4.6 %copy-start.2 = (bf16[16,72,2048]{2,1,0:T(8,128)(2,1)}, bf16[16,72,2048]{2,1,0:T(8,128)(2,1)S(1)}, u32[]{:S(2)}) copy-start(bf16[16,72,2048]{2,1,0:T(8,128)(2,1)S(1)} %all_to_all.24) | copy-start | bytes 14155780
  85.5 8.0 %collective-permute-start = (bf16[1152,2048]{1,0:T(8,128)(2,1)S(1)}, bf16[1152,2048]{1,0:T(8,128)(2,1)}, u32[]{:S(2)}, u32[]{:S(2)}) collective-permute-start(bf16[1152,2048]{1,0:T(8,128)(2,1)S(1)} %bitcast.33), channel_id=1, source_target_pairs={{0,1},{1,0},{2,3},{3,2},{4,5},{5,4},{6,7},{7,6},{8,9},{9,8},{10,11... | collective-permute-start | bytes 14155784 | tf_op jit(solution)/shard_map/ppermute | solution.py:303
  90.1 18.4 %collective-permute-start.2 = (bf16[3,192,2048]{2,1,0:T(8,128)(2,1)}, bf16[3,192,2048]{2,1,0:T(8,128)(2,1)S(1)}, u32[]{:S(2)}, u32[]{:S(2)}) collective-permute-start(bf16[3,192,2048]{2,1,0:T(8,128)(2,1)} %shard_map.95), channel_id=1, source_target_pairs={{0,1},{1,0},{2,3},{3,2},{4,5},{5,4},{6,7},{7,6},{8,9},{9,8},{10,11... | collective-permute-start | bytes 7077896 | tf_op jit(solution)/shard_map/ppermute | solution.py:303
  103.5 4.9 %collective-permute-start.1 = (bf16[1152,256]{1,0:T(8,128)(2,1)}, bf16[1152,256]{1,0:T(8,128)(2,1)S(1)}, u32[]{:S(2)}, u32[]{:S(2)}) collective-permute-start(bf16[1152,256]{1,0:T(8,128)(2,1)} %get-tuple-element.18.own_ref.hid_ref), channel_id=1, source_target_pairs={{0,1},{1,0},{2,3},{3,2},{4,5},{5,4},{6,7},{7,6},{8,9},{9,8},{10,11... | collective-permute-start | bytes 1769480 | tf_op jit(solution)/shard_map/ppermute | solution.py:303
  103.9 13.7 %all-to-all-start.2 = ((f32[16,1,128]{2,1,0:T(1,128)}), f32[16,1,128]{2,1,0:T(1,128)S(1)}, u32[]{:S(2)}, u32[]{:S(2)}) async-start(f32[16,1,128]{2,1,0:T(1,128)} %bitcast.8), calls=%async_computation.2 | async-start | bytes 16384 | tf_op jit(solution)/shard_map/all_to_all | solution.py:299
  108.5 1.4 copy-start.4
  109.9 0.8 copy-start.5
  117.5 7.3 %copy-start.6 = (f32[16,1,128]{2,1,0:T(1,128)}, f32[16,1,128]{2,1,0:T(1,128)S(1)}, u32[]{:S(2)}) copy-start(f32[16,1,128]{2,1,0:T(1,128)S(1)} %all-to-all-done.2) | copy-start | bytes 24580
  117.5 74.2 %all-to-all-start.1 = ((bf16[16,72,2048]{2,1,0:T(8,128)(2,1)}), bf16[16,72,2048]{2,1,0:T(8,128)(2,1)}, u32[]{:S(2)}, u32[]{:S(2)}) async-start(bf16[16,72,2048]{2,1,0:T(8,128)(2,1)} %bitcast.29), calls=%async_computation.1 | async-start | bytes 9437184 | tf_op jit(solution)/shard_map/all_to_all | solution.py:299
  124.8 80.2 %reduce-scatter.2.cloned.1.call-start = ((), (), s32[]{:S(2)}) async-start(), calls=%async_computation.6 | async-start | bytes 5898240 | tf_op jit(solution)/shard_map/reduce_scatter | solution.py:345
  137.5 3.1 %collective-permute-start.3 = (bf16[2,1152,256]{2,1,0:T(8,128)(2,1)}, bf16[2,1152,256]{2,1,0:T(8,128)(2,1)S(1)}, u32[]{:S(2)}, u32[]{:S(2)}) collective-permute-start(bf16[2,1152,256]{2,1,0:T(8,128)(2,1)} %get-tuple-element.25.dgu_ref.own_ref), channel_id=1, source_target_pairs={{0,1},{1,0},{2,3},{3,2},{4,5},{5,4},{6,7},{7,6},{8,9},{9,8},{10,11... | collective-permute-start | bytes 3538952 | tf_op jit(solution)/shard_map/ppermute | solution.py:303
  140.6 1.0 copy-start.7
  191.7 41.7 %copy-start.1 = (bf16[128,4096]{1,0:T(8,128)(2,1)S(1)}, bf16[128,4096]{1,0:T(8,128)(2,1)}, u32[]{:S(2)}) copy-start(bf16[128,4096]{1,0:T(8,128)(2,1)} %param.6) | copy-start | bytes 3145732
  205.0 24.5 %all-to-all-start.3 = ((bf16[16,72,512]{2,1,0:T(8,128)(2,1)}), bf16[16,72,512]{2,1,0:T(8,128)(2,1)S(1)}, u32[]{:S(2)}, u32[]{:S(2)}) async-start(bf16[16,72,512]{2,1,0:T(8,128)(2,1)} %bitcast.39), calls=%async_computation.4 | async-start | bytes 2359296 | tf_op jit(solution)/shard_map/all_to_all | solution.py:299
  213.3 8.8 %collective-permute-start.4 = (bf16[128,512]{1,0:T(8,128)(2,1)S(1)}, bf16[128,512]{1,0:T(8,128)(2,1)S(1)}, u32[]{:S(2)}, u32[]{:S(2)}) collective-permute-start(bf16[128,512]{1,0:T(8,128)(2,1)S(1)} %get-tuple-element.30), channel_id=1, source_target_pairs={{0,2},{1,3},{2,4},{3,5},{4,6},{5,7},{6,0},{7,1},{8,10},{9,11},{10,... | collective-permute-start | bytes 393224 | tf_op jit(solution)/shard_map/ppermute | solution.py:307
  213.6 8.6 %collective-permute-start.5 = (bf16[128,512]{1,0:T(8,128)(2,1)S(1)}, bf16[128,512]{1,0:T(8,128)(2,1)S(1)}, u32[]{:S(2)}, u32[]{:S(2)}) collective-permute-start(bf16[128,512]{1,0:T(8,128)(2,1)S(1)} %get-tuple-element.32), channel_id=1, source_target_pairs={{0,4},{1,5},{2,6},{3,7},{4,0},{5,1},{6,2},{7,3},{8,12},{9,13},{10,... | collective-permute-start | bytes 393224 | tf_op jit(solution)/shard_map/ppermute | solution.py:307
  215.6 7.1 %collective-permute-start.6 = (bf16[128,512]{1,0:T(8,128)(2,1)S(1)}, bf16[128,512]{1,0:T(8,128)(2,1)S(1)}, u32[]{:S(2)}, u32[]{:S(2)}) collective-permute-start(bf16[128,512]{1,0:T(8,128)(2,1)S(1)} %get-tuple-element.31), channel_id=1, source_target_pairs={{0,6},{1,7},{2,0},{3,1},{4,2},{5,3},{6,4},{7,5},{8,14},{9,15},{10,... | collective-permute-start | bytes 393224 | tf_op jit(solution)/shard_map/ppermute | solution.py:307
  229.5 1.0 copy-start.3
Sparse Core Ops, SparseCore 0:
  11.7 109.4 all-gather.1
  151.0 53.9 reduce-scatter.1

commit v8 on v7

--- a/solution.py
+++ b/solution.py
@@ -91,7 +91,7 @@
     dgu_ref[1, :, :UNITS] = (dhid * gate * sig).astype(BF16)
 
 
-def weight_grad_kernel(core_ref, own_ref, other_ref, cot_ref, dgu_ref, hid_ref, gu_ref, down_ref):
+def weight_grad_kernel(core_ref, after_ref, own_ref, other_ref, cot_ref, dgu_ref, hid_ref, gu_ref, down_ref):
     down_ref[...] = tn(hid_ref[:, :UNITS], cot_ref[...]).astype(BF16)
     owned = pl.program_id(0) // DEPTH == core_ref[0]
 
@@ -233,7 +233,7 @@
         ],
         [by_rows(ROWS, D), by_rows(2, ROWS, WIDE)],
         [shaped(ALL_ROWS, D), shaped(2, ALL_ROWS, WIDE)],
-        4_000_000_000, 30_000_000,
+        1_000_000, 100_000,
     )(grad_rows, row_of, weight, gate, up, wd)
 
 
@@ -241,17 +241,18 @@
     return stepped(
         back_kernel, 1, STEPS,
         [by_rows(2, ROWS, WIDE), by_rows(2, ROWS, WIDE), whole(wgu.shape), whole((2, UNITS, HALF))],
-        by_rows(DEPTH, ROWS, SHARE), shaped(DEPTH, ALL_ROWS, SHARE), 4_000_000_000, 10_000_000,
+        by_rows(DEPTH, ROWS, SHARE), shaped(DEPTH, ALL_ROWS, SHARE), 1_000_000, 100_000,
     )(core, own, other, wgu, lent)
 
 
-def weight_grads(core, own, other, cot, dgu, hidden):
+def weight_grads(core, after, own, other, cot, dgu, hidden):
     def block(first):
         return lambda i, c: (0, jnp.clip(i - DEPTH * (c[0] if first else 1 - c[0]), 0, DEPTH - 1))
 
     return stepped(
         weight_grad_kernel, 1, TENSOR,
         [
+            pl.BlockSpec(memory_space=pl.ANY),
             pl.BlockSpec((ALL_ROWS, SHARE), block(True)),
             pl.BlockSpec((ALL_ROWS, SHARE), block(False)),
             pl.BlockSpec((ALL_ROWS, SHARE), lambda i, c: (0, i)),
@@ -263,7 +264,7 @@
             pl.BlockSpec((UNITS, SHARE), lambda i, c: (0, i)),
         ],
         [shaped(2, UNITS, D), shaped(UNITS, D)], 6_000_000_000, 25_000_000,
-    )(core, own, other, cot, dgu, hidden)
+    )(core, after, own, other, cot, dgu, hidden)
 
 
 def combine(returned, own_weight):
@@ -307,6 +308,26 @@
     return lax.ppermute(x, "tensor", [(t, (t + 2 * d) % TENSOR) for t in range(TENSOR)])
 
 
+def ring_over_levels(x, level):
+    half = ALL_ROWS // 2
+
+    def block(d):
+        return lax.dynamic_index_in_dim(x, (level + d) % DEPTH, 0, keepdims=False)
+
+    def add(*terms):
+        return sum(t.astype(F32) for t in terms).astype(BF16)
+
+    far, above, below, own = block(2), block(1), block(3), block(0)
+    far_up, far_down = up_levels(far[:half], 1), up_levels(far[half:], -1)
+    far_up, far_down, above, below = lax.optimization_barrier((far_up, far_down, above, below))
+    from_below, from_above = up_levels(above[half:], 1), up_levels(below[:half], -1)
+    through_up = up_levels(add(above[:half], far_up), 1)
+    through_down = up_levels(add(below[half:], far_down), -1)
+    return jnp.concatenate(
+        [add(own[:half], through_up, from_above), add(own[half:], from_below, through_down)], axis=0
+    )
+
+
 def on_device(tokens, expert_ids, gate_probs, grad_out, gate_up, down_proj):
     part = TOK // TENSOR
     member = lax.axis_index("tensor")
@@ -342,13 +363,10 @@
 
     cot, dgu = unit_grads(grad_rows, row_of, weight, gate, up, wd)
     pair_back = back_rows(core_list, dgu, swap_cores(dgu), wgu, lent)
-    back_sum = lax.psum_scatter(
-        pair_back, "tensor", scatter_dimension=0, tiled=False,
-        axis_index_groups=[[2 * z + c for z in range(DEPTH)] for c in range(2)],
-    )
-    grad_gate_up, grad_down = weight_grads(core_list, own_rows, other_rows, cot, dgu, hidden)
-    parts = depth_parts(level_list, out_back, own_weight, grad_down)
-    parts, back_sum = lax.optimization_barrier((parts, back_sum))
+    grad_gate_up, grad_down = weight_grads(core_list, pair_back, own_rows, other_rows, cot, dgu, hidden)
+    back_sum = ring_over_levels(pair_back, level)
+    back_sum, grad_down = lax.optimization_barrier((back_sum, grad_down))
+    parts = depth_parts(level_list, out_back, own_weight, back_sum)
     grad_back = over_experts(back_sum.reshape(GROUPS, CAP, SHARE))
     mixed = parts[0].astype(F32)
     for d in range(1, DEPTH):

time: 243 us -> 245 us (level)
  waiting for transfers between devices: 48.2 us -> 32.2 us
  starting transfers between devices: 23.7 us -> 33.8 us
  local copies, waits for them, and re-layouts: 9.24 us -> 14.2 us
  other arithmetic: 2.95 us -> 7.72 us
    all_to_all x3, waiting for transfers between devices: 29.4 us -> 0.01 us  [over_experts(): return lax.all_to_all(x, 'expert', split_axis=0, concat_axis=0, tiled=True)]
    ppermute x3 -> x9, waiting for transfers between devices: 5.25 us -> 25.8 us  [up_levels(): lax.ppermute(x, 'tensor', [(t, (t + 2 * d) % TENSOR) for t in range(TENSO...]
    ppermute x3 -> x9, starting transfers between devices: 4.16 us -> 14.3 us  [up_levels(): lax.ppermute(x, 'tensor', [(t, (t + 2 * d) % TENSOR) for t in range(TENSO...]
    reduce_scatter x1 -> x0, waiting for transfers between devices: 7.01 us -> none  [on_device(): lax.psum_scatter(pair_back, 'tensor', scatter_dimension=0, tiled=False, a...]
    convert_element_type x0 -> x3, other arithmetic: none -> 3.66 us  [add(): return sum((t.astype(F32) for t in terms)).astype(BF16)]
    slice x0 -> x3, local copies, waits for them, and re-layouts: none -> 3.06 us  [the longest x1 1.32 us: ring_over_levels(): far_up, far_down = (up_levels(far[:half], 1), up_levels(far[half:], -1))]
  transfers between devices with their start and end apart: 12 -> 17, of which waited for: 7 -> 7; matrix products, arithmetic and copies ran while one was open for 3% -> 7% of each run, Pallas kernels for 29% -> 28%
where the time goes in v8:
time: 245 us; the launch traced here: 244 us
  Pallas kernels  71.5 us (29%)
  blocking collectives  69.5 us (28%)
  starting transfers between devices  33.8 us (14%)
  waiting for transfers between devices  32.2 us (13%)
  local copies, waits for them, and re-layouts  14.2 us (6%)
  between operations  14.2 us (6%)
  other arithmetic  7.72 us (3%)
    all_to_all x1, blocking collectives, over_experts(): return lax.all_to_all(x, 'expert', split_axis=0, concat_axis=0, tiled=True)  69.5 us
    ppermute x9, waiting for transfers between devices, up_levels(): lax.ppermute(x, 'tensor', [(t, (t + 2 * d) % TENSOR) for t in range(TENSO...  25.8 us
    all_to_all x3, starting transfers between devices, over_experts(): return lax.all_to_all(x, 'expert', split_axis=0, concat_axis=0, tiled=True)  19.2 us
    pallas_call x1, Pallas kernels, weight_grads(): stepped(weight_grad_kernel, 1, TENSOR, [pl.BlockSpec(memory_space=pl.ANY)...  15 us
    ppermute x9, starting transfers between devices, up_levels(): lax.ppermute(x, 'tensor', [(t, (t + 2 * d) % TENSOR) for t in range(TENSO...  14.3 us
    pallas_call x1, Pallas kernels, unit_grads(): stepped(unit_grad_kernel, 0, STEPS, [by_rows(STEP_GROUPS * TOK, D), ROW_S...  11.9 us
    pallas_call x1, Pallas kernels, hidden_units(): stepped(hidden_kernel, 1, STEPS, [by_rows(ROWS, HALF), by_rows(ROWS, HALF...  10.1 us
    pallas_call x1, Pallas kernels, back_rows(): stepped(back_kernel, 1, STEPS, [by_rows(2, ROWS, WIDE), by_rows(2, ROWS,...  9.28 us
  transfers between devices with their start and end apart: 17, of which 7 were waited for; matrix products, arithmetic and copies ran while one was open for 7% of the time, Pallas kernels for 28%

profile of v8, /device:TPU:2, one launch (start us, length us, event | category | flops | bytes accessed | tf_op | source)
XLA Modules:
  0.0 243.9 jit_solution(16687327035342257411)
XLA Ops:
  7.2 0.0 copy-start
  7.2 0.0 all-gather.2.cloned.1.call-start
  7.2 1.6 constant_dynamic-slice_fusion
  8.9 0.0 all-gather.2.cloned.1.call-update
  8.9 1.3 select_reduce_fusion
  10.2 0.8 constant_dynamic-slice_fusion.1.x_ref
  11.1 4.8 %shard_map.93.after_ref = bf16[16,72,2048]{2,1,0:T(8,128)(2,1)} custom-call(bf16[128,2048]{1,0:T(8,128)(2,1)} %constant_dynamic-slice_fusion.1.x_ref, f32[16,128]{1,0:T(8,128)} %bitcast.2.w_ref), custom_call_target="tpu_custom_call" | custom-call | flops 600000000 | bytes 5300000 | tf_op jit(solution)/shard_map/pallas_call | solution.py:182
  15.9 69.5 %all_to_all.24 = bf16[16,72,2048]{2,1,0:T(8,128)(2,1)S(1)} all-to-all(bf16[16,72,2048]{2,1,0:T(8,128)(2,1)} %shard_map.93.after_ref), channel_id=1, replica_groups=mesh['expert'=16,'tensor'=8] {'expert'}, dimensions={0} | all-to-all | bytes 9437184 | tf_op jit(solution)/shard_map/all_to_all | solution.py:300
  85.5 0.0 collective-permute-start
  85.5 4.6 %shard_map.95 = bf16[3,192,2048]{2,1,0:T(8,128)(2,1)} custom-call(s32[1]{0:T(128)S(6)} %sub.8.core_ref, bf16[16,72,2048]{2,1,0:T(8,128)(2,1)} %shard_map.93.after_ref, bf16[2,192,4096]{2,1,0:T(8,128)(2,1)} %bitcast.55, bf16[192,4096]{1,0:T(8,128)(2,1)} %bitcast.52), custom_call_target="tpu_custom_call" | custom-call | bytes 4700000 | tf_op jit(solution)/shard_map/pallas_call | solution.py:191
  90.1 0.0 collective-permute-start.2
  90.1 3.4 %collective-permute-done.other_ref = bf16[1152,2048]{1,0:T(8,128)(2,1)} collective-permute-done((bf16[1152,2048]{1,0:T(8,128)(2,1)S(1)}, bf16[1152,2048]{1,0:T(8,128)(2,1)}, u32[]{:S(2)}, u32[]{:S(2)}) %collective-permute-start) | collective-permute-done | bytes 4718624 | tf_op jit(solution)/shard_map/ppermute | solution.py:304
  93.5 10.1 %shard_map.94 = (f32[1152,192]{1,0:T(8,128)}, f32[1152,192]{1,0:T(8,128)}, bf16[1152,256]{1,0:T(8,128)(2,1)}) custom-call(s32[1]{0:T(128)} %bitcast.1.core_ref, bf16[1152,2048]{1,0:T(8,128)(2,1)} %bitcast.50, bf16[1152,2048]{1,0:T(8,128)(2,1)} %collective-permute-done.other_ref, bf16[2,192,4096]{2,1,0:T(8,128)(2,1)} %bitcast.56), custom_call_target="tpu_custom_call" | custom-call | flops 4000000000 | bytes 15000000 | tf_op jit(solution)/shard_map/pallas_call | solution.py:204
  103.6 0.3 collective-permute-start.1
  103.9 4.6 %all-to-all-start.2 = ((f32[16,1,128]{2,1,0:T(1,128)}), f32[16,1,128]{2,1,0:T(1,128)S(1)}, u32[]{:S(2)}, u32[]{:S(2)}) async-start(f32[16,1,128]{2,1,0:T(1,128)} %bitcast.8), calls=%async_computation.2 | async-start | bytes 16384 | tf_op jit(solution)/shard_map/all_to_all | solution.py:300
  108.5 0.0 collective-permute-done.2.lent_ref
  108.5 0.0 copy-start.3
  108.5 0.0 collective-permute-done.1.other_ref
  108.5 1.4 copy-done.3
  109.9 0.8 copy-done.6
  110.7 6.8 %shard_map.96 = bf16[1152,2048]{1,0:T(8,128)(2,1)} custom-call(s32[1]{0:T(128)} %bitcast.1.core_ref, bf16[1152,256]{1,0:T(8,128)(2,1)} %get-tuple-element.22.own_ref.hid_ref, bf16[1152,256]{1,0:T(8,128)(2,1)} %copy-done.6, bf16[192,4096]{1,0:T(8,128)(2,1)} %bitcast.53, bf16[3,192,2048]{2,1,0:T(8,128)(2,1)} %copy-done.3), custom_call_target="tpu_custom_call" | custom-call | flops 2000000000 | bytes 8000000 | tf_op jit(solution)/shard_map/pallas_call | solution.py:217
  117.5 0.0 all-to-all-done.2
  117.5 7.3 %all-to-all-start.1 = ((bf16[16,72,2048]{2,1,0:T(8,128)(2,1)}), bf16[16,72,2048]{2,1,0:T(8,128)(2,1)}, u32[]{:S(2)}, u32[]{:S(2)}) async-start(bf16[16,72,2048]{2,1,0:T(8,128)(2,1)} %bitcast.48), calls=%async_computation.1 | async-start | bytes 9437184 | tf_op jit(solution)/shard_map/all_to_all | solution.py:300
  124.8 0.7 fusion.5
  125.5 11.9 %shard_map.97 = (bf16[1152,4096]{1,0:T(8,128)(2,1)}, bf16[2,1152,256]{2,1,0:T(8,128)(2,1)}) custom-call(bf16[2048,4096]{1,0:T(8,128)(2,1)} %all-gather.2.cloned.1.call-done.g_ref, s32[8,1,256]{2,1,0:T(1,128)} %bitcast.60, f32[8,1,256]{2,1,0:T(1,128)} %bitcast.59, f32[1152,192]{1,0:T(8,128)} %get-tuple-element.26.gate_ref, ...), custom_call_target="tpu_custom_call" | custom-call | flops 1000000 | bytes 100000 | tf_op jit(solution)/shard_map/pallas_call | solution.py:228
  137.4 0.0 collective-permute-start.3
  137.5 3.0 %collective-permute-done.3.other_ref = bf16[2,1152,256]{2,1,0:T(8,128)(2,1)S(1)} collective-permute-done((bf16[2,1152,256]{2,1,0:T(8,128)(2,1)}, bf16[2,1152,256]{2,1,0:T(8,128)(2,1)S(1)}, u32[]{:S(2)}, u32[]{:S(2)}) %collective-permute-start.3) | collective-permute-done | bytes 1179680 | tf_op jit(solution)/shard_map/ppermute | solution.py:304
  140.5 1.0 copy-done.5
  141.5 9.3 %shard_map.98.after_ref = bf16[4,1152,512]{2,1,0:T(8,128)(2,1)} custom-call(s32[1]{0:T(128)} %bitcast.1.core_ref, bf16[2,1152,256]{2,1,0:T(8,128)(2,1)} %get-tuple-element.28.own_ref.dgu_ref, bf16[2,1152,256]{2,1,0:T(8,128)(2,1)} %copy-done.5, bf16[2,192,4096]{2,1,0:T(8,128)(2,1)} %bitcast.57, bf16[3,192,2048]{2,1,0:T(8,128)(2,1)} %copy-done.3), custom_call_target="tpu_custom_call" | custom-call | flops 1000000 | bytes 100000 | tf_op jit(solution)/shard_map/pallas_call | solution.py:241
  150.8 1.3 dynamic-slice_bitcast_fusion.3
  152.1 1.8 collective-permute-start.4
  154.0 2.9 %collective-permute-start.5 = (bf16[576,512]{1,0:T(8,128)(2,1)S(1)}, bf16[576,512]{1,0:T(8,128)(2,1)S(1)}, u32[]{:S(2)}, u32[]{:S(2)}) collective-permute-start(bf16[576,512]{1,0:T(8,128)(2,1)S(1)} %get-tuple-element.42), channel_id=1, source_target_pairs={{0,6},{1,7},{2,0},{3,1},{4,2},{5,3},{6,4},{7,5},{8,14},{9,15},{10,... | collective-permute-start | bytes 1769480 | tf_op jit(solution)/shard_map/ppermute | solution.py:308
  156.9 1.8 dynamic-slice_bitcast_fusion
  158.6 11.8 %collective-permute-done.4 = bf16[576,512]{1,0:T(8,128)(2,1)S(1)} collective-permute-done((bf16[576,512]{1,0:T(8,128)(2,1)S(1)}, bf16[576,512]{1,0:T(8,128)(2,1)S(1)}, u32[]{:S(2)}, u32[]{:S(2)}) %collective-permute-start.4) | collective-permute-done | bytes 589856 | tf_op jit(solution)/shard_map/ppermute | solution.py:308
  170.5 0.0 collective-permute-done.5
  170.5 0.9 slice.50
  171.3 1.0 add_convert_fusion
  172.3 3.0 %collective-permute-start.9 = (bf16[576,512]{1,0:T(8,128)(2,1)}, bf16[576,512]{1,0:T(8,128)(2,1)S(1)}, u32[]{:S(2)}, u32[]{:S(2)}) collective-permute-start(bf16[576,512]{1,0:T(8,128)(2,1)} %add_convert_fusion), channel_id=1, source_target_pairs={{0,6},{1,7},{2,0},{3,1},{4,2},{5,3},{6,4},{7,5},{8,14},{9,15},{10,... | collective-permute-start | bytes 1769480 | tf_op jit(solution)/shard_map/ppermute | solution.py:308
  175.3 0.9 slice.52
  176.2 1.0 add_convert_fusion.1
  177.2 0.0 collective-permute-start.6
  177.2 3.2 %collective-permute-start.7 = (bf16[576,512]{1,0:T(8,128)(2,1)}, bf16[576,512]{1,0:T(8,128)(2,1)S(1)}, u32[]{:S(2)}, u32[]{:S(2)}) collective-permute-start(bf16[576,512]{1,0:T(8,128)(2,1)} %slice.50), channel_id=1, source_target_pairs={{0,6},{1,7},{2,0},{3,1},{4,2},{5,3},{6,4},{7,5},{8,14},{9,15},{10,... | collective-permute-start | bytes 1769480 | tf_op jit(solution)/shard_map/ppermute | solution.py:308
  180.4 0.0 collective-permute-start.8
  180.4 1.4 copy.33.w_ref
  181.8 15.0 %shard_map.99 = (bf16[2,192,4096]{2,1,0:T(8,128)(2,1)}, bf16[192,4096]{1,0:T(8,128)(2,1)}) custom-call(s32[1]{0:T(128)} %bitcast.1.core_ref, bf16[4,1152,512]{2,1,0:T(8,128)(2,1)} %shard_map.98.after_ref, bf16[1152,2048]{1,0:T(8,128)(2,1)} %bitcast.51, bf16[1152,2048]{1,0:T(8,128)(2,1)} %collective-permute-done.other_ref, ...), custom_call_target="tpu_custom_call" | custom-call | flops 6000000000 | bytes 25000000 | tf_op jit(solution)/shard_map/pallas_call | solution.py:252
  196.8 0.0 collective-permute-done.9
  196.8 0.0 collective-permute-done.6
  196.8 3.6 %collective-permute-done.7 = bf16[576,512]{1,0:T(8,128)(2,1)S(1)} collective-permute-done((bf16[576,512]{1,0:T(8,128)(2,1)}, bf16[576,512]{1,0:T(8,128)(2,1)S(1)}, u32[]{:S(2)}, u32[]{:S(2)}) %collective-permute-start.7) | collective-permute-done | bytes 589856 | tf_op jit(solution)/shard_map/ppermute | solution.py:308
  200.4 5.1 %collective-permute-done.8 = bf16[576,512]{1,0:T(8,128)(2,1)S(1)} collective-permute-done((bf16[576,512]{1,0:T(8,128)(2,1)}, bf16[576,512]{1,0:T(8,128)(2,1)S(1)}, u32[]{:S(2)}, u32[]{:S(2)}) %collective-permute-start.8) | collective-permute-done | bytes 589856 | tf_op jit(solution)/shard_map/ppermute | solution.py:308
  205.6 1.7 fusion.3
  207.3 1.1 pad_maximum_fusion.after_ref
  208.4 0.0 all-to-all-done.1.r_ref
  208.4 7.3 %all-to-all-start.3 = ((bf16[16,72,512]{2,1,0:T(8,128)(2,1)}), bf16[16,72,512]{2,1,0:T(8,128)(2,1)S(1)}, u32[]{:S(2)}, u32[]{:S(2)}) async-start(bf16[16,72,512]{2,1,0:T(8,128)(2,1)} %bitcast.23), calls=%async_computation.3 | async-start | bytes 2359296 | tf_op jit(solution)/shard_map/all_to_all | solution.py:300
  215.7 6.2 %shard_map.100 = bf16[4,128,512]{2,1,0:T(8,128)(2,1)} custom-call(s32[1]{0:T(128)} %bitcast.z_ref, bf16[16,72,2048]{2,1,0:T(8,128)(2,1)} %all-to-all-done.1.r_ref, f32[128,16]{1,0:T(8,128)} %copy.33.w_ref, bf16[1152,512]{1,0:T(8,128)(2,1)} %pad_maximum_fusion.after_ref), custom_call_target="tpu_custom_call" | custom-call | flops 89999998976 | bytes 5300000 | tf_op jit(solution)/shard_map/pallas_call | solution.py:281
  221.9 1.1 slice_bitcast_fusion.2
  223.0 0.1 collective-permute-start.10
  223.1 1.1 collective-permute-start.11
  224.2 2.1 collective-permute-start.12
  226.3 4.3 %collective-permute-done.10 = bf16[128,512]{1,0:T(8,128)(2,1)S(1)} collective-permute-done((bf16[128,512]{1,0:T(8,128)(2,1)S(1)}, bf16[128,512]{1,0:T(8,128)(2,1)S(1)}, u32[]{:S(2)}, u32[]{:S(2)}) %collective-permute-start.10) | collective-permute-done | bytes 131104 | tf_op jit(solution)/shard_map/ppermute | solution.py:308
  230.7 0.0 collective-permute-done.11
  230.7 0.9 collective-permute-done.12
  231.6 1.6 fusion.8
  233.2 1.0 copy-done.4
  234.2 2.8 %shard_map.101 = bf16[128,512]{1,0:T(8,128)(2,1)} custom-call(bf16[16,72,512]{2,1,0:T(8,128)(2,1)} %copy-done.4, f32[128,16]{1,0:T(8,128)} %copy.33.w_ref), custom_call_target="tpu_custom_call" | custom-call | flops 200000000 | bytes 1400000 | tf_op jit(solution)/shard_map/pallas_call | solution.py:271
  (13 shorter events, 0.0 us)
Async XLA Ops:
  7.2 3.1 %copy-start = (bf16[128,4096]{1,0:T(8,128)(2,1)S(1)}, bf16[128,4096]{1,0:T(8,128)(2,1)}, u32[]{:S(2)}) copy-start(bf16[128,4096]{1,0:T(8,128)(2,1)} %param.6) | copy-start | bytes 3145732
  7.2 118.3 %all-gather.2.cloned.1.call-start = ((), (), s32[]{:S(2)}) async-start(), calls=%async_computation.4 | async-start | bytes 16908288 | tf_op jit(solution)/shard_map/all_gather | solution.py:339
  85.4 4.6 %copy-start.2 = (bf16[16,72,2048]{2,1,0:T(8,128)(2,1)}, bf16[16,72,2048]{2,1,0:T(8,128)(2,1)S(1)}, u32[]{:S(2)}) copy-start(bf16[16,72,2048]{2,1,0:T(8,128)(2,1)S(1)} %all_to_all.24) | copy-start | bytes 14155780
  85.5 8.0 %collective-permute-start = (bf16[1152,2048]{1,0:T(8,128)(2,1)S(1)}, bf16[1152,2048]{1,0:T(8,128)(2,1)}, u32[]{:S(2)}, u32[]{:S(2)}) collective-permute-start(bf16[1152,2048]{1,0:T(8,128)(2,1)S(1)} %bitcast.49), channel_id=1, source_target_pairs={{0,1},{1,0},{2,3},{3,2},{4,5},{5,4},{6,7},{7,6},{8,9},{9,8},{10,11... | collective-permute-start | bytes 14155784 | tf_op jit(solution)/shard_map/ppermute | solution.py:304
  90.1 18.4 %collective-permute-start.2 = (bf16[3,192,2048]{2,1,0:T(8,128)(2,1)}, bf16[3,192,2048]{2,1,0:T(8,128)(2,1)S(1)}, u32[]{:S(2)}, u32[]{:S(2)}) collective-permute-start(bf16[3,192,2048]{2,1,0:T(8,128)(2,1)} %shard_map.95), channel_id=1, source_target_pairs={{0,1},{1,0},{2,3},{3,2},{4,5},{5,4},{6,7},{7,6},{8,9},{9,8},{10,11... | collective-permute-start | bytes 7077896 | tf_op jit(solution)/shard_map/ppermute | solution.py:304
  103.6 4.9 %collective-permute-start.1 = (bf16[1152,256]{1,0:T(8,128)(2,1)}, bf16[1152,256]{1,0:T(8,128)(2,1)S(1)}, u32[]{:S(2)}, u32[]{:S(2)}) collective-permute-start(bf16[1152,256]{1,0:T(8,128)(2,1)} %get-tuple-element.22.own_ref.hid_ref), channel_id=1, source_target_pairs={{0,1},{1,0},{2,3},{3,2},{4,5},{5,4},{6,7},{7,6},{8,9},{9,8},{10,11... | collective-permute-start | bytes 1769480 | tf_op jit(solution)/shard_map/ppermute | solution.py:304
  103.9 13.6 %all-to-all-start.2 = ((f32[16,1,128]{2,1,0:T(1,128)}), f32[16,1,128]{2,1,0:T(1,128)S(1)}, u32[]{:S(2)}, u32[]{:S(2)}) async-start(f32[16,1,128]{2,1,0:T(1,128)} %bitcast.8), calls=%async_computation.2 | async-start | bytes 16384 | tf_op jit(solution)/shard_map/all_to_all | solution.py:300
  108.5 1.4 copy-start.3
  109.9 0.8 copy-start.6
  117.5 7.3 %copy-start.7 = (f32[16,1,128]{2,1,0:T(1,128)}, f32[16,1,128]{2,1,0:T(1,128)S(1)}, u32[]{:S(2)}) copy-start(f32[16,1,128]{2,1,0:T(1,128)S(1)} %all-to-all-done.2) | copy-start | bytes 24580
  117.5 90.9 %all-to-all-start.1 = ((bf16[16,72,2048]{2,1,0:T(8,128)(2,1)}), bf16[16,72,2048]{2,1,0:T(8,128)(2,1)}, u32[]{:S(2)}, u32[]{:S(2)}) async-start(bf16[16,72,2048]{2,1,0:T(8,128)(2,1)} %bitcast.48), calls=%async_computation.1 | async-start | bytes 9437184 | tf_op jit(solution)/shard_map/all_to_all | solution.py:300
  137.4 3.1 %collective-permute-start.3 = (bf16[2,1152,256]{2,1,0:T(8,128)(2,1)}, bf16[2,1152,256]{2,1,0:T(8,128)(2,1)S(1)}, u32[]{:S(2)}, u32[]{:S(2)}) collective-permute-start(bf16[2,1152,256]{2,1,0:T(8,128)(2,1)} %get-tuple-element.28.own_ref.dgu_ref), channel_id=1, source_target_pairs={{0,1},{1,0},{2,3},{3,2},{4,5},{5,4},{6,7},{7,6},{8,9},{9,8},{10,11... | collective-permute-start | bytes 3538952 | tf_op jit(solution)/shard_map/ppermute | solution.py:304
  140.5 1.0 copy-start.5
  152.1 18.3 %collective-permute-start.4 = (bf16[576,512]{1,0:T(8,128)(2,1)S(1)}, bf16[576,512]{1,0:T(8,128)(2,1)S(1)}, u32[]{:S(2)}, u32[]{:S(2)}) collective-permute-start(bf16[576,512]{1,0:T(8,128)(2,1)S(1)} %get-tuple-element.43), channel_id=1, source_target_pairs={{0,2},{1,3},{2,4},{3,5},{4,6},{5,7},{6,0},{7,1},{8,10},{9,11},{10,... | collective-permute-start | bytes 1769480 | tf_op jit(solution)/shard_map/ppermute | solution.py:308
  154.0 16.5 %collective-permute-start.5 = (bf16[576,512]{1,0:T(8,128)(2,1)S(1)}, bf16[576,512]{1,0:T(8,128)(2,1)S(1)}, u32[]{:S(2)}, u32[]{:S(2)}) collective-permute-start(bf16[576,512]{1,0:T(8,128)(2,1)S(1)} %get-tuple-element.42), channel_id=1, source_target_pairs={{0,6},{1,7},{2,0},{3,1},{4,2},{5,3},{6,4},{7,5},{8,14},{9,15},{10,... | collective-permute-start | bytes 1769480 | tf_op jit(solution)/shard_map/ppermute | solution.py:308
  172.3 24.5 %collective-permute-start.9 = (bf16[576,512]{1,0:T(8,128)(2,1)}, bf16[576,512]{1,0:T(8,128)(2,1)S(1)}, u32[]{:S(2)}, u32[]{:S(2)}) collective-permute-start(bf16[576,512]{1,0:T(8,128)(2,1)} %add_convert_fusion), channel_id=1, source_target_pairs={{0,6},{1,7},{2,0},{3,1},{4,2},{5,3},{6,4},{7,5},{8,14},{9,15},{10,... | collective-permute-start | bytes 1769480 | tf_op jit(solution)/shard_map/ppermute | solution.py:308
  177.2 19.7 %collective-permute-start.6 = (bf16[576,512]{1,0:T(8,128)(2,1)}, bf16[576,512]{1,0:T(8,128)(2,1)S(1)}, u32[]{:S(2)}, u32[]{:S(2)}) collective-permute-start(bf16[576,512]{1,0:T(8,128)(2,1)} %add_convert_fusion.1), channel_id=1, source_target_pairs={{0,2},{1,3},{2,4},{3,5},{4,6},{5,7},{6,0},{7,1},{8,10},{9,11},{10,... | collective-permute-start | bytes 1769480 | tf_op jit(solution)/shard_map/ppermute | solution.py:308
  177.2 23.2 %collective-permute-start.7 = (bf16[576,512]{1,0:T(8,128)(2,1)}, bf16[576,512]{1,0:T(8,128)(2,1)S(1)}, u32[]{:S(2)}, u32[]{:S(2)}) collective-permute-start(bf16[576,512]{1,0:T(8,128)(2,1)} %slice.50), channel_id=1, source_target_pairs={{0,6},{1,7},{2,0},{3,1},{4,2},{5,3},{6,4},{7,5},{8,14},{9,15},{10,... | collective-permute-start | bytes 1769480 | tf_op jit(solution)/shard_map/ppermute | solution.py:308
  180.4 25.1 %collective-permute-start.8 = (bf16[576,512]{1,0:T(8,128)(2,1)}, bf16[576,512]{1,0:T(8,128)(2,1)S(1)}, u32[]{:S(2)}, u32[]{:S(2)}) collective-permute-start(bf16[576,512]{1,0:T(8,128)(2,1)} %slice.52), channel_id=1, source_target_pairs={{0,2},{1,3},{2,4},{3,5},{4,6},{5,7},{6,0},{7,1},{8,10},{9,11},{10,... | collective-permute-start | bytes 1769480 | tf_op jit(solution)/shard_map/ppermute | solution.py:308
  208.4 24.8 %all-to-all-start.3 = ((bf16[16,72,512]{2,1,0:T(8,128)(2,1)}), bf16[16,72,512]{2,1,0:T(8,128)(2,1)S(1)}, u32[]{:S(2)}, u32[]{:S(2)}) async-start(bf16[16,72,512]{2,1,0:T(8,128)(2,1)} %bitcast.23), calls=%async_computation.3 | async-start | bytes 2359296 | tf_op jit(solution)/shard_map/all_to_all | solution.py:300
  221.9 15.2 %copy-start.1 = (bf16[128,4096]{1,0:T(8,128)(2,1)S(1)}, bf16[128,4096]{1,0:T(8,128)(2,1)}, u32[]{:S(2)}) copy-start(bf16[128,4096]{1,0:T(8,128)(2,1)} %param.6) | copy-start | bytes 3145732
  223.0 7.7 %collective-permute-start.10 = (bf16[128,512]{1,0:T(8,128)(2,1)S(1)}, bf16[128,512]{1,0:T(8,128)(2,1)S(1)}, u32[]{:S(2)}, u32[]{:S(2)}) collective-permute-start(bf16[128,512]{1,0:T(8,128)(2,1)S(1)} %get-tuple-element.44), channel_id=1, source_target_pairs={{0,2},{1,3},{2,4},{3,5},{4,6},{5,7},{6,0},{7,1},{8,10},{9,11},{10,... | collective-permute-start | bytes 393224 | tf_op jit(solution)/shard_map/ppermute | solution.py:308
  223.1 7.6 %collective-permute-start.11 = (bf16[128,512]{1,0:T(8,128)(2,1)S(1)}, bf16[128,512]{1,0:T(8,128)(2,1)S(1)}, u32[]{:S(2)}, u32[]{:S(2)}) collective-permute-start(bf16[128,512]{1,0:T(8,128)(2,1)S(1)} %get-tuple-element.46), channel_id=1, source_target_pairs={{0,4},{1,5},{2,6},{3,7},{4,0},{5,1},{6,2},{7,3},{8,12},{9,13},{10,... | collective-permute-start | bytes 393224 | tf_op jit(solution)/shard_map/ppermute | solution.py:308
  224.2 7.4 %collective-permute-start.12 = (bf16[128,512]{1,0:T(8,128)(2,1)S(1)}, bf16[128,512]{1,0:T(8,128)(2,1)S(1)}, u32[]{:S(2)}, u32[]{:S(2)}) collective-permute-start(bf16[128,512]{1,0:T(8,128)(2,1)S(1)} %get-tuple-element.45), channel_id=1, source_target_pairs={{0,6},{1,7},{2,0},{3,1},{4,2},{5,3},{6,4},{7,5},{8,14},{9,15},{10,... | collective-permute-start | bytes 393224 | tf_op jit(solution)/shard_map/ppermute | solution.py:308
  233.2 1.0 copy-start.4
Sparse Core Ops, SparseCore 0:
  11.7 109.4 all-gather.1

commit v9 on v8

--- a/solution.py
+++ b/solution.py
@@ -317,10 +317,10 @@
     def add(*terms):
         return sum(t.astype(F32) for t in terms).astype(BF16)
 
-    far, above, below, own = block(2), block(1), block(3), block(0)
+    far, above, below, own = lax.optimization_barrier((block(2), block(1), block(3), block(0)))
     far_up, far_down = up_levels(far[:half], 1), up_levels(far[half:], -1)
-    far_up, far_down, above, below = lax.optimization_barrier((far_up, far_down, above, below))
     from_below, from_above = up_levels(above[half:], 1), up_levels(below[:half], -1)
+    far_up, far_down = lax.optimization_barrier((far_up, far_down))
     through_up = up_levels(add(above[:half], far_up), 1)
     through_down = up_levels(add(below[half:], far_down), -1)
     return jnp.concatenate(

time: 245 us -> 238 us (0.971)
  waiting for transfers between devices: 32.2 us -> 23.3 us
    ppermute x9, waiting for transfers between devices: 25.8 us -> 16.8 us  [up_levels(): lax.ppermute(x, 'tensor', [(t, (t + 2 * d) % TENSOR) for t in range(TENSO...]
    unnamed x16 -> x18, local copies, waits for them, and re-layouts: 4.26 us -> 5.07 us
  transfers between devices with their start and end apart: 17 -> 17, of which waited for: 7 -> 7; matrix products, arithmetic and copies ran while one was open for 7% -> 7% of each run, Pallas kernels for 28% -> 29%
where the time goes in v9:
time: 238 us; the launch traced here: 237 us
  Pallas kernels  71.5 us (30%)
  blocking collectives  69.5 us (29%)
  starting transfers between devices  35.7 us (15%)
  waiting for transfers between devices  23.3 us (10%)
  local copies, waits for them, and re-layouts  14.6 us (6%)
  between operations  14.2 us (6%)
  other arithmetic  7.72 us (3%)
    all_to_all x1, blocking collectives, over_experts(): return lax.all_to_all(x, 'expert', split_axis=0, concat_axis=0, tiled=True)  69.5 us
    all_to_all x3, starting transfers between devices, over_experts(): return lax.all_to_all(x, 'expert', split_axis=0, concat_axis=0, tiled=True)  19.1 us
    ppermute x9, waiting for transfers between devices, up_levels(): lax.ppermute(x, 'tensor', [(t, (t + 2 * d) % TENSOR) for t in range(TENSO...  16.8 us
    ppermute x9, starting transfers between devices, up_levels(): lax.ppermute(x, 'tensor', [(t, (t + 2 * d) % TENSOR) for t in range(TENSO...  16.3 us
    pallas_call x1, Pallas kernels, weight_grads(): stepped(weight_grad_kernel, 1, TENSOR, [pl.BlockSpec(memory_space=pl.ANY)...  15 us
    pallas_call x1, Pallas kernels, unit_grads(): stepped(unit_grad_kernel, 0, STEPS, [by_rows(STEP_GROUPS * TOK, D), ROW_S...  11.9 us
    pallas_call x1, Pallas kernels, hidden_units(): stepped(hidden_kernel, 1, STEPS, [by_rows(ROWS, HALF), by_rows(ROWS, HALF...  10.1 us
    pallas_call x1, Pallas kernels, back_rows(): stepped(back_kernel, 1, STEPS, [by_rows(2, ROWS, WIDE), by_rows(2, ROWS,...  9.27 us
  transfers between devices with their start and end apart: 17, of which 7 were waited for; matrix products, arithmetic and copies ran while one was open for 7% of the time, Pallas kernels for 29%

profile of v9, /device:TPU:2, one launch (start us, length us, event | category | flops | bytes accessed | tf_op | source)
XLA Modules:
  0.0 237.2 jit_solution(12470560391225639723)
XLA Ops:
  7.2 0.0 copy-start
  7.2 0.0 all-gather.2.cloned.1.call-start
  7.2 1.6 constant_dynamic-slice_fusion
  8.9 0.0 all-gather.2.cloned.1.call-update
  8.9 1.3 select_reduce_fusion
  10.2 0.8 constant_dynamic-slice_fusion.1.x_ref
  11.1 4.8 %shard_map.93.after_ref = bf16[16,72,2048]{2,1,0:T(8,128)(2,1)} custom-call(bf16[128,2048]{1,0:T(8,128)(2,1)} %constant_dynamic-slice_fusion.1.x_ref, f32[16,128]{1,0:T(8,128)} %bitcast.2.w_ref), custom_call_target="tpu_custom_call" | custom-call | flops 600000000 | bytes 5300000 | tf_op jit(solution)/shard_map/pallas_call | solution.py:182
  15.9 69.5 %all_to_all.24 = bf16[16,72,2048]{2,1,0:T(8,128)(2,1)S(1)} all-to-all(bf16[16,72,2048]{2,1,0:T(8,128)(2,1)} %shard_map.93.after_ref), channel_id=1, replica_groups=mesh['expert'=16,'tensor'=8] {'expert'}, dimensions={0} | all-to-all | bytes 9437184 | tf_op jit(solution)/shard_map/all_to_all | solution.py:300
  85.4 0.0 collective-permute-start
  85.5 4.6 %shard_map.95 = bf16[3,192,2048]{2,1,0:T(8,128)(2,1)} custom-call(s32[1]{0:T(128)S(6)} %sub.8.core_ref, bf16[16,72,2048]{2,1,0:T(8,128)(2,1)} %shard_map.93.after_ref, bf16[2,192,4096]{2,1,0:T(8,128)(2,1)} %bitcast.45, bf16[192,4096]{1,0:T(8,128)(2,1)} %bitcast.42), custom_call_target="tpu_custom_call" | custom-call | bytes 4700000 | tf_op jit(solution)/shard_map/pallas_call | solution.py:191
  90.1 0.0 collective-permute-start.2
  90.1 3.4 %collective-permute-done.other_ref = bf16[1152,2048]{1,0:T(8,128)(2,1)} collective-permute-done((bf16[1152,2048]{1,0:T(8,128)(2,1)S(1)}, bf16[1152,2048]{1,0:T(8,128)(2,1)}, u32[]{:S(2)}, u32[]{:S(2)}) %collective-permute-start) | collective-permute-done | bytes 4718624 | tf_op jit(solution)/shard_map/ppermute | solution.py:304
  93.5 10.1 %shard_map.94 = (f32[1152,192]{1,0:T(8,128)}, f32[1152,192]{1,0:T(8,128)}, bf16[1152,256]{1,0:T(8,128)(2,1)}) custom-call(s32[1]{0:T(128)} %bitcast.1.core_ref, bf16[1152,2048]{1,0:T(8,128)(2,1)} %bitcast.40, bf16[1152,2048]{1,0:T(8,128)(2,1)} %collective-permute-done.other_ref, bf16[2,192,4096]{2,1,0:T(8,128)(2,1)} %bitcast.46), custom_call_target="tpu_custom_call" | custom-call | flops 4000000000 | bytes 15000000 | tf_op jit(solution)/shard_map/pallas_call | solution.py:204
  103.6 0.3 collective-permute-start.1
  103.9 4.6 %all-to-all-start.2 = ((f32[16,1,128]{2,1,0:T(1,128)}), f32[16,1,128]{2,1,0:T(1,128)S(1)}, u32[]{:S(2)}, u32[]{:S(2)}) async-start(f32[16,1,128]{2,1,0:T(1,128)} %bitcast.8), calls=%async_computation.2 | async-start | bytes 16384 | tf_op jit(solution)/shard_map/all_to_all | solution.py:300
  108.5 0.0 collective-permute-done.2.lent_ref
  108.5 0.0 copy-start.3
  108.5 0.0 collective-permute-done.1.other_ref
  108.5 1.4 copy-done.3
  109.9 0.8 copy-done.7
  110.7 6.8 %shard_map.96 = bf16[1152,2048]{1,0:T(8,128)(2,1)} custom-call(s32[1]{0:T(128)} %bitcast.1.core_ref, bf16[1152,256]{1,0:T(8,128)(2,1)} %get-tuple-element.24.own_ref.hid_ref, bf16[1152,256]{1,0:T(8,128)(2,1)} %copy-done.7, bf16[192,4096]{1,0:T(8,128)(2,1)} %bitcast.43, bf16[3,192,2048]{2,1,0:T(8,128)(2,1)} %copy-done.3), custom_call_target="tpu_custom_call" | custom-call | flops 2000000000 | bytes 8000000 | tf_op jit(solution)/shard_map/pallas_call | solution.py:217
  117.5 0.0 all-to-all-done.2
  117.5 7.2 %all-to-all-start.1 = ((bf16[16,72,2048]{2,1,0:T(8,128)(2,1)}), bf16[16,72,2048]{2,1,0:T(8,128)(2,1)}, u32[]{:S(2)}, u32[]{:S(2)}) async-start(bf16[16,72,2048]{2,1,0:T(8,128)(2,1)} %bitcast.38), calls=%async_computation.1 | async-start | bytes 9437184 | tf_op jit(solution)/shard_map/all_to_all | solution.py:300
  124.8 0.7 fusion.1
  125.5 11.9 %shard_map.97 = (bf16[1152,4096]{1,0:T(8,128)(2,1)}, bf16[2,1152,256]{2,1,0:T(8,128)(2,1)}) custom-call(bf16[2048,4096]{1,0:T(8,128)(2,1)} %all-gather.2.cloned.1.call-done.g_ref, s32[8,1,256]{2,1,0:T(1,128)} %bitcast.50, f32[8,1,256]{2,1,0:T(1,128)} %bitcast.49, f32[1152,192]{1,0:T(8,128)} %get-tuple-element.28.gate_ref, ...), custom_call_target="tpu_custom_call" | custom-call | flops 1000000 | bytes 100000 | tf_op jit(solution)/shard_map/pallas_call | solution.py:228
  137.5 0.0 collective-permute-start.3
  137.6 3.0 %collective-permute-done.3.other_ref = bf16[2,1152,256]{2,1,0:T(8,128)(2,1)S(1)} collective-permute-done((bf16[2,1152,256]{2,1,0:T(8,128)(2,1)}, bf16[2,1152,256]{2,1,0:T(8,128)(2,1)S(1)}, u32[]{:S(2)}, u32[]{:S(2)}) %collective-permute-start.3) | collective-permute-done | bytes 1179680 | tf_op jit(solution)/shard_map/ppermute | solution.py:304
  140.5 1.0 copy-done.5
  141.5 9.3 %shard_map.98.after_ref = bf16[4,1152,512]{2,1,0:T(8,128)(2,1)} custom-call(s32[1]{0:T(128)} %bitcast.1.core_ref, bf16[2,1152,256]{2,1,0:T(8,128)(2,1)} %get-tuple-element.30.own_ref.dgu_ref, bf16[2,1152,256]{2,1,0:T(8,128)(2,1)} %copy-done.5, bf16[2,192,4096]{2,1,0:T(8,128)(2,1)} %bitcast.47, bf16[3,192,2048]{2,1,0:T(8,128)(2,1)} %copy-done.3), custom_call_target="tpu_custom_call" | custom-call | flops 1000000 | bytes 100000 | tf_op jit(solution)/shard_map/pallas_call | solution.py:241
  150.8 2.6 %dynamic-slice_bitcast_fusion = (bf16[1152,512]{1,0:T(8,128)(2,1)S(1)}, bf16[1152,512]{1,0:T(8,128)(2,1)S(1)}, bf16[1152,512]{1,0:T(8,128)(2,1)S(1)}, bf16[1152,512]{1,0:T(8,128)(2,1)S(1)}) fusion(bf16[4,1152,512]{2,1,0:T(8,128)(2,1)} %shard_map.98.after_ref, s32[]{:T(128)S(6)} %select_n.78, s32[]{:T(128)S(6)} %select_n.76, s32[]{:T(128)S(6)} %select_n.74, ...), kind=kLoop, calls=%fused_computation.5 | loop fusion | bytes 9437200 | tf_op jit(solution)/shard_map/jit(dynamic_index_in_dim)/squeeze | solution.py:315
  153.4 0.1 fusion.10
  153.5 1.9 collective-permute-start.4
  155.4 2.9 %collective-permute-start.5 = (bf16[576,512]{1,0:T(8,128)(2,1)S(1)}, bf16[576,512]{1,0:T(8,128)(2,1)S(1)}, u32[]{:S(2)}, u32[]{:S(2)}) collective-permute-start(bf16[576,512]{1,0:T(8,128)(2,1)S(1)} %get-tuple-element.48), channel_id=1, source_target_pairs={{0,6},{1,7},{2,0},{3,1},{4,2},{5,3},{6,4},{7,5},{8,14},{9,15},{10,... | collective-permute-start | bytes 1769480 | tf_op jit(solution)/shard_map/ppermute | solution.py:308
  158.2 0.9 slice.40
  159.1 1.9 collective-permute-start.7
  161.1 0.9 slice.42
  161.9 0.1 collective-permute-start.8
  162.0 10.3 %collective-permute-done.4 = bf16[576,512]{1,0:T(8,128)(2,1)S(1)} collective-permute-done((bf16[576,512]{1,0:T(8,128)(2,1)S(1)}, bf16[576,512]{1,0:T(8,128)(2,1)S(1)}, u32[]{:S(2)}, u32[]{:S(2)}) %collective-permute-start.4) | collective-permute-done | bytes 589856 | tf_op jit(solution)/shard_map/ppermute | solution.py:308
  172.3 0.0 collective-permute-done.5
  172.3 1.0 add_convert_fusion.1
  173.2 3.3 %collective-permute-start.9 = (bf16[576,512]{1,0:T(8,128)(2,1)}, bf16[576,512]{1,0:T(8,128)(2,1)S(1)}, u32[]{:S(2)}, u32[]{:S(2)}) collective-permute-start(bf16[576,512]{1,0:T(8,128)(2,1)} %add_convert_fusion.1), channel_id=1, source_target_pairs={{0,6},{1,7},{2,0},{3,1},{4,2},{5,3},{6,4},{7,5},{8,14},{9,15},{10,... | collective-permute-start | bytes 1769480 | tf_op jit(solution)/shard_map/ppermute | solution.py:308
  176.6 1.0 add_convert_fusion.3
  177.6 0.0 collective-permute-start.6
  177.6 1.4 copy.33.w_ref
  179.0 15.0 %shard_map.99 = (bf16[2,192,4096]{2,1,0:T(8,128)(2,1)}, bf16[192,4096]{1,0:T(8,128)(2,1)}) custom-call(s32[1]{0:T(128)} %bitcast.1.core_ref, bf16[4,1152,512]{2,1,0:T(8,128)(2,1)} %shard_map.98.after_ref, bf16[1152,2048]{1,0:T(8,128)(2,1)} %bitcast.41, bf16[1152,2048]{1,0:T(8,128)(2,1)} %collective-permute-done.other_ref, ...), custom_call_target="tpu_custom_call" | custom-call | flops 6000000000 | bytes 25000000 | tf_op jit(solution)/shard_map/pallas_call | solution.py:252
  194.0 0.0 collective-permute-done.7
  194.0 0.0 collective-permute-done.8
  194.0 2.6 %collective-permute-done.9 = bf16[576,512]{1,0:T(8,128)(2,1)S(1)} collective-permute-done((bf16[576,512]{1,0:T(8,128)(2,1)}, bf16[576,512]{1,0:T(8,128)(2,1)S(1)}, u32[]{:S(2)}, u32[]{:S(2)}) %collective-permute-start.9) | collective-permute-done | bytes 589856 | tf_op jit(solution)/shard_map/ppermute | solution.py:308
  196.6 0.8 copy-done.6
  197.4 1.7 add_convert_fusion.2
  199.1 1.1 pad_maximum_fusion.after_ref
  200.2 7.2 %all-to-all-start.3 = ((bf16[16,72,512]{2,1,0:T(8,128)(2,1)}), bf16[16,72,512]{2,1,0:T(8,128)(2,1)S(1)}, u32[]{:S(2)}, u32[]{:S(2)}) async-start(bf16[16,72,512]{2,1,0:T(8,128)(2,1)} %bitcast.21), calls=%async_computation.3 | async-start | bytes 2359296 | tf_op jit(solution)/shard_map/all_to_all | solution.py:300
  207.4 6.1 %shard_map.100 = bf16[4,128,512]{2,1,0:T(8,128)(2,1)} custom-call(s32[1]{0:T(128)} %bitcast.z_ref, bf16[16,72,2048]{2,1,0:T(8,128)(2,1)} %all-to-all-done.1.r_ref, f32[128,16]{1,0:T(8,128)} %copy.33.w_ref, bf16[1152,512]{1,0:T(8,128)(2,1)} %pad_maximum_fusion.after_ref), custom_call_target="tpu_custom_call" | custom-call | flops 89999998976 | bytes 5300000 | tf_op jit(solution)/shard_map/pallas_call | solution.py:281
  213.6 1.1 slice_bitcast_fusion.2
  214.7 1.8 collective-permute-start.10
  216.5 3.4 %collective-permute-start.11 = (bf16[128,512]{1,0:T(8,128)(2,1)S(1)}, bf16[128,512]{1,0:T(8,128)(2,1)S(1)}, u32[]{:S(2)}, u32[]{:S(2)}) collective-permute-start(bf16[128,512]{1,0:T(8,128)(2,1)S(1)} %get-tuple-element.52), channel_id=1, source_target_pairs={{0,4},{1,5},{2,6},{3,7},{4,0},{5,1},{6,2},{7,3},{8,12},{9,13},{10,... | collective-permute-start | bytes 393224 | tf_op jit(solution)/shard_map/ppermute | solution.py:308
  219.8 1.1 collective-permute-start.12
  220.9 1.8 collective-permute-done.10
  222.7 2.1 collective-permute-done.11
  224.8 0.1 collective-permute-done.12
  224.9 1.6 fusion.4
  226.5 0.0 all-to-all-done.3.r_ref
  226.5 1.0 copy-done.4
  227.6 2.8 %shard_map.101 = bf16[128,512]{1,0:T(8,128)(2,1)} custom-call(bf16[16,72,512]{2,1,0:T(8,128)(2,1)} %copy-done.4, f32[128,16]{1,0:T(8,128)} %copy.33.w_ref), custom_call_target="tpu_custom_call" | custom-call | flops 200000000 | bytes 1400000 | tf_op jit(solution)/shard_map/pallas_call | solution.py:271
  (15 shorter events, 0.0 us)
Async XLA Ops:
  7.2 3.1 %copy-start = (bf16[128,4096]{1,0:T(8,128)(2,1)S(1)}, bf16[128,4096]{1,0:T(8,128)(2,1)}, u32[]{:S(2)}) copy-start(bf16[128,4096]{1,0:T(8,128)(2,1)} %param.6) | copy-start | bytes 3145732
  7.2 118.3 %all-gather.2.cloned.1.call-start = ((), (), s32[]{:S(2)}) async-start(), calls=%async_computation.4 | async-start | bytes 16908288 | tf_op jit(solution)/shard_map/all_gather | solution.py:339
  85.4 4.6 %copy-start.2 = (bf16[16,72,2048]{2,1,0:T(8,128)(2,1)}, bf16[16,72,2048]{2,1,0:T(8,128)(2,1)S(1)}, u32[]{:S(2)}) copy-start(bf16[16,72,2048]{2,1,0:T(8,128)(2,1)S(1)} %all_to_all.24) | copy-start | bytes 14155780
  85.4 8.0 %collective-permute-start = (bf16[1152,2048]{1,0:T(8,128)(2,1)S(1)}, bf16[1152,2048]{1,0:T(8,128)(2,1)}, u32[]{:S(2)}, u32[]{:S(2)}) collective-permute-start(bf16[1152,2048]{1,0:T(8,128)(2,1)S(1)} %bitcast.39), channel_id=1, source_target_pairs={{0,1},{1,0},{2,3},{3,2},{4,5},{5,4},{6,7},{7,6},{8,9},{9,8},{10,11... | collective-permute-start | bytes 14155784 | tf_op jit(solution)/shard_map/ppermute | solution.py:304
  90.1 18.5 %collective-permute-start.2 = (bf16[3,192,2048]{2,1,0:T(8,128)(2,1)}, bf16[3,192,2048]{2,1,0:T(8,128)(2,1)S(1)}, u32[]{:S(2)}, u32[]{:S(2)}) collective-permute-start(bf16[3,192,2048]{2,1,0:T(8,128)(2,1)} %shard_map.95), channel_id=1, source_target_pairs={{0,1},{1,0},{2,3},{3,2},{4,5},{5,4},{6,7},{7,6},{8,9},{9,8},{10,11... | collective-permute-start | bytes 7077896 | tf_op jit(solution)/shard_map/ppermute | solution.py:304
  103.6 4.9 %collective-permute-start.1 = (bf16[1152,256]{1,0:T(8,128)(2,1)}, bf16[1152,256]{1,0:T(8,128)(2,1)S(1)}, u32[]{:S(2)}, u32[]{:S(2)}) collective-permute-start(bf16[1152,256]{1,0:T(8,128)(2,1)} %get-tuple-element.24.own_ref.hid_ref), channel_id=1, source_target_pairs={{0,1},{1,0},{2,3},{3,2},{4,5},{5,4},{6,7},{7,6},{8,9},{9,8},{10,11... | collective-permute-start | bytes 1769480 | tf_op jit(solution)/shard_map/ppermute | solution.py:304
  103.9 13.6 %all-to-all-start.2 = ((f32[16,1,128]{2,1,0:T(1,128)}), f32[16,1,128]{2,1,0:T(1,128)S(1)}, u32[]{:S(2)}, u32[]{:S(2)}) async-start(f32[16,1,128]{2,1,0:T(1,128)} %bitcast.8), calls=%async_computation.2 | async-start | bytes 16384 | tf_op jit(solution)/shard_map/all_to_all | solution.py:300
  108.5 1.4 copy-start.3
  109.9 0.8 copy-start.7
  117.5 7.3 %copy-start.8 = (f32[16,1,128]{2,1,0:T(1,128)}, f32[16,1,128]{2,1,0:T(1,128)S(1)}, u32[]{:S(2)}) copy-start(f32[16,1,128]{2,1,0:T(1,128)S(1)} %all-to-all-done.2) | copy-start | bytes 24580
  117.5 82.7 %all-to-all-start.1 = ((bf16[16,72,2048]{2,1,0:T(8,128)(2,1)}), bf16[16,72,2048]{2,1,0:T(8,128)(2,1)}, u32[]{:S(2)}, u32[]{:S(2)}) async-start(bf16[16,72,2048]{2,1,0:T(8,128)(2,1)} %bitcast.38), calls=%async_computation.1 | async-start | bytes 9437184 | tf_op jit(solution)/shard_map/all_to_all | solution.py:300
  137.5 3.1 %collective-permute-start.3 = (bf16[2,1152,256]{2,1,0:T(8,128)(2,1)}, bf16[2,1152,256]{2,1,0:T(8,128)(2,1)S(1)}, u32[]{:S(2)}, u32[]{:S(2)}) collective-permute-start(bf16[2,1152,256]{2,1,0:T(8,128)(2,1)} %get-tuple-element.30.own_ref.dgu_ref), channel_id=1, source_target_pairs={{0,1},{1,0},{2,3},{3,2},{4,5},{5,4},{6,7},{7,6},{8,9},{9,8},{10,11... | collective-permute-start | bytes 3538952 | tf_op jit(solution)/shard_map/ppermute | solution.py:304
  140.5 1.0 copy-start.5
  153.5 18.8 %collective-permute-start.4 = (bf16[576,512]{1,0:T(8,128)(2,1)S(1)}, bf16[576,512]{1,0:T(8,128)(2,1)S(1)}, u32[]{:S(2)}, u32[]{:S(2)}) collective-permute-start(bf16[576,512]{1,0:T(8,128)(2,1)S(1)} %get-tuple-element.49), channel_id=1, source_target_pairs={{0,2},{1,3},{2,4},{3,5},{4,6},{5,7},{6,0},{7,1},{8,10},{9,11},{10,... | collective-permute-start | bytes 1769480 | tf_op jit(solution)/shard_map/ppermute | solution.py:308
  155.4 16.9 %collective-permute-start.5 = (bf16[576,512]{1,0:T(8,128)(2,1)S(1)}, bf16[576,512]{1,0:T(8,128)(2,1)S(1)}, u32[]{:S(2)}, u32[]{:S(2)}) collective-permute-start(bf16[576,512]{1,0:T(8,128)(2,1)S(1)} %get-tuple-element.48), channel_id=1, source_target_pairs={{0,6},{1,7},{2,0},{3,1},{4,2},{5,3},{6,4},{7,5},{8,14},{9,15},{10,... | collective-permute-start | bytes 1769480 | tf_op jit(solution)/shard_map/ppermute | solution.py:308
  159.1 34.9 %collective-permute-start.7 = (bf16[576,512]{1,0:T(8,128)(2,1)}, bf16[576,512]{1,0:T(8,128)(2,1)S(1)}, u32[]{:S(2)}, u32[]{:S(2)}) collective-permute-start(bf16[576,512]{1,0:T(8,128)(2,1)} %slice.40), channel_id=1, source_target_pairs={{0,6},{1,7},{2,0},{3,1},{4,2},{5,3},{6,4},{7,5},{8,14},{9,15},{10,... | collective-permute-start | bytes 1769480 | tf_op jit(solution)/shard_map/ppermute | solution.py:308
  161.9 32.0 %collective-permute-start.8 = (bf16[576,512]{1,0:T(8,128)(2,1)}, bf16[576,512]{1,0:T(8,128)(2,1)S(1)}, u32[]{:S(2)}, u32[]{:S(2)}) collective-permute-start(bf16[576,512]{1,0:T(8,128)(2,1)} %slice.42), channel_id=1, source_target_pairs={{0,2},{1,3},{2,4},{3,5},{4,6},{5,7},{6,0},{7,1},{8,10},{9,11},{10,... | collective-permute-start | bytes 1769480 | tf_op jit(solution)/shard_map/ppermute | solution.py:308
  173.2 23.3 %collective-permute-start.9 = (bf16[576,512]{1,0:T(8,128)(2,1)}, bf16[576,512]{1,0:T(8,128)(2,1)S(1)}, u32[]{:S(2)}, u32[]{:S(2)}) collective-permute-start(bf16[576,512]{1,0:T(8,128)(2,1)} %add_convert_fusion.1), channel_id=1, source_target_pairs={{0,6},{1,7},{2,0},{3,1},{4,2},{5,3},{6,4},{7,5},{8,14},{9,15},{10,... | collective-permute-start | bytes 1769480 | tf_op jit(solution)/shard_map/ppermute | solution.py:308
  177.6 19.8 %collective-permute-start.6 = (bf16[576,512]{1,0:T(8,128)(2,1)}, bf16[576,512]{1,0:T(8,128)(2,1)}, u32[]{:S(2)}, u32[]{:S(2)}) collective-permute-start(bf16[576,512]{1,0:T(8,128)(2,1)} %add_convert_fusion.3), channel_id=1, source_target_pairs={{0,2},{1,3},{2,4},{3,5},{4,6},{5,7},{6,0},{7,1},{8,10},{9,11},{10,... | collective-permute-start | bytes 1769480 | tf_op jit(solution)/shard_map/ppermute | solution.py:308
  196.6 0.8 copy-start.6
  200.2 26.3 %all-to-all-start.3 = ((bf16[16,72,512]{2,1,0:T(8,128)(2,1)}), bf16[16,72,512]{2,1,0:T(8,128)(2,1)S(1)}, u32[]{:S(2)}, u32[]{:S(2)}) async-start(bf16[16,72,512]{2,1,0:T(8,128)(2,1)} %bitcast.21), calls=%async_computation.3 | async-start | bytes 2359296 | tf_op jit(solution)/shard_map/all_to_all | solution.py:300
  213.6 16.8 %copy-start.1 = (bf16[128,4096]{1,0:T(8,128)(2,1)S(1)}, bf16[128,4096]{1,0:T(8,128)(2,1)}, u32[]{:S(2)}) copy-start(bf16[128,4096]{1,0:T(8,128)(2,1)} %param.6) | copy-start | bytes 3145732
  214.7 8.0 %collective-permute-start.10 = (bf16[128,512]{1,0:T(8,128)(2,1)S(1)}, bf16[128,512]{1,0:T(8,128)(2,1)S(1)}, u32[]{:S(2)}, u32[]{:S(2)}) collective-permute-start(bf16[128,512]{1,0:T(8,128)(2,1)S(1)} %get-tuple-element.50), channel_id=1, source_target_pairs={{0,2},{1,3},{2,4},{3,5},{4,6},{5,7},{6,0},{7,1},{8,10},{9,11},{10,... | collective-permute-start | bytes 393224 | tf_op jit(solution)/shard_map/ppermute | solution.py:308
  216.5 8.3 %collective-permute-start.11 = (bf16[128,512]{1,0:T(8,128)(2,1)S(1)}, bf16[128,512]{1,0:T(8,128)(2,1)S(1)}, u32[]{:S(2)}, u32[]{:S(2)}) collective-permute-start(bf16[128,512]{1,0:T(8,128)(2,1)S(1)} %get-tuple-element.52), channel_id=1, source_target_pairs={{0,4},{1,5},{2,6},{3,7},{4,0},{5,1},{6,2},{7,3},{8,12},{9,13},{10,... | collective-permute-start | bytes 393224 | tf_op jit(solution)/shard_map/ppermute | solution.py:308
  219.8 5.1 %collective-permute-start.12 = (bf16[128,512]{1,0:T(8,128)(2,1)S(1)}, bf16[128,512]{1,0:T(8,128)(2,1)S(1)}, u32[]{:S(2)}, u32[]{:S(2)}) collective-permute-start(bf16[128,512]{1,0:T(8,128)(2,1)S(1)} %get-tuple-element.51), channel_id=1, source_target_pairs={{0,6},{1,7},{2,0},{3,1},{4,2},{5,3},{6,4},{7,5},{8,14},{9,15},{10,... | collective-permute-start | bytes 393224 | tf_op jit(solution)/shard_map/ppermute | solution.py:308
  226.5 1.0 copy-start.4
Sparse Core Ops, SparseCore 0:
  11.7 109.4 all-gather.1
